TPU v7x, 256 devices: a whole 4x4x8 slice. The times are simulated.
256 devices in a mesh: dp: 8 (over z), expert: 32 (over x, y, core).
Axes of the slice: x: 4, y: 4, z: 8, core: 2. Of those that a mesh axis runs over, the one named last changes fastest.
Arguments:
- tokens: bfloat16 [32768, 2048], P(('dp', 'expert')), may hold values from -6 to 6
- out_grad: bfloat16 [32768, 2048], P(('dp', 'expert')), may hold values from -6 to 6
- routes: int32 [32768, 2], P(('dp', 'expert')), may hold values from 0 to 31, all different within a row; in each aligned block of 128 rows (0 to 127, 128 to 255, ...) at most 14 rows name the same one
- gates: float32 [32768, 2], P(('dp', 'expert')), may hold values from 0.2 to 1
- weights: bfloat16 [32, 2048, 2304], P('expert'), may hold values from -0.125 to 0.125
Outputs:
- layer_out: bfloat16 [32768, 2048], P(('dp', 'expert'))
- grad_tokens: bfloat16 [32768, 2048], P(('dp', 'expert'))
- grad_weights: bfloat16 [32, 1024, 2304], P('expert', 'dp')
Inputs may be any that keep to these rules, and one draw needn't show every extreme that they name: `routes`: within the 128 tokens of one device, no slot is named by more than 14 of their rows, a bound that some block reaches; a token names 2 different slots.
All inputs are finite; a program needn't handle non-finite values.
Results may differ from a plain program's by a relative error of at most 0.019.
Values may be sent and summed in bfloat16 or wider, within the bound.
No kernel may reach another device: no remote copies, remote signals or barrier semaphores. Data moves between devices by JAX's collectives and lax.ppermute only.
A program may use at most 128 MiB of HBM per device.

v0:
```python
import jax
import jax.numpy as jnp
from jax import lax
from jax.sharding import PartitionSpec as P


def from_behind(block, axis, distance):
    devices = range(lax.axis_size(axis))
    route = [((i - distance) % len(devices), i) for i in devices]
    return lax.ppermute(block, axis, route)


def slot_positions(flat_routes, slot_count):
    onehot = (flat_routes[:, None] == jnp.arange(slot_count, dtype=jnp.int32)[None, :]).astype(
        jnp.int32
    )
    before = jnp.cumsum(onehot, axis=0) - onehot
    return jnp.sum(before * onehot, axis=1)


def forward_rows(weight, rows_x):
    hidden_width = weight.shape[1] // 3
    gate_up = jnp.dot(rows_x, weight[:, : 2 * hidden_width], preferred_element_type=jnp.float32)
    gate_pre = gate_up[:, :hidden_width]
    up_pre = gate_up[:, hidden_width:]
    sigmoid_gate = jax.nn.sigmoid(gate_pre)
    active = gate_pre * sigmoid_gate
    hidden = (active * up_pre).astype(jnp.bfloat16)
    rows_y = lax.dot_general(
        hidden,
        weight[:, 2 * hidden_width :],
        (((1,), (1,)), ((), ())),
        preferred_element_type=jnp.float32,
    ).astype(jnp.bfloat16)
    return (rows_y, (gate_pre, up_pre, sigmoid_gate, hidden))


def backward_rows(weight, rows_x, rows_dy, kept_state):
    gate_pre, up_pre, sigmoid_gate, hidden = kept_state
    hidden_width = weight.shape[1] // 3
    d_hidden = jnp.dot(rows_dy, weight[:, 2 * hidden_width :], preferred_element_type=jnp.float32)
    d_gate = d_hidden * up_pre * sigmoid_gate * (1.0 + gate_pre * (1.0 - sigmoid_gate))
    d_up = d_hidden * gate_pre * sigmoid_gate
    d_both = jnp.concatenate([d_gate, d_up], axis=1).astype(jnp.bfloat16)
    rows_dx = lax.dot_general(
        d_both,
        weight[:, : 2 * hidden_width],
        (((1,), (1,)), ((), ())),
        preferred_element_type=jnp.float32,
    ).astype(jnp.bfloat16)
    grad_in = lax.dot_general(
        rows_x, d_both, (((0,), (0,)), ((), ())), preferred_element_type=jnp.float32
    )
    grad_down = lax.dot_general(
        rows_dy, hidden, (((0,), (0,)), ((), ())), preferred_element_type=jnp.float32
    )
    return (rows_dx, jnp.concatenate([grad_in, grad_down], axis=1))


def local(tokens, out_grad, routes, gates, weights):
    slot_count = lax.axis_size("expert")
    token_count = tokens.shape[0]
    top_count = routes.shape[1]
    model_width = tokens.shape[1]
    capacity = 7 * token_count * top_count // (4 * slot_count)
    rows_dev = token_count * top_count
    flat_routes = routes.reshape(-1)
    row_place = flat_routes * capacity + slot_positions(flat_routes, slot_count)
    slot_table = (
        jnp.full((slot_count * capacity,), rows_dev, jnp.int32)
        .at[row_place]
        .set(jnp.arange(rows_dev, dtype=jnp.int32))
    )
    is_live = slot_table < rows_dev
    safe_row = jnp.minimum(slot_table, rows_dev - 1)
    token_index = safe_row // top_count
    send_x = jnp.where(is_live[:, None], tokens[token_index], jnp.zeros((), tokens.dtype))
    gate_row = jnp.where(is_live, gates.reshape(-1)[safe_row], 0.0)
    send_dy = (gate_row[:, None] * out_grad[token_index].astype(jnp.float32)).astype(jnp.bfloat16)
    came_x, came_dy = (
        lax.all_to_all(
            send_x.reshape(slot_count, capacity, model_width),
            "expert",
            split_axis=0,
            concat_axis=0,
            tiled=True,
        ),
        lax.all_to_all(
            send_dy.reshape(slot_count, capacity, model_width),
            "expert",
            split_axis=0,
            concat_axis=0,
            tiled=True,
        ),
    )
    rows_x = came_x.reshape(-1, model_width)
    rows_dy = came_dy.reshape(-1, model_width)
    weight = weights[0]
    rows_y, kept_state = forward_rows(weight, rows_x)
    back_y = lax.all_to_all(
        rows_y.reshape(slot_count, capacity, model_width),
        "expert",
        split_axis=0,
        concat_axis=0,
        tiled=True,
    )
    rows_dx, partial_value = backward_rows(weight, rows_x, rows_dy, kept_state)
    back_dx = lax.all_to_all(
        rows_dx.reshape(slot_count, capacity, model_width),
        "expert",
        split_axis=0,
        concat_axis=0,
        tiled=True,
    )
    mine_y = (
        back_y.reshape(-1, model_width)[row_place]
        .reshape(token_count, top_count, model_width)
        .astype(jnp.float32)
    )
    layer_out = jnp.sum(gates[:, :, None] * mine_y, axis=1).astype(jnp.bfloat16)
    mine_dx = (
        back_dx.reshape(-1, model_width)[row_place]
        .reshape(token_count, top_count, model_width)
        .astype(jnp.float32)
    )
    grad_tokens = jnp.sum(mine_dx, axis=1).astype(jnp.bfloat16)
    rounded = partial_value.astype(jnp.bfloat16).astype(jnp.float32)
    halves = rounded.reshape(2, model_width // 2, rounded.shape[1])
    upper_half = lax.axis_index("expert") >= slot_count // 2
    own_half = jnp.where(upper_half, halves[1], halves[0])
    sent_half = jnp.where(upper_half, halves[0], halves[1]).astype(jnp.bfloat16)
    came_half = from_behind(sent_half, "expert", slot_count // 2)
    both_terms = own_half + came_half.astype(jnp.float32)
    total_sum = lax.psum_scatter(
        both_terms.astype(jnp.bfloat16), "dp", scatter_dimension=0, tiled=True
    )
    grad_weights = total_sum[None]
    return (layer_out, grad_tokens, grad_weights)


def solution(mesh):
    placed = (
        P(("dp", "expert"), None),
        P(("dp", "expert"), None),
        P(("dp", "expert"), None),
        P(("dp", "expert"), None),
        P("expert", None, None),
    )
    return jax.shard_map(
        local,
        mesh=mesh,
        in_specs=placed,
        out_specs=(P(("dp", "expert"), None), P(("dp", "expert"), None), P("expert", "dp", None)),
        check_vma=False,
    )
```

profile of v0, /device:TPU:4, one launch (start us, length us, event | category | flops | bytes accessed | tf_op | source)
XLA Modules:
  0.0 340.8 jit_solution(4298475525995086609)
XLA Ops:
  12.6 3.2 gather_fusion.2
  15.9 3.2 gather_fusion
  19.1 2.5 gather.18
  23.1 7.7 %all-to-all-start = ((bf16[32,14,2048]{2,1,0:T(8,128)(2,1)}), bf16[32,14,2048]{2,1,0:T(8,128)(2,1)S(1)}, u32[]{:S(2)}, u32[]{:S(2)}) async-start(bf16[32,14,2048]{2,1,0:T(8,128)(2,1)} %broadcast_select_fusion), calls=%async_computation | async-start | bytes 4194304 | tf_op jit(solution)/shard_map/all_to_all | solution.py:81
  31.0 3.2 gather_fusion.3
  34.2 3.7 %reshape.113 = f32[32,14,2048]{2,1,0:T(8,128)} reshape(bf16[448,2048]{1,0:T(8,128)(2,1)} %gather_fusion.3) | data formatting | bytes 5505024 | tf_op jit(solution)/shard_map/convert_element_type | solution.py:79
  37.9 3.8 %multiply_convert_fusion = bf16[32,14,2048]{2,1,0:T(8,128)(2,1)} fusion(f32[32,14,2048]{2,1,0:T(8,128)} %reshape.113, f32[32,14]{1,0:T(8,128)S(1)} %mul.70), kind=kLoop, calls=%fused_computation.14 | loop fusion | flops 1835008 | bytes 5506816 | tf_op jit(solution)/shard_map/convert_element_type | solution.py:79
  41.7 15.1 %all-to-all-done = bf16[32,14,2048]{2,1,0:T(8,128)(2,1)S(1)} async-done(((bf16[32,14,2048]{2,1,0:T(8,128)(2,1)}), bf16[32,14,2048]{2,1,0:T(8,128)(2,1)S(1)}, u32[]{:S(2)}, u32[]{:S(2)}) %all-to-all-start) | async-done | bytes 1835040 | tf_op jit(solution)/shard_map/all_to_all | solution.py:81
  56.8 7.7 %all-to-all-start.2 = ((bf16[32,14,2048]{2,1,0:T(8,128)(2,1)}), bf16[32,14,2048]{2,1,0:T(8,128)(2,1)}, u32[]{:S(2)}, u32[]{:S(2)}) async-start(bf16[32,14,2048]{2,1,0:T(8,128)(2,1)} %multiply_convert_fusion), calls=%async_computation.2 | async-start | bytes 4194304 | tf_op jit(solution)/shard_map/all_to_all | solution.py:88
  66.3 7.9 %fusion.2 = f32[448,1536]{1,0:T(8,128)} fusion(bf16[448,2048]{1,0:T(8,128)(2,1)} %reshape.104, bf16[2048,2304]{1,0:T(8,128)(2,1)} %bitcast.35), kind=kOutput, calls=%fused_computation.12 | convolution fusion | flops 2818572288 | bytes 10878976 | tf_op jit(solution)/shard_map/dot_general | solution.py:23
  74.2 16.2 %all-to-all-done.2 = bf16[32,14,2048]{2,1,0:T(8,128)(2,1)} async-done(((bf16[32,14,2048]{2,1,0:T(8,128)(2,1)}), bf16[32,14,2048]{2,1,0:T(8,128)(2,1)}, u32[]{:S(2)}, u32[]{:S(2)}) %all-to-all-start.2) | async-done | bytes 1835040 | tf_op jit(solution)/shard_map/all_to_all | solution.py:88
  90.4 2.5 reshape.108
  92.9 4.7 %multiply_convert_fusion.2 = (bf16[448,768]{1,0:T(8,128)(2,1)S(1)}, bf16[448,768]{1,0:T(8,128)(2,1)S(1)}, bf16[448,768]{1,0:T(8,128)(2,1)S(1)}) fusion(f32[448,1536]{1,0:T(8,128)} %fusion.2, bf16[448,2048]{1,0:T(8,128)(2,1)S(1)} %reshape.108, bf16[2048,2304]{1,0:T(8,128)(2,1)} %bitcast.36), kind=kOutput, calls=%fused_computation.25 | convolution fusion | flops 1414791168 | bytes 9797632 | tf_op jit(solution)/shard_map/dot_general | solution.py:41
  99.6 3.8 %convolution_convert_fusion = bf16[2048,1536]{0,1:T(8,128)(2,1)S(1)} fusion(bf16[448,2048]{1,0:T(8,128)(2,1)S(1)} %copy-done.5, bf16[448,768]{1,0:T(8,128)(2,1)S(1)} %get-tuple-element.15, bf16[448,768]{1,0:T(8,128)(2,1)S(1)} %get-tuple-element.14), kind=kOutput, calls=%fused_computation.9 | convolution fusion | flops 2824470528 | bytes 9502720 | tf_op jit(solution)/shard_map/dot_general | solution.py:51
  103.4 7.2 %maximum_convert_fusion = f32[2048,2304]{0,1:T(8,128)} fusion(bf16[2048,768]{0,1:T(8,128)(2,1)S(1)} %convolution_convert_fusion.1, bf16[2048,1536]{0,1:T(8,128)(2,1)S(1)} %convolution_convert_fusion), kind=kLoop, calls=%fused_computation.6 | loop fusion | flops 18874368 | bytes 28311552 | tf_op jit(solution)/shard_map/convert_element_type | solution.py:127
  110.6 9.3 %select_convert_fusion = bf16[1024,2304]{0,1:T(8,128)(2,1)} fusion(f32[2048,2304]{0,1:T(8,128)} %maximum_convert_fusion, pred[]{:T(512)S(6)} %ge.3), kind=kLoop, calls=%fused_computation.8 | loop fusion | flops 2359296 | bytes 14155777 | tf_op jit(solution)/shard_map/convert_element_type | solution.py:131
  119.9 3.3 collective-permute-start
  123.2 102.6 %collective-permute-done = bf16[1024,2304]{0,1:T(8,128)(2,1)S(1)} collective-permute-done((bf16[1024,2304]{0,1:T(8,128)(2,1)}, bf16[1024,2304]{0,1:T(8,128)(2,1)S(1)}, u32[]{:S(2)}, u32[]{:S(2)}) %collective-permute-start) | collective-permute-done | bytes 4718624 | tf_op jit(solution)/shard_map/ppermute | solution.py:10
  225.8 10.2 %add_convert_fusion = bf16[1024,2304]{0,1:T(8,128)(2,1)} fusion(bf16[1024,2304]{0,1:T(8,128)(2,1)S(1)} %collective-permute-done, f32[2048,2304]{0,1:T(8,128)} %maximum_convert_fusion, pred[]{:T(512)S(6)} %ge.3), kind=kLoop, calls=%fused_computation.7 | loop fusion | flops 9437184 | bytes 28311552 | tf_op jit(solution)/shard_map/convert_element_type | solution.py:135
  236.1 6.8 %copy.24 = bf16[1024,2304]{1,0:T(8,128)(2,1)} copy(bf16[1024,2304]{0,1:T(8,128)(2,1)} %add_convert_fusion) | data formatting | bytes 9437184
  242.9 3.5 %convolution_convert_fusion.2 = bf16[448,2048]{1,0:T(8,128)(2,1)S(1)} fusion(bf16[448,768]{1,0:T(8,128)(2,1)S(1)} %get-tuple-element.16, bf16[2048,2304]{1,0:T(8,128)(2,1)} %bitcast.37), kind=kOutput, calls=%fused_computation.17 | convolution fusion | flops 1410203648 | bytes 5668864 | tf_op jit(solution)/shard_map/dot_general | solution.py:29
  248.0 6.4 %all-to-all-start.1 = ((bf16[32,14,2048]{2,1,0:T(8,128)(2,1)}), bf16[32,14,2048]{2,1,0:T(8,128)(2,1)S(1)}, u32[]{:S(2)}, u32[]{:S(2)}) async-start(bf16[32,14,2048]{2,1,0:T(8,128)(2,1)} %reshape.105), calls=%async_computation.1 | async-start | bytes 4194304 | tf_op jit(solution)/shard_map/all_to_all | solution.py:100
  254.5 7.8 %fusion.4 = bf16[448,2048]{1,0:T(8,128)(2,1)} fusion(bf16[2048,2304]{1,0:T(8,128)(2,1)} %bitcast.38, bf16[448,768]{1,0:T(8,128)(2,1)} %copy-done.8, bf16[448,768]{1,0:T(8,128)(2,1)S(1)} %copy-done.7), kind=kOutput, calls=%fused_computation.16 | convolution fusion | flops 2822242304 | bytes 9502720 | tf_op jit(solution)/shard_map/dot_general | solution.py:45
  262.2 3.7 %reshape.109 = bf16[32,14,2048]{2,1,0:T(8,128)(2,1)} reshape(bf16[448,2048]{1,0:T(8,128)(2,1)} %fusion.4) | data formatting | bytes 3670016 | tf_op jit(solution)/shard_map/reshape | solution.py:109
  265.9 14.4 %all-to-all-done.1 = bf16[32,14,2048]{2,1,0:T(8,128)(2,1)S(1)} async-done(((bf16[32,14,2048]{2,1,0:T(8,128)(2,1)}), bf16[32,14,2048]{2,1,0:T(8,128)(2,1)S(1)}, u32[]{:S(2)}, u32[]{:S(2)}) %all-to-all-start.1) | async-done | bytes 1835040 | tf_op jit(solution)/shard_map/all_to_all | solution.py:100
  281.7 7.8 %all-to-all-start.3 = ((bf16[32,14,2048]{2,1,0:T(8,128)(2,1)}), bf16[32,14,2048]{2,1,0:T(8,128)(2,1)}, u32[]{:S(2)}, u32[]{:S(2)}) async-start(bf16[32,14,2048]{2,1,0:T(8,128)(2,1)} %reshape.109), calls=%async_computation.3 | async-start | bytes 4194304 | tf_op jit(solution)/shard_map/all_to_all | solution.py:108
  289.5 2.6 reshape.106
  295.7 19.6 %all-to-all-done.3 = bf16[32,14,2048]{2,1,0:T(8,128)(2,1)} async-done(((bf16[32,14,2048]{2,1,0:T(8,128)(2,1)}), bf16[32,14,2048]{2,1,0:T(8,128)(2,1)}, u32[]{:S(2)}, u32[]{:S(2)}) %all-to-all-start.3) | async-done | bytes 1835040 | tf_op jit(solution)/shard_map/all_to_all | solution.py:108
  315.3 2.5 reshape.110
  320.2 2.7 reshape.111
  322.9 4.6 %reduce_sum.35 = bf16[128,2048]{1,0:T(8,128)(2,1)} reduce(bf16[128,2,2048]{2,1,0:T(2,128)(2,1)} %reshape.111, bf16[]{:T(256)} %constant.39.clone.1), dimensions={1}, to_apply=%region_5.6 | reduce | flops 262144 | bytes 1572866 | tf_op jit(solution)/shard_map/reduce_sum | solution.py:126
  327.6 3.9 %multiply_reduce_fusion = bf16[128,2048]{1,0:T(8,128)(2,1)} fusion(f32[128,2,2048]{2,1,0:T(2,128)S(1)} %copy-done.4, f32[128,2]{1,0:T(8,128)S(1)} %copy.17), kind=kLoop, calls=%fused_computation.21 | loop fusion | flops 786432 | bytes 2622464 | tf_op jit(solution)/shard_map/reduce_sum | solution.py:120
  (53 shorter events, 22.4 us)
Async XLA Ops:
  7.2 8.7 %copy-start = (bf16[128,2048]{1,0:T(8,128)(2,1)S(1)}, bf16[128,2048]{1,0:T(8,128)(2,1)}, u32[]{:S(2)}) copy-start(bf16[128,2048]{1,0:T(8,128)(2,1)} %param.5) | copy-start | bytes 1572868
  23.1 7.8 %copy-start.2 = (bf16[128,2048]{1,0:T(8,128)(2,1)S(1)}, bf16[128,2048]{1,0:T(8,128)(2,1)}, u32[]{:S(2)}) copy-start(bf16[128,2048]{1,0:T(8,128)(2,1)} %param.6) | copy-start | bytes 1572868
  23.1 33.7 %all-to-all-start = ((bf16[32,14,2048]{2,1,0:T(8,128)(2,1)}), bf16[32,14,2048]{2,1,0:T(8,128)(2,1)S(1)}, u32[]{:S(2)}, u32[]{:S(2)}) async-start(bf16[32,14,2048]{2,1,0:T(8,128)(2,1)} %broadcast_select_fusion), calls=%async_computation | async-start | bytes 4194304 | tf_op jit(solution)/shard_map/all_to_all | solution.py:81
  56.8 33.6 %all-to-all-start.2 = ((bf16[32,14,2048]{2,1,0:T(8,128)(2,1)}), bf16[32,14,2048]{2,1,0:T(8,128)(2,1)}, u32[]{:S(2)}, u32[]{:S(2)}) async-start(bf16[32,14,2048]{2,1,0:T(8,128)(2,1)} %multiply_convert_fusion), calls=%async_computation.2 | async-start | bytes 4194304 | tf_op jit(solution)/shard_map/all_to_all | solution.py:88
  64.5 267.0 %reduce-scatter.4.cloned.1.call-start = ((), (), s32[]{:S(2)}) async-start(), calls=%async_computation.5 | async-start | bytes 5308416
  97.6 1.9 copy-start.6
  97.6 1.9 copy-start.8
  97.6 2.0 copy-start.5
  119.9 105.9 %collective-permute-start = (bf16[1024,2304]{0,1:T(8,128)(2,1)}, bf16[1024,2304]{0,1:T(8,128)(2,1)S(1)}, u32[]{:S(2)}, u32[]{:S(2)}) collective-permute-start(bf16[1024,2304]{0,1:T(8,128)(2,1)} %select_convert_fusion), channel_id=1, source_target_pairs={{16,0},{17,1},{18,2},{19,3},{20,4},{21,5},{22,6},{23,7},{24,8},{25... | collective-permute-start | bytes 14155784 | tf_op jit(solution)/shard_map/ppermute | solution.py:10
  248.0 6.4 %copy-start.7 = (bf16[448,768]{1,0:T(8,128)(2,1)S(1)}, bf16[448,768]{1,0:T(8,128)(2,1)}, u32[]{:S(2)}) copy-start(bf16[448,768]{1,0:T(8,128)(2,1)} %copy-done.6) | copy-start | bytes 2064388
  248.0 32.3 %all-to-all-start.1 = ((bf16[32,14,2048]{2,1,0:T(8,128)(2,1)}), bf16[32,14,2048]{2,1,0:T(8,128)(2,1)S(1)}, u32[]{:S(2)}, u32[]{:S(2)}) async-start(bf16[32,14,2048]{2,1,0:T(8,128)(2,1)} %reshape.105), calls=%async_computation.1 | async-start | bytes 4194304 | tf_op jit(solution)/shard_map/all_to_all | solution.py:100
  280.3 1.4 copy-start.3
  281.7 33.7 %all-to-all-start.3 = ((bf16[32,14,2048]{2,1,0:T(8,128)(2,1)}), bf16[32,14,2048]{2,1,0:T(8,128)(2,1)}, u32[]{:S(2)}, u32[]{:S(2)}) async-start(bf16[32,14,2048]{2,1,0:T(8,128)(2,1)} %reshape.109), calls=%async_computation.3 | async-start | bytes 4194304 | tf_op jit(solution)/shard_map/all_to_all | solution.py:108
  320.2 7.3 %copy-start.4 = (f32[128,2,2048]{2,1,0:T(2,128)S(1)}, f32[128,2,2048]{2,1,0:T(2,128)}, u32[]{:S(2)}) copy-start(f32[128,2,2048]{2,1,0:T(2,128)} %reshape.112) | copy-start | bytes 6291460
  322.9 11.0 %copy-start.1 = (bf16[128,2048]{1,0:T(8,128)(2,1)S(1)}, bf16[128,2048]{1,0:T(8,128)(2,1)}, u32[]{:S(2)}) copy-start(bf16[128,2048]{1,0:T(8,128)(2,1)} %param.5) | copy-start | bytes 1572868
Sparse Core Ops, SparseCore 0:
  243.0 61.3 reduce-scatter.3
where the time goes:
time: 345 us; the launch traced here: 341 us
  waiting for transfers between devices  168 us (49%)
  local copies, waits for them, and re-layouts  53.9 us (16%)
  other arithmetic  42.2 us (12%)
  starting transfers between devices  33.1 us (10%)
  matrix products  29.5 us (9%)
  between operations  14.3 us (4%)
    ppermute x1, waiting for transfers between devices, from_behind(): return lax.ppermute(block, axis, route)  103 us
    all_to_all x1, waiting for transfers between devices, local(): lax.all_to_all(rows_dx.reshape(slot_count, capacity, model_width), 'exper...  19.6 us
    all_to_all x1, waiting for transfers between devices, local(): lax.all_to_all(send_dy.reshape(slot_count, capacity, model_width), 'exper...  16.2 us
    all_to_all x1, waiting for transfers between devices, local(): lax.all_to_all(send_x.reshape(slot_count, capacity, model_width), 'expert...  15.1 us
    all_to_all x1, waiting for transfers between devices, local(): lax.all_to_all(rows_y.reshape(slot_count, capacity, model_width), 'expert...  14.4 us
    unnamed x23, local copies, waits for them, and re-layouts  12.3 us
    convert_element_type x1, other arithmetic, local(): both_terms.astype(jnp.bfloat16)  10.2 us
    convert_element_type x1, other arithmetic, local(): sent_half = jnp.where(upper_half, halves[0], halves[1]).astype(jnp.bfloat16)  9.33 us
  transfers between devices with their start and end apart: 6, of which 5 were waited for; matrix products, arithmetic and copies ran while one was open for 17% of the time, Pallas kernels for 0%

commit v1 on v0

v1 whole, which is shorter than its diff:
```python
import jax
import jax.numpy as jnp
from jax import lax
from jax.experimental import pallas as pl
from jax.experimental.pallas import tpu as pltpu
from jax.sharding import PartitionSpec as P

BF16 = jnp.bfloat16
F32 = jnp.float32
ROWS = 16
VMEM_LIMIT = 58 * 1024 * 1024


def dot(a, b, dims):
    return lax.dot_general(a, b, (dims, ((), ())), preferred_element_type=F32)


def dispatch_mask(routes, slots):
    top, tokens = routes.shape
    slot = lax.broadcasted_iota(jnp.int32, (slots, tokens), 0)
    names = [routes[k : k + 1, :] == slot for k in range(top)]
    named = names[0]
    for one in names[1:]:
        named = named | one
    earlier = (
        lax.broadcasted_iota(jnp.int32, (tokens, tokens), 0)
        < lax.broadcasted_iota(jnp.int32, (tokens, tokens), 1)
    )
    place = dot(
        jnp.where(named, 1.0, 0.0).astype(BF16),
        jnp.where(earlier, 1.0, 0.0).astype(BF16),
        ((1,), (0,)),
    ).astype(jnp.int32)
    place = jnp.where(named, place, ROWS)
    at = lax.broadcasted_iota(jnp.int32, (slots, ROWS, tokens), 1)
    return names, place[:, None, :] == at


def slot_gates(names, gates):
    total = jnp.where(names[0], gates[0:1, :], 0.0)
    for k in range(1, len(names)):
        total = total + jnp.where(names[k], gates[k : k + 1, :], 0.0)
    return total


def pack_kernel(routes_ref, gates_ref, tokens_ref, out_grad_ref, send_ref):
    slots, _, width = send_ref.shape
    names, mask = dispatch_mask(routes_ref[...], slots)
    weight = slot_gates(names, gates_ref[...])
    row_gate = jnp.sum(jnp.where(mask, weight[:, None, :], 0.0), axis=2, keepdims=True)
    pick = jnp.where(mask, 1.0, 0.0).reshape(slots * ROWS, -1).astype(BF16)
    step = 512
    for c in range(0, width, step):
        cols = slice(c, c + step)
        x = dot(pick, tokens_ref[:, cols], ((1,), (0,)))
        send_ref[:, :ROWS, cols] = x.astype(BF16).reshape(slots, ROWS, step)
        g = dot(pick, out_grad_ref[:, cols], ((1,), (0,))).reshape(slots, ROWS, step)
        send_ref[:, ROWS:, cols] = (row_gate * g).astype(BF16)


def grads_kernel(rows_ref, g_ref, u_ref, v_ref, partial_ref, qg_ref, qu_ref, h_ref):
    slots, _, width = rows_ref.shape
    rows = slots * ROWS
    x = rows_ref[:, :ROWS, :].reshape(rows, width)
    dy = rows_ref[:, ROWS:, :].reshape(rows, width)
    a = dot(x, g_ref[...], ((1,), (0,)))
    b = dot(x, u_ref[...], ((1,), (0,)))
    e = dot(dy, v_ref[...], ((1,), (0,)))
    s = jax.nn.sigmoid(a)
    active = a * s
    h = (active * b).astype(BF16)
    qg = (e * b * s * (1.0 + a * (1.0 - s))).astype(BF16)
    qu = (e * active).astype(BF16)
    h_ref[...] = h
    qg_ref[...] = qg
    qu_ref[...] = qu
    chunk = h.shape[1]
    block = partial_ref.shape[0] // 16
    for n, (lhs, rhs) in enumerate(((x, qg), (x, qu), (dy, h))):
        value = dot(lhs, rhs, ((0,), (0,))).astype(BF16)
        for half in range(2):
            for d in range(8):
                partial_ref[
                    pl.ds((2 * d + half) * block, block), pl.ds(n * chunk, chunk)
                ] = value[(half * 8 + d) * block : (half * 8 + d + 1) * block]


def back_kernel(h_ref, qg_ref, qu_ref, w_ref, out_ref):
    slots, _, block = out_ref.shape
    ff = h_ref.shape[1]
    y = dot(h_ref[...], w_ref[:, 2 * ff :], ((1,), (1,)))
    out_ref[:, :ROWS, :] = y.astype(BF16).reshape(slots, ROWS, block)
    dx = dot(qg_ref[...], w_ref[:, :ff], ((1,), (1,)))
    dx = dx + dot(qu_ref[...], w_ref[:, ff : 2 * ff], ((1,), (1,)))
    out_ref[:, ROWS:, :] = dx.astype(BF16).reshape(slots, ROWS, block)


def combine_kernel(routes_ref, gates_ref, back_ref, layer_ref, grad_ref):
    slots, _, width = back_ref.shape
    names, mask = dispatch_mask(routes_ref[...], slots)
    weight = slot_gates(names, gates_ref[...])
    rows = slots * ROWS
    gate = jnp.where(mask, weight[:, None, :], 0.0).reshape(rows, -1)
    high = gate.astype(BF16)
    low = (gate - high.astype(F32)).astype(BF16)
    pick = jnp.where(mask, 1.0, 0.0).reshape(rows, -1).astype(BF16)
    step = 512
    for c in range(0, width, step):
        cols = slice(c, c + step)
        y = back_ref[:, :ROWS, cols].reshape(rows, step)
        value = dot(high, y, ((0,), (0,))) + dot(low, y, ((0,), (0,)))
        layer_ref[:, cols] = value.astype(BF16)
        dx = back_ref[:, ROWS:, cols].reshape(rows, step)
        grad_ref[:, cols] = dot(pick, dx, ((0,), (0,))).astype(BF16)


def join_kernel(which_ref, summed_ref, came_ref, out_ref):
    half, columns = came_ref.shape
    chunk = 256
    steps = columns // chunk // 3
    own = summed_ref[pl.ds(pl.multiple_of(which_ref[0] * half, half), half), :]
    total = (own.astype(F32) + came_ref[...].astype(F32)).astype(BF16)
    for j in range(steps):
        for n in range(3):
            old, new = (3 * j + n) * chunk, (n * steps + j) * chunk
            out_ref[0, :, new : new + chunk] = total[:, old : old + chunk]


def params():
    return pltpu.CompilerParams(vmem_limit_bytes=VMEM_LIMIT)


def cost(flops, moved):
    return pl.CostEstimate(flops=flops, bytes_accessed=moved, transcendentals=0)


def local(tokens, out_grad, routes, gates, weights):
    slots = lax.axis_size("expert")
    groups = lax.axis_size("dp")
    count, width = tokens.shape
    weight = weights[0]
    ff = weight.shape[1] // 3
    rows = slots * ROWS
    chunk = 256
    steps = ff // chunk
    routes_t = routes.T
    gates_t = gates.T
    pair = jax.ShapeDtypeStruct((slots, 2 * ROWS, width), BF16)
    sent = pl.pallas_call(
        pack_kernel,
        out_shape=pair,
        compiler_params=params(),
        cost_estimate=cost(4 * rows * count * width, 6 * rows * width),
        name="pack",
    )(routes_t, gates_t, tokens, out_grad)
    came = lax.all_to_all(sent, "expert", split_axis=0, concat_axis=0, tiled=True)
    row_spec = pl.BlockSpec((rows, chunk), lambda j: (0, j))
    partial, qg, qu, h = pl.pallas_call(
        grads_kernel,
        grid=(steps,),
        in_specs=[
            pl.BlockSpec((slots, 2 * ROWS, width), lambda j: (0, 0, 0)),
            pl.BlockSpec((width, chunk), lambda j: (0, j)),
            pl.BlockSpec((width, chunk), lambda j: (0, steps + j)),
            pl.BlockSpec((width, chunk), lambda j: (0, 2 * steps + j)),
        ],
        out_specs=[
            pl.BlockSpec((width, 3 * chunk), lambda j: (0, j)),
            row_spec,
            row_spec,
            row_spec,
        ],
        out_shape=[jax.ShapeDtypeStruct((width, 3 * ff), BF16)]
        + [jax.ShapeDtypeStruct((rows, ff), BF16)] * 3,
        compiler_params=params(),
        cost_estimate=cost(12 * rows * width * ff, 24 * width * ff),
        name="grads",
    )(came, weight, weight, weight)
    summed = lax.psum_scatter(partial, "dp", scatter_dimension=0, tiled=True)
    block = 256
    whole = pl.BlockSpec((rows, ff), lambda j: (0, 0))
    back = pl.pallas_call(
        back_kernel,
        grid=(width // block,),
        in_specs=[whole, whole, whole, pl.BlockSpec((block, 3 * ff), lambda j: (j, 0))],
        out_specs=pl.BlockSpec((slots, 2 * ROWS, block), lambda j: (0, 0, j)),
        out_shape=pair,
        compiler_params=params(),
        cost_estimate=cost(6 * rows * width * ff, 12 * width * ff),
        name="back",
    )(h, qg, qu, weight)
    home = lax.all_to_all(back, "expert", split_axis=0, concat_axis=0, tiled=True)
    layer_out, grad_tokens = pl.pallas_call(
        combine_kernel,
        out_shape=[jax.ShapeDtypeStruct((count, width), BF16)] * 2,
        compiler_params=params(),
        cost_estimate=cost(6 * rows * count * width, 6 * rows * width),
        name="combine",
    )(routes_t, gates_t, home)
    half = width // 2 // groups
    upper = (lax.axis_index("expert") >= slots // 2).astype(jnp.int32)
    other = lax.dynamic_slice_in_dim(summed, (1 - upper) * half, half, 0)
    route = [((i + slots // 2) % slots, i) for i in range(slots)]
    came_half = lax.ppermute(other, "expert", route)
    total = pl.pallas_call(
        join_kernel,
        in_specs=[pl.BlockSpec(memory_space=pltpu.SMEM)] + [pl.BlockSpec(memory_space=pltpu.VMEM)] * 2,
        out_shape=jax.ShapeDtypeStruct((1, half, 3 * ff), BF16),
        compiler_params=params(),
        name="join",
    )(upper.reshape(1), summed, came_half)
    return (layer_out, grad_tokens, total)


def solution(mesh):
    placed = (
        P(("dp", "expert"), None),
        P(("dp", "expert"), None),
        P(("dp", "expert"), None),
        P(("dp", "expert"), None),
        P("expert", None, None),
    )
    return jax.shard_map(
        local,
        mesh=mesh,
        in_specs=placed,
        out_specs=(P(("dp", "expert"), None), P(("dp", "expert"), None), P("expert", "dp", None)),
        check_vma=False,
    )
```

time: 345 us -> 222 us (0.64); the launches traced: 341 us -> 222 us
  waiting for transfers between devices: 168 us -> 99.7 us
  blocking collectives: 0 us -> 56.3 us
  local copies, waits for them, and re-layouts: 53.9 us -> 1.92 us
  Pallas kernels: 0 us -> 42.2 us
  other arithmetic: 42.2 us -> 0 us
  matrix products: 29.5 us -> 0 us
  starting transfers between devices: 33.1 us -> 7.43 us
    ppermute x1, waiting for transfers between devices: 103 us -> 11.8 us  [local(): came_half = lax.ppermute(other, 'expert', route)]
    reduce_scatter x0 -> x1, waiting for transfers between devices: none -> 87.9 us  [local(): summed = lax.psum_scatter(partial, 'dp', scatter_dimension=0, tiled=True)]
    all_to_all x4 -> x1, waiting for transfers between devices: 65.2 us -> 0.01 us  [local(): lax.all_to_all(back, 'expert', split_axis=0, concat_axis=0, tiled=True)]
    all_to_all x0 -> x1, blocking collectives: none -> 56.3 us  [local(): lax.all_to_all(sent, 'expert', split_axis=0, concat_axis=0, tiled=True)]
    pallas_call x0 -> x5, Pallas kernels: none -> 42.2 us  [the longest x1 19.4 us: local(): pl.pallas_call(grads_kernel, grid=(steps,), in_specs=[pl.BlockSpec((slots...]
    convert_element_type x5 -> x0, other arithmetic: 30.6 us -> none  [the longest x1 10.2 us: local(): both_terms.astype(jnp.bfloat16)]
    dot_general x6 -> x0, matrix products: 29.5 us -> none  [the longest x1 7.91 us: forward_rows(): jnp.dot(rows_x, weight[:, :2 * hidden_width], preferred_element_type=jnp....]
    all_to_all x4 -> x1, starting transfers between devices: 29.6 us -> 6.76 us  [local(): lax.all_to_all(back, 'expert', split_axis=0, concat_axis=0, tiled=True)]
  transfers between devices with their start and end apart: 6 -> 3, of which waited for: 5 -> 2; matrix products, arithmetic and copies ran while one was open for 17% -> 0% of each run, Pallas kernels for 0% -> 7%
where the time goes in v1:
time: 222 us
  waiting for transfers between devices  99.7 us (45%)
  blocking collectives  56.3 us (25%)
  Pallas kernels  42.2 us (19%)
  between operations  14.1 us (6%)
  starting transfers between devices  7.43 us (3%)
    reduce_scatter x1, waiting for transfers between devices, local(): summed = lax.psum_scatter(partial, 'dp', scatter_dimension=0, tiled=True)  87.9 us
    all_to_all x1, blocking collectives, local(): lax.all_to_all(sent, 'expert', split_axis=0, concat_axis=0, tiled=True)  56.3 us
    pallas_call x1, Pallas kernels, local(): pl.pallas_call(grads_kernel, grid=(steps,), in_specs=[pl.BlockSpec((slots...  19.4 us
    ppermute x1, waiting for transfers between devices, local(): came_half = lax.ppermute(other, 'expert', route)  11.8 us
    pallas_call x1, Pallas kernels, local(): pl.pallas_call(back_kernel, grid=(width // block,), in_specs=[whole, whol...  11.6 us
    all_to_all x1, starting transfers between devices, local(): lax.all_to_all(back, 'expert', split_axis=0, concat_axis=0, tiled=True)  6.76 us
    pallas_call x1, Pallas kernels, local(): pl.pallas_call(pack_kernel, out_shape=pair, compiler_params=params(), cos...  4.58 us
  transfers between devices with their start and end apart: 3, of which 2 were waited for; matrix products, arithmetic and copies ran while one was open for 0% of the time, Pallas kernels for 7%

profile of v1, /device:TPU:4, one launch (start us, length us, event | category | flops | bytes accessed | tf_op | source)
XLA Modules:
  0.0 221.6 jit_solution(14652624567678165821)
XLA Ops:
  7.2 0.0 reduce-scatter.2.cloned.1.call-start
  7.2 4.6 %pack.1 = bf16[32,32,2048]{2,1,0:T(8,128)(2,1)} custom-call(s32[2,128]{1,0:T(2,128)} %bitcast.4, f32[2,128]{1,0:T(2,128)} %bitcast.6, bf16[128,2048]{1,0:T(8,128)(2,1)} %tokens_ref.1, bf16[128,2048]{1,0:T(8,128)(2,1)} %out_grad_ref.1), custom_call_target="tpu_custom_call" | custom-call | flops 536870912 | bytes 6291456 | tf_op jit(solution)/shard_map/pack/pallas_call | solution.py:149
  11.8 56.3 %all_to_all.10.rows_ref = bf16[32,32,2048]{2,1,0:T(8,128)(2,1)} all-to-all(bf16[32,32,2048]{2,1,0:T(8,128)(2,1)} %pack.1), channel_id=1, replica_groups=mesh['dp'=8,'expert'=32] {'expert'}, dimensions={0} | all-to-all | bytes 8388608 | tf_op jit(solution)/shard_map/all_to_all | solution.py:156
  68.1 19.4 %grads.1 = (bf16[2048,2304]{1,0:T(8,128)(2,1)}, bf16[512,768]{1,0:T(8,128)(2,1)}, bf16[512,768]{1,0:T(8,128)(2,1)}, bf16[512,768]{1,0:T(8,128)(2,1)}) custom-call(bf16[32,32,2048]{2,1,0:T(8,128)(2,1)} %all_to_all.10.rows_ref, bf16[2048,2304]{1,0:T(8,128)(2,1)} %bitcast.8, bf16[2048,2304]{1,0:T(8,128)(2,1)} %bitcast.9, bf16[2048,2304]{1,0:T(8,128)(2,1)} %bitcast.10), custom_call_target="tpu_custom_call" | custom-call | flops 9663676416 | bytes 37748736 | tf_op jit(solution)/shard_map/grads/pallas_call | solution.py:158
  87.4 0.0 reduce-scatter.2.cloned.1.call-update
  87.5 11.6 %back.1 = bf16[32,32,2048]{2,1,0:T(8,128)(2,1)} custom-call(bf16[512,768]{1,0:T(8,128)(2,1)} %get-tuple-element.9.h_ref, bf16[512,768]{1,0:T(8,128)(2,1)} %get-tuple-element.10.qg_ref, bf16[512,768]{1,0:T(8,128)(2,1)} %get-tuple-element.11.qu_ref, bf16[2048,2304]{1,0:T(8,128)(2,1)} %bitcast.11), custom_call_target="tpu_custom_call" | custom-call | flops 4831838208 | bytes 18874368 | tf_op jit(solution)/shard_map/back/pallas_call | solution.py:182
  99.0 6.8 %all-to-all-start.1 = ((bf16[32,32,2048]{2,1,0:T(8,128)(2,1)}), bf16[32,32,2048]{2,1,0:T(8,128)(2,1)}, u32[]{:S(2)}, u32[]{:S(2)}) async-start(bf16[32,32,2048]{2,1,0:T(8,128)(2,1)} %back.1), calls=%async_computation.1 | async-start | bytes 8388608 | tf_op jit(solution)/shard_map/all_to_all | solution.py:192
  105.8 87.9 %reduce-scatter.2.cloned.1.call-done.summed_ref = bf16[256,2304]{1,0:T(8,128)(2,1)} async-done(((bf16[2048,2304]{1,0:T(8,128)(2,1)}), bf16[256,2304]{1,0:T(8,128)(2,1)}) %reduce-scatter.2.cloned.1.call-update) | async-done | bytes 1179664 | tf_op jit(solution)/shard_map/reduce_scatter | solution.py:179
  193.8 1.1 constant_dynamic-slice_fusion
  194.9 0.6 collective-permute-start
  195.5 0.0 all-to-all-done.1.back_ref
  195.5 4.3 %combine.1 = (bf16[128,2048]{1,0:T(8,128)(2,1)}, bf16[128,2048]{1,0:T(8,128)(2,1)}) custom-call(s32[2,128]{1,0:T(2,128)} %bitcast.5, f32[2,128]{1,0:T(2,128)} %bitcast.7, bf16[32,32,2048]{2,1,0:T(8,128)(2,1)} %all-to-all-done.1.back_ref), custom_call_target="tpu_custom_call" | custom-call | flops 805306368 | bytes 6291456 | tf_op jit(solution)/shard_map/combine/pallas_call | solution.py:193
  199.8 11.8 %collective-permute-done.came_ref = bf16[128,2304]{1,0:T(8,128)(2,1)S(1)} collective-permute-done((bf16[128,2304]{1,0:T(8,128)(2,1)S(1)}, bf16[128,2304]{1,0:T(8,128)(2,1)S(1)}, u32[]{:S(2)}, u32[]{:S(2)}) %collective-permute-start) | collective-permute-done | bytes 589856 | tf_op jit(solution)/shard_map/ppermute | solution.py:204
  211.6 0.0 copy-start
  211.6 0.8 copy-done
  212.4 2.4 %join.1 = bf16[1,128,2304]{2,1,0:T(8,128)(2,1)} custom-call(s32[1]{0:T(128)} %bitcast.3.which_ref, bf16[256,2304]{1,0:T(8,128)(2,1)} %reduce-scatter.2.cloned.1.call-done.summed_ref, bf16[128,2304]{1,0:T(8,128)(2,1)} %copy-done), custom_call_target="tpu_custom_call" | custom-call | tf_op jit(solution)/shard_map/join/pallas_call | solution.py:205
Async XLA Ops:
  7.2 186.6 %reduce-scatter.2.cloned.1.call-start = ((), (), s32[]{:S(2)}) async-start(), calls=%async_computation.3 | async-start | bytes 10616832 | tf_op jit(solution)/shard_map/reduce_scatter | solution.py:179
  99.0 96.5 %all-to-all-start.1 = ((bf16[32,32,2048]{2,1,0:T(8,128)(2,1)}), bf16[32,32,2048]{2,1,0:T(8,128)(2,1)}, u32[]{:S(2)}, u32[]{:S(2)}) async-start(bf16[32,32,2048]{2,1,0:T(8,128)(2,1)} %back.1), calls=%async_computation.1 | async-start | bytes 8388608 | tf_op jit(solution)/shard_map/all_to_all | solution.py:192
  194.9 16.7 %collective-permute-start = (bf16[128,2304]{1,0:T(8,128)(2,1)S(1)}, bf16[128,2304]{1,0:T(8,128)(2,1)S(1)}, u32[]{:S(2)}, u32[]{:S(2)}) collective-permute-start(bf16[128,2304]{1,0:T(8,128)(2,1)S(1)} %constant_dynamic-slice_fusion), channel_id=1, source_target_pairs={{16,0},{17,1},{18,2},{19,3},{20,4},{21,5},{22,6},{23,7},{24,8},{25... | collective-permute-start | bytes 1769480 | tf_op jit(solution)/shard_map/ppermute | solution.py:204
  211.6 0.8 copy-start
Sparse Core Ops, SparseCore 0:
  87.6 106.1 reduce-scatter.1

commit v2 on v1

v2 whole, which is shorter than its diff:
```python
import functools

import jax
import jax.numpy as jnp
from jax import lax
from jax.experimental import pallas as pl
from jax.experimental.pallas import tpu as pltpu
from jax.sharding import PartitionSpec as P

BF16 = jnp.bfloat16
F32 = jnp.float32
ROWS = 16


def dot(a, b, dims):
    return lax.dot_general(a, b, (dims, ((), ())), preferred_element_type=F32)


def dispatch_mask(routes, slots):
    top, tokens = routes.shape
    slot = lax.broadcasted_iota(jnp.int32, (slots, tokens), 0)
    names = [routes[k : k + 1, :] == slot for k in range(top)]
    named = names[0]
    for one in names[1:]:
        named = named | one
    earlier = (
        lax.broadcasted_iota(jnp.int32, (tokens, tokens), 0)
        < lax.broadcasted_iota(jnp.int32, (tokens, tokens), 1)
    )
    place = dot(
        jnp.where(named, 1.0, 0.0).astype(BF16),
        jnp.where(earlier, 1.0, 0.0).astype(BF16),
        ((1,), (0,)),
    ).astype(jnp.int32)
    place = jnp.where(named, place, ROWS)
    at = lax.broadcasted_iota(jnp.int32, (slots, ROWS, tokens), 1)
    return names, place[:, None, :] == at


def slot_gates(names, gates):
    total = jnp.where(names[0], gates[0:1, :], 0.0)
    for k in range(1, len(names)):
        total = total + jnp.where(names[k], gates[k : k + 1, :], 0.0)
    return total


def pack_kernel(routes_ref, gates_ref, tokens_ref, out_grad_ref, send_ref, pick_ref, gate_ref):
    slots, _, step = send_ref.shape

    @pl.when(pl.program_id(0) == 0)
    def _():
        names, mask = dispatch_mask(routes_ref[...], slots)
        weight = slot_gates(names, gates_ref[...])
        gate_ref[...] = jnp.sum(jnp.where(mask, weight[:, None, :], 0.0), axis=2, keepdims=True)
        pick_ref[...] = jnp.where(mask, 1.0, 0.0).reshape(slots * ROWS, -1).astype(BF16)

    pick = pick_ref[...]
    x = dot(pick, tokens_ref[...], ((1,), (0,)))
    send_ref[:, :ROWS, :] = x.astype(BF16).reshape(slots, ROWS, step)
    g = dot(pick, out_grad_ref[...], ((1,), (0,))).reshape(slots, ROWS, step)
    send_ref[:, ROWS:, :] = (gate_ref[...] * g).astype(BF16)


def expert_rows(at, rows_ref, w_ref, qg_ref, qu_ref, h_ref):
    chunk = h_ref.shape[1]
    ff = w_ref.shape[1] // 3
    slots, _, width = rows_ref.shape
    rows = slots * ROWS
    x = rows_ref[:, :ROWS, :].reshape(rows, width)
    dy = rows_ref[:, ROWS:, :].reshape(rows, width)
    a = dot(x, w_ref[:, pl.ds(pl.multiple_of(at * chunk, chunk), chunk)], ((1,), (0,)))
    b = dot(x, w_ref[:, pl.ds(pl.multiple_of(ff + at * chunk, chunk), chunk)], ((1,), (0,)))
    e = dot(dy, w_ref[:, pl.ds(pl.multiple_of(2 * ff + at * chunk, chunk), chunk)], ((1,), (0,)))
    s = jax.nn.sigmoid(a)
    active = a * s
    h_ref[...] = (active * b).astype(BF16)
    qg_ref[...] = (e * b * s * (1.0 + a * (1.0 - s))).astype(BF16)
    qu_ref[...] = (e * active).astype(BF16)


def first_kernel(groups, rows_ref, w_ref, partial_ref, qg_ref, qu_ref, h_ref):
    slots, _, width = rows_ref.shape
    rows = slots * ROWS
    part = pl.program_id(1)
    block = width // 2 // groups

    @pl.when(part == 0)
    def _():
        expert_rows(pl.program_id(0) + 1, rows_ref, w_ref, qg_ref, qu_ref, h_ref)

    for n, rhs_ref in enumerate((qg_ref, qu_ref, h_ref)):

        @pl.when(part == n + 1)
        def _(n=n, rhs_ref=rhs_ref):
            begin = ROWS if n == 2 else 0
            lhs = rows_ref[:, begin : begin + ROWS, :].reshape(rows, width)
            value = dot(lhs, rhs_ref[...], ((0,), (0,))).astype(BF16)
            for half in range(2):
                for d in range(groups):
                    old, new = (half * groups + d) * block, (2 * d + half) * block
                    partial_ref[new : new + block] = value[old : old + block]


def second_kernel(
    which_ref, rows_ref, w_ref, own_ref, sent_ref, qg_ref, qu_ref, h_ref
):
    slots, _, width = rows_ref.shape
    rows, half = slots * ROWS, width // 2
    part = pl.program_id(0)

    @pl.when(part == 0)
    def _():
        expert_rows(0, rows_ref, w_ref, qg_ref, qu_ref, h_ref)

    for n, rhs_ref in enumerate((qg_ref, qu_ref, h_ref)):

        @pl.when(part == n + 1)
        def _(n=n, rhs_ref=rhs_ref):
            begin = ROWS if n == 2 else 0
            for out_ref, which in ((own_ref, which_ref[0]), (sent_ref, 1 - which_ref[0])):
                cols = pl.ds(pl.multiple_of(which * half, half), half)
                lhs = rows_ref[:, begin : begin + ROWS, cols].reshape(rows, half)
                out_ref[...] = dot(lhs, rhs_ref[...], ((0,), (0,))).astype(BF16)


def back_kernel(h0_ref, qg0_ref, qu0_ref, h_ref, qg_ref, qu_ref, w_ref, out_ref):
    slots, _, block = out_ref.shape
    chunk = h0_ref.shape[1]
    ff = w_ref.shape[1] // 3
    lines = pl.ds(pl.multiple_of(pl.program_id(0) * block, block), block)

    def product(first_ref, rest_ref, base):
        value = dot(first_ref[...], w_ref[lines, base : base + chunk], ((1,), (1,)))
        return value + dot(rest_ref[...], w_ref[lines, base + chunk : base + ff], ((1,), (1,)))

    y = product(h0_ref, h_ref, 2 * ff)
    out_ref[:, :ROWS, :] = y.astype(BF16).reshape(slots, ROWS, block)
    dx = product(qg0_ref, qg_ref, 0) + product(qu0_ref, qu_ref, ff)
    out_ref[:, ROWS:, :] = dx.astype(BF16).reshape(slots, ROWS, block)


def combine_kernel(routes_ref, gates_ref, back_ref, layer_ref, grad_ref):
    slots, _, width = back_ref.shape
    names, mask = dispatch_mask(routes_ref[...], slots)
    weight = slot_gates(names, gates_ref[...])
    rows = slots * ROWS
    gate = jnp.where(mask, weight[:, None, :], 0.0).reshape(rows, -1)
    high = gate.astype(BF16)
    low = (gate - high.astype(F32)).astype(BF16)
    pick = jnp.where(mask, 1.0, 0.0).reshape(rows, -1).astype(BF16)
    step = 512
    for c in range(0, width, step):
        cols = slice(c, c + step)
        y = back_ref[:, :ROWS, cols].reshape(rows, step)
        value = dot(high, y, ((0,), (0,))) + dot(low, y, ((0,), (0,)))
        layer_ref[:, cols] = value.astype(BF16)
        dx = back_ref[:, ROWS:, cols].reshape(rows, step)
        grad_ref[:, cols] = dot(pick, dx, ((0,), (0,))).astype(BF16)


def join_kernel(which_ref, early_ref, came_ref, late_ref, out_ref):
    half, columns = came_ref.shape
    chunk = late_ref.shape[1] // 3
    steps = columns // (3 * chunk) + 1
    own = early_ref[pl.ds(pl.multiple_of(which_ref[0] * half, half), half), :]
    total = (own.astype(F32) + came_ref[...].astype(F32)).astype(BF16)
    for n in range(3):
        base = n * steps * chunk
        out_ref[0, :, base : base + chunk] = late_ref[:, n * chunk : (n + 1) * chunk]
        for j in range(1, steps):
            old, new = (3 * (j - 1) + n) * chunk, base + j * chunk
            out_ref[0, :, new : new + chunk] = total[:, old : old + chunk]


def params(mib):
    return pltpu.CompilerParams(vmem_limit_bytes=mib * 1024 * 1024)


def cost(flops, moved):
    return pl.CostEstimate(flops=flops, bytes_accessed=moved, transcendentals=0)


def local(tokens, out_grad, routes, gates, weights):
    slots = lax.axis_size("expert")
    groups = lax.axis_size("dp")
    count, width = tokens.shape
    top = routes.shape[1]
    weight = weights[0]
    ff = weight.shape[1] // 3
    rows = slots * ROWS
    chunk = 256
    steps = ff // chunk
    half = width // 2
    routes_t = routes.T
    gates_t = gates.T
    upper = (lax.axis_index("expert") >= slots // 2).astype(jnp.int32)
    which = upper.reshape(1)
    smem = pl.BlockSpec(memory_space=pltpu.SMEM)
    vmem = pl.BlockSpec(memory_space=pltpu.VMEM)
    pair = pltpu.HBM((slots, 2 * ROWS, width), BF16)
    step = 512
    sent = pl.pallas_call(
        pack_kernel,
        grid=(width // step,),
        in_specs=[
            pl.BlockSpec((top, count), lambda c: (0, 0)),
            pl.BlockSpec((top, count), lambda c: (0, 0)),
            pl.BlockSpec((count, step), lambda c: (0, c)),
            pl.BlockSpec((count, step), lambda c: (0, c)),
        ],
        out_specs=pl.BlockSpec((slots, 2 * ROWS, step), lambda c: (0, 0, c)),
        out_shape=pair,
        scratch_shapes=[pltpu.VMEM((rows, count), BF16), pltpu.VMEM((slots, ROWS, 1), F32)],
        compiler_params=params(56),
        cost_estimate=cost(4 * rows * count * width, 6 * rows * width),
        name="pack",
    )(routes_t, gates_t, tokens, out_grad)
    came = lax.all_to_all(sent, "expert", split_axis=0, concat_axis=0, tiled=True)

    state = jax.ShapeDtypeStruct((rows, ff - chunk), BF16)
    state_spec = pl.BlockSpec((rows, chunk), lambda j, p: (0, j))
    early, qg, qu, h = pl.pallas_call(
        functools.partial(first_kernel, groups),
        grid=(steps - 1, 4),
        in_specs=[vmem, vmem],
        out_specs=[pl.BlockSpec((width, chunk), lambda j, p: (0, 3 * j + jnp.maximum(p - 1, 0)))]
        + [state_spec] * 3,
        out_shape=[pltpu.HBM((width, 3 * (ff - chunk)), BF16)] + [state] * 3,
        compiler_params=params(24),
        cost_estimate=cost(8 * rows * width * ff, 16 * width * ff),
        name="early_grads",
    )(came, weight)
    early_sum = lax.psum_scatter(early, "dp", scatter_dimension=0, tiled=True)
    state = jax.ShapeDtypeStruct((rows, chunk), BF16)
    state_spec = pl.BlockSpec((rows, chunk), lambda p: (0, 0))
    half_spec = pl.BlockSpec((half, chunk), lambda p: (0, jnp.maximum(p - 1, 0)))
    own, sent_half, qg0, qu0, h0 = pl.pallas_call(
        second_kernel,
        grid=(4,),
        in_specs=[smem, vmem, vmem],
        out_specs=[half_spec] * 2 + [state_spec] * 3,
        out_shape=[pltpu.HBM((half, 3 * chunk), BF16)] * 2 + [state] * 3,
        compiler_params=params(24),
        cost_estimate=cost(4 * rows * width * ff, 8 * width * ff),
        name="late_grads",
    )(which, came, weight)
    route = [((i + slots // 2) % slots, i) for i in range(slots)]
    came_half = lax.ppermute(sent_half, "expert", route)
    block = 512
    back = pl.pallas_call(
        back_kernel,
        grid=(width // block,),
        in_specs=[vmem] * 7,
        out_specs=pl.BlockSpec((slots, 2 * ROWS, block), lambda j: (0, 0, j)),
        out_shape=pair,
        compiler_params=params(24),
        cost_estimate=cost(6 * rows * width * ff, 12 * width * ff),
        name="back",
    )(h0, qg0, qu0, h, qg, qu, weight)
    home = lax.all_to_all(back, "expert", split_axis=0, concat_axis=0, tiled=True)
    late = (own.astype(F32) + came_half.astype(F32)).astype(BF16)
    late_sum = lax.psum_scatter(late, "dp", scatter_dimension=0, tiled=True)
    layer_out, grad_tokens = pl.pallas_call(
        combine_kernel,
        out_shape=[jax.ShapeDtypeStruct((count, width), BF16)] * 2,
        compiler_params=params(24),
        cost_estimate=cost(6 * rows * count * width, 6 * rows * width),
        name="combine",
    )(routes_t, gates_t, home)
    kept = half // groups
    other = lax.dynamic_slice_in_dim(early_sum, (1 - upper) * kept, kept, 0)
    came_early = lax.ppermute(other, "expert", route)
    grad_weights = pl.pallas_call(
        join_kernel,
        in_specs=[smem, vmem, vmem, vmem],
        out_shape=jax.ShapeDtypeStruct((1, kept, 3 * ff), BF16),
        compiler_params=params(8),
        name="join",
    )(which, early_sum, came_early, late_sum)
    return (layer_out, grad_tokens, grad_weights)


def solution(mesh):
    placed = (
        P(("dp", "expert"), None),
        P(("dp", "expert"), None),
        P(("dp", "expert"), None),
        P(("dp", "expert"), None),
        P("expert", None, None),
    )
    return jax.shard_map(
        local,
        mesh=mesh,
        in_specs=placed,
        out_specs=(P(("dp", "expert"), None), P(("dp", "expert"), None), P("expert", "dp", None)),
        check_vma=False,
    )
```

time: 222 us -> 212 us (0.955)
  waiting for transfers between devices: 99.7 us -> 83.7 us
  local copies, waits for them, and re-layouts: 1.92 us -> 13.1 us
  Pallas kernels: 42.2 us -> 33 us
    reduce_scatter x1 -> x2, waiting for transfers between devices: 87.9 us -> 41.6 us  [the longest x1 24.5 us: local(): early_sum = lax.psum_scatter(early, 'dp', scatter_dimension=0, tiled=True)]
    all_to_all x1, waiting for transfers between devices: 0.01 us -> 18.5 us  [local(): lax.all_to_all(back, 'expert', split_axis=0, concat_axis=0, tiled=True)]
    ppermute x1 -> x2, waiting for transfers between devices: 11.8 us -> 23.6 us  [the longest x1 23.6 us: local(): came_half = lax.ppermute(sent_half, 'expert', route)]
    unnamed x2 -> x20, local copies, waits for them, and re-layouts: 0.82 us -> 12 us
    pallas_call x4 -> x5, Pallas kernels: 37.9 us -> 28.7 us  [the longest x1 10.4 us: local(): pl.pallas_call(functools.partial(first_kernel, groups), grid=(steps - 1,...]
  transfers between devices with their start and end apart: 3 -> 5, of which waited for: 2 -> 4; matrix products, arithmetic and copies ran while one was open for 0% -> 1% of each run, Pallas kernels for 7% -> 8%
where the time goes in v2:
time: 212 us; the launch traced here: 211 us
  waiting for transfers between devices  83.7 us (39%)
  blocking collectives  56.2 us (27%)
  Pallas kernels  33 us (16%)
  between operations  14.1 us (7%)
  local copies, waits for them, and re-layouts  13.1 us (6%)
  starting transfers between devices  9.29 us (4%)
    all_to_all x1, blocking collectives, local(): lax.all_to_all(sent, 'expert', split_axis=0, concat_axis=0, tiled=True)  56.2 us
    reduce_scatter x1, waiting for transfers between devices, local(): early_sum = lax.psum_scatter(early, 'dp', scatter_dimension=0, tiled=True)  24.5 us
    ppermute x1, waiting for transfers between devices, local(): came_half = lax.ppermute(sent_half, 'expert', route)  23.6 us
    all_to_all x1, waiting for transfers between devices, local(): lax.all_to_all(back, 'expert', split_axis=0, concat_axis=0, tiled=True)  18.5 us
    reduce_scatter x1, waiting for transfers between devices, local(): late_sum = lax.psum_scatter(late, 'dp', scatter_dimension=0, tiled=True)  17 us
    unnamed x20, local copies, waits for them, and re-layouts  12 us
    pallas_call x1, Pallas kernels, local(): pl.pallas_call(functools.partial(first_kernel, groups), grid=(steps - 1,...  10.4 us
    pallas_call x1, Pallas kernels, local(): pl.pallas_call(back_kernel, grid=(width // block,), in_specs=[vmem] * 7,...  6.71 us
  transfers between devices with their start and end apart: 5, of which 4 were waited for; matrix products, arithmetic and copies ran while one was open for 1% of the time, Pallas kernels for 8%

profile of v2, /device:TPU:4, one launch (start us, length us, event | category | flops | bytes accessed | tf_op | source)
XLA Modules:
  0.0 211.0 jit_solution(13487481585126780478)
XLA Ops:
  7.2 0.0 reduce-scatter.3.cloned.1.call-start
  7.2 5.1 %pack.1 = bf16[32,32,2048]{2,1,0:T(8,128)(2,1)} custom-call(s32[2,128]{1,0:T(2,128)} %bitcast.7, f32[2,128]{1,0:T(2,128)} %bitcast.9, bf16[128,2048]{1,0:T(8,128)(2,1)} %tokens_ref.1, bf16[128,2048]{1,0:T(8,128)(2,1)} %out_grad_ref.1), custom_call_target="tpu_custom_call" | custom-call | flops 536870912 | bytes 6291456 | tf_op jit(solution)/shard_map/pack/pallas_call | solution.py:202
  12.4 56.2 %all_to_all.10.rows_ref = bf16[32,32,2048]{2,1,0:T(8,128)(2,1)S(1)} all-to-all(bf16[32,32,2048]{2,1,0:T(8,128)(2,1)} %pack.1), channel_id=1, replica_groups=mesh['dp'=8,'expert'=32] {'expert'}, dimensions={0} | all-to-all | bytes 8388608 | tf_op jit(solution)/shard_map/all_to_all | solution.py:218
  68.5 5.2 %copy-done.2 = bf16[1,2048,2304]{2,1,0:T(8,128)(2,1)S(1)} copy-done((bf16[1,2048,2304]{2,1,0:T(8,128)(2,1)S(1)}, bf16[1,2048,2304]{2,1,0:T(8,128)(2,1)}, u32[]{:S(2)}) %copy-start.2) | copy-done | bytes 9437208
  73.7 10.4 %early_grads.1 = (bf16[2048,1536]{1,0:T(8,128)(2,1)}, bf16[512,512]{1,0:T(8,128)(2,1)S(1)}, bf16[512,512]{1,0:T(8,128)(2,1)S(1)}, bf16[512,512]{1,0:T(8,128)(2,1)S(1)}) custom-call(bf16[32,32,2048]{2,1,0:T(8,128)(2,1)S(1)} %all_to_all.10.rows_ref, bf16[2048,2304]{1,0:T(8,128)(2,1)S(1)} %bitcast.4), custom_call_target="tpu_custom_call" | custom-call | flops 6442450944 | bytes 25165824 | tf_op jit(solution)/shard_map/early_grads/pallas_call | solution.py:222
  84.1 0.0 copy-done
  84.1 0.0 reduce-scatter.3.cloned.1.call-update
  84.1 0.0 copy-start.1
  84.1 2.2 %copy-done.1 = bf16[32,32,2048]{2,1,0:T(8,128)(2,1)S(1)} copy-done((bf16[32,32,2048]{2,1,0:T(8,128)(2,1)S(1)}, bf16[32,32,2048]{2,1,0:T(8,128)(2,1)}, u32[]{:S(2)}) %copy-start.1) | copy-done | bytes 4194328
  86.3 3.7 %copy-done.3 = bf16[1,2048,2304]{2,1,0:T(8,128)(2,1)S(1)} copy-done((bf16[1,2048,2304]{2,1,0:T(8,128)(2,1)S(1)}, bf16[1,2048,2304]{2,1,0:T(8,128)(2,1)}, u32[]{:S(2)}) %copy-start.3) | copy-done | bytes 9437208
  90.0 5.6 %late_grads.1 = (bf16[1024,768]{1,0:T(8,128)(2,1)}, bf16[1024,768]{1,0:T(8,128)(2,1)}, bf16[512,256]{1,0:T(8,128)(2,1)S(1)}, bf16[512,256]{1,0:T(8,128)(2,1)S(1)}, bf16[512,256]{1,0:T(8,128)(2,1)S(1)}) custom-call(s32[1]{0:T(128)} %bitcast.2.which_ref, bf16[32,32,2048]{2,1,0:T(8,128)(2,1)S(1)} %copy-done.1, bf16[2048,2304]{1,0:T(8,128)(2,1)S(1)} %bitcast.5), custom_call_target="tpu_custom_call" | custom-call | flops 3221225472 | bytes 12582912 | tf_op jit(solution)/shard_map/late_grads/pallas_call | solution.py:237
  95.6 2.2 %collective-permute-start.1 = (bf16[1024,768]{1,0:T(8,128)(2,1)}, bf16[1024,768]{1,0:T(8,128)(2,1)S(1)}, u32[]{:S(2)}, u32[]{:S(2)}) collective-permute-start(bf16[1024,768]{1,0:T(8,128)(2,1)} %get-tuple-element.24), channel_id=1, source_target_pairs={{16,0},{17,1},{18,2},{19,3},{20,4},{21,5},{22,6},{23,7},{24,8},{25... | collective-permute-start | bytes 4718600 | tf_op jit(solution)/shard_map/ppermute | solution.py:248
  97.8 0.0 copy-done.4
  97.8 6.7 %back.1 = bf16[32,32,2048]{2,1,0:T(8,128)(2,1)} custom-call(bf16[512,256]{1,0:T(8,128)(2,1)S(1)} %get-tuple-element.14.h0_ref, bf16[512,256]{1,0:T(8,128)(2,1)S(1)} %get-tuple-element.15.qg0_ref, bf16[512,256]{1,0:T(8,128)(2,1)S(1)} %get-tuple-element.16.qu0_ref, bf16[512,512]{1,0:T(8,128)(2,1)S(1)} %get-tuple-element.17.h_ref, ...), custom_call_target="tpu_custom_call" | custom-call | flops 4831838208 | bytes 18874368 | tf_op jit(solution)/shard_map/back/pallas_call | solution.py:250
  104.5 6.4 %all-to-all-start.1 = ((bf16[32,32,2048]{2,1,0:T(8,128)(2,1)}), bf16[32,32,2048]{2,1,0:T(8,128)(2,1)}, u32[]{:S(2)}, u32[]{:S(2)}) async-start(bf16[32,32,2048]{2,1,0:T(8,128)(2,1)} %back.1), calls=%async_computation.1 | async-start | bytes 8388608 | tf_op jit(solution)/shard_map/all_to_all | solution.py:260
  110.9 0.0 reduce-scatter.5.cloned.1.call-start
  110.9 23.6 %collective-permute-done.1 = bf16[1024,768]{1,0:T(8,128)(2,1)S(1)} collective-permute-done((bf16[1024,768]{1,0:T(8,128)(2,1)}, bf16[1024,768]{1,0:T(8,128)(2,1)S(1)}, u32[]{:S(2)}, u32[]{:S(2)}) %collective-permute-start.1) | collective-permute-done | bytes 1572896 | tf_op jit(solution)/shard_map/ppermute | solution.py:248
  134.5 0.0 copy-done.9
  134.5 1.6 add_convert_fusion
  136.2 0.0 reduce-scatter.5.cloned.1.call-update
  136.2 24.5 %reduce-scatter.3.cloned.1.call-done.early_ref = bf16[256,1536]{1,0:T(8,128)(2,1)} async-done(((bf16[2048,1536]{1,0:T(8,128)(2,1)}), bf16[256,1536]{1,0:T(8,128)(2,1)}) %reduce-scatter.3.cloned.1.call-update) | async-done | bytes 786448 | tf_op jit(solution)/shard_map/reduce_scatter | solution.py:233
  160.7 1.1 constant_dynamic-slice_fusion
  161.8 0.6 collective-permute-start
  162.5 18.5 %all-to-all-done.1.back_ref = bf16[32,32,2048]{2,1,0:T(8,128)(2,1)} async-done(((bf16[32,32,2048]{2,1,0:T(8,128)(2,1)}), bf16[32,32,2048]{2,1,0:T(8,128)(2,1)}, u32[]{:S(2)}, u32[]{:S(2)}) %all-to-all-start.1) | async-done | bytes 4194336 | tf_op jit(solution)/shard_map/all_to_all | solution.py:260
  181.0 0.0 copy-done.7
  181.0 0.0 copy-done.8
  181.0 4.3 %combine.1 = (bf16[128,2048]{1,0:T(8,128)(2,1)}, bf16[128,2048]{1,0:T(8,128)(2,1)}) custom-call(s32[2,128]{1,0:T(2,128)S(1)} %bitcast.8, f32[2,128]{1,0:T(2,128)S(1)} %bitcast.10, bf16[32,32,2048]{2,1,0:T(8,128)(2,1)} %all-to-all-done.1.back_ref), custom_call_target="tpu_custom_call" | custom-call | flops 805306368 | bytes 6291456 | tf_op jit(solution)/shard_map/combine/pallas_call | solution.py:263
  185.3 17.0 %reduce-scatter.5.cloned.1.call-done.late_ref = bf16[128,768]{1,0:T(8,128)(2,1)} async-done(((bf16[1024,768]{1,0:T(8,128)(2,1)}), bf16[128,768]{1,0:T(8,128)(2,1)}) %reduce-scatter.5.cloned.1.call-update) | async-done | bytes 196624 | tf_op jit(solution)/shard_map/reduce_scatter | solution.py:262
  202.3 0.0 collective-permute-done.came_ref
  202.3 0.0 copy-done.5
  202.3 0.9 copy-done.6
  203.3 0.9 join.1
  (9 shorter events, 0.0 us)
Async XLA Ops:
  7.2 153.6 %reduce-scatter.3.cloned.1.call-start = ((), (), s32[]{:S(2)}) async-start(), calls=%async_computation.4 | async-start | bytes 7077888 | tf_op jit(solution)/shard_map/reduce_scatter | solution.py:233
  68.5 15.6 %copy-start = (bf16[32,32,2048]{2,1,0:T(8,128)(2,1)}, bf16[32,32,2048]{2,1,0:T(8,128)(2,1)S(1)}, u32[]{:S(2)}) copy-start(bf16[32,32,2048]{2,1,0:T(8,128)(2,1)S(1)} %all_to_all.10.rows_ref) | copy-start | bytes 12582916
  68.5 5.2 %copy-start.2 = (bf16[1,2048,2304]{2,1,0:T(8,128)(2,1)S(1)}, bf16[1,2048,2304]{2,1,0:T(8,128)(2,1)}, u32[]{:S(2)}) copy-start(bf16[1,2048,2304]{2,1,0:T(8,128)(2,1)} %param.9) | copy-start | bytes 28311556
  84.1 2.2 %copy-start.1 = (bf16[32,32,2048]{2,1,0:T(8,128)(2,1)S(1)}, bf16[32,32,2048]{2,1,0:T(8,128)(2,1)}, u32[]{:S(2)}) copy-start(bf16[32,32,2048]{2,1,0:T(8,128)(2,1)} %copy-done) | copy-start | bytes 12582916
  86.3 3.7 %copy-start.3 = (bf16[1,2048,2304]{2,1,0:T(8,128)(2,1)S(1)}, bf16[1,2048,2304]{2,1,0:T(8,128)(2,1)}, u32[]{:S(2)}) copy-start(bf16[1,2048,2304]{2,1,0:T(8,128)(2,1)} %param.9) | copy-start | bytes 28311556
  90.0 7.8 %copy-start.4 = (bf16[1,2048,2304]{2,1,0:T(8,128)(2,1)S(1)}, bf16[1,2048,2304]{2,1,0:T(8,128)(2,1)}, u32[]{:S(2)}) copy-start(bf16[1,2048,2304]{2,1,0:T(8,128)(2,1)} %param.9) | copy-start | bytes 28311556
  95.6 38.9 %collective-permute-start.1 = (bf16[1024,768]{1,0:T(8,128)(2,1)}, bf16[1024,768]{1,0:T(8,128)(2,1)S(1)}, u32[]{:S(2)}, u32[]{:S(2)}) collective-permute-start(bf16[1024,768]{1,0:T(8,128)(2,1)} %get-tuple-element.24), channel_id=1, source_target_pairs={{16,0},{17,1},{18,2},{19,3},{20,4},{21,5},{22,6},{23,7},{24,8},{25... | collective-permute-start | bytes 4718600 | tf_op jit(solution)/shard_map/ppermute | solution.py:248
  104.5 30.0 %copy-start.9 = (bf16[1024,768]{1,0:T(8,128)(2,1)S(1)}, bf16[1024,768]{1,0:T(8,128)(2,1)}, u32[]{:S(2)}) copy-start(bf16[1024,768]{1,0:T(8,128)(2,1)} %get-tuple-element.23) | copy-start | bytes 4718596
  104.5 76.5 %all-to-all-start.1 = ((bf16[32,32,2048]{2,1,0:T(8,128)(2,1)}), bf16[32,32,2048]{2,1,0:T(8,128)(2,1)}, u32[]{:S(2)}, u32[]{:S(2)}) async-start(bf16[32,32,2048]{2,1,0:T(8,128)(2,1)} %back.1), calls=%async_computation.1 | async-start | bytes 8388608 | tf_op jit(solution)/shard_map/all_to_all | solution.py:260
  110.9 91.4 %reduce-scatter.5.cloned.1.call-start = ((), (), s32[]{:S(2)}) async-start(), calls=%async_computation.5 | async-start | bytes 1769472 | tf_op jit(solution)/shard_map/reduce_scatter | solution.py:262
  134.5 46.5 %copy-start.7 = (s32[128,2]{0,1:T(2,128)S(1)}, s32[128,2]{0,1:T(2,128)}, u32[]{:S(2)}) copy-start(s32[128,2]{0,1:T(2,128)} %param.7) | copy-start | bytes 3076
  134.5 46.5 %copy-start.8 = (f32[128,2]{0,1:T(2,128)S(1)}, f32[128,2]{0,1:T(2,128)}, u32[]{:S(2)}) copy-start(f32[128,2]{0,1:T(2,128)} %param.8) | copy-start | bytes 3076
  160.7 41.6 %copy-start.5 = (bf16[256,1536]{1,0:T(8,128)(2,1)S(1)}, bf16[256,1536]{1,0:T(8,128)(2,1)}, u32[]{:S(2)}) copy-start(bf16[256,1536]{1,0:T(8,128)(2,1)} %reduce-scatter.3.cloned.1.call-done.early_ref) | copy-start | bytes 2359300
  161.8 40.5 %collective-permute-start = (bf16[128,1536]{1,0:T(8,128)(2,1)S(1)}, bf16[128,1536]{1,0:T(8,128)(2,1)S(1)}, u32[]{:S(2)}, u32[]{:S(2)}) collective-permute-start(bf16[128,1536]{1,0:T(8,128)(2,1)S(1)} %constant_dynamic-slice_fusion), channel_id=1, source_target_pairs={{16,0},{17,1},{18,2},{19,3},{20,4},{21,5},{22,6},{23,7},{24,8},{25... | collective-permute-start | bytes 1179656 | tf_op jit(solution)/shard_map/ppermute | solution.py:272
  202.3 0.9 copy-start.6
Sparse Core Ops, SparseCore 0:
  84.2 76.4 reduce-scatter.2
  163.3 38.9 reduce-scatter.4

commit v3 on v2

v3 whole, which is shorter than its diff:
```python
import functools

import jax
import jax.numpy as jnp
from jax import lax
from jax.experimental import pallas as pl
from jax.experimental.pallas import tpu as pltpu
from jax.sharding import PartitionSpec as P

BF16 = jnp.bfloat16
F32 = jnp.float32
ROWS = 16


def dot(a, b, dims):
    return lax.dot_general(a, b, (dims, ((), ())), preferred_element_type=F32)


def dispatch_mask(routes, slots):
    top, tokens = routes.shape
    slot = lax.broadcasted_iota(jnp.int32, (slots, tokens), 0)
    names = [routes[k : k + 1, :] == slot for k in range(top)]
    named = names[0]
    for one in names[1:]:
        named = named | one
    earlier = (
        lax.broadcasted_iota(jnp.int32, (tokens, tokens), 0)
        < lax.broadcasted_iota(jnp.int32, (tokens, tokens), 1)
    )
    place = dot(
        jnp.where(named, 1.0, 0.0).astype(BF16),
        jnp.where(earlier, 1.0, 0.0).astype(BF16),
        ((1,), (0,)),
    ).astype(jnp.int32)
    place = jnp.where(named, place, ROWS)
    at = lax.broadcasted_iota(jnp.int32, (slots, ROWS, tokens), 1)
    return names, place[:, None, :] == at


def slot_gates(names, gates):
    total = jnp.where(names[0], gates[0:1, :], 0.0)
    for k in range(1, len(names)):
        total = total + jnp.where(names[k], gates[k : k + 1, :], 0.0)
    return total


def pack_kernel(routes_ref, gates_ref, tokens_ref, out_grad_ref, send_ref, pick_ref, gate_ref):
    slots, _, step = send_ref.shape

    @pl.when(pl.program_id(0) == 0)
    def _():
        names, mask = dispatch_mask(routes_ref[...], slots)
        weight = slot_gates(names, gates_ref[...])
        gate_ref[...] = jnp.sum(jnp.where(mask, weight[:, None, :], 0.0), axis=2, keepdims=True)
        pick_ref[...] = jnp.where(mask, 1.0, 0.0).reshape(slots * ROWS, -1).astype(BF16)

    pick = pick_ref[...]
    x = dot(pick, tokens_ref[...], ((1,), (0,)))
    send_ref[:, :ROWS, :] = x.astype(BF16).reshape(slots, ROWS, step)
    g = dot(pick, out_grad_ref[...], ((1,), (0,))).reshape(slots, ROWS, step)
    send_ref[:, ROWS:, :] = (gate_ref[...] * g).astype(BF16)


def expert_rows(rows_ref, g, u, v, qg_ref, qu_ref, h_ref):
    slots, _, width = rows_ref.shape
    rows = slots * ROWS
    x = rows_ref[:, :ROWS, :].reshape(rows, width)
    dy = rows_ref[:, ROWS:, :].reshape(rows, width)
    a = dot(x, g, ((1,), (0,)))
    b = dot(x, u, ((1,), (0,)))
    e = dot(dy, v, ((1,), (0,)))
    s = jax.nn.sigmoid(a)
    active = a * s
    h_ref[...] = (active * b).astype(BF16)
    qg_ref[...] = (e * b * s * (1.0 + a * (1.0 - s))).astype(BF16)
    qu_ref[...] = (e * active).astype(BF16)


def early_kernel(plan, groups, rows_ref, w_ref, partial_ref, qg_ref, qu_ref, h_ref):
    slots, _, width = rows_ref.shape
    rows = slots * ROWS
    block = width // 2 // groups
    refs = (qg_ref, qu_ref, h_ref)
    for step, (j, n) in enumerate(plan):

        @pl.when(pl.program_id(0) == step)
        def _(j=j, n=n):
            if n is None:
                chunk, ff = h_ref.shape[1], w_ref.shape[1] // 3
                begins = [n * ff + j * chunk for n in range(3)]
                expert_rows(rows_ref, *(w_ref[:, at : at + chunk] for at in begins), *refs)
                return
            begin = ROWS if n == 2 else 0
            lhs = rows_ref[:, begin : begin + ROWS, :].reshape(rows, width)
            value = dot(lhs, refs[n][...], ((0,), (0,))).astype(BF16)
            for half in range(2):
                for d in range(groups):
                    old, new = (half * groups + d) * block, (2 * d + half) * block
                    partial_ref[new : new + block] = value[old : old + block]


def late_kernel(
    plan,
    which_ref,
    rows_ref,
    g_ref,
    u_ref,
    v_ref,
    kept_ref,
    own_ref,
    sent_ref,
    qg_ref,
    qu_ref,
    h_ref,
):
    slots, _, width = rows_ref.shape
    rows, half = slots * ROWS, width // 2
    refs = (qg_ref, qu_ref, h_ref)
    for step, (j, n) in enumerate(plan):

        @pl.when(pl.program_id(0) == step)
        def _(j=j, n=n):
            if n is None:
                expert_rows(rows_ref, g_ref[...], u_ref[...], v_ref[...], *refs)
                return
            rhs = refs[n][...] if j == 0 else kept_ref[...]
            begin = ROWS if n == 2 else 0
            for out_ref, which in ((own_ref, which_ref[0]), (sent_ref, 1 - which_ref[0])):
                cols = pl.ds(pl.multiple_of(which * half, half), half)
                lhs = rows_ref[:, begin : begin + ROWS, cols].reshape(rows, half)
                out_ref[...] = dot(lhs, rhs, ((0,), (0,))).astype(BF16)


def back_kernel(h0_ref, qg0_ref, qu0_ref, h_ref, qg_ref, qu_ref, w_ref, y_ref, dx_ref):
    slots, _, block = y_ref.shape
    chunk = h0_ref.shape[1]
    ff = w_ref.shape[1] // 3

    def product(first_ref, rest_ref, base):
        value = dot(first_ref[...], w_ref[:, base : base + chunk], ((1,), (1,)))
        return value + dot(rest_ref[...], w_ref[:, base + chunk : base + ff], ((1,), (1,)))

    y = product(h0_ref, h_ref, 2 * ff)
    y_ref[...] = y.astype(BF16).reshape(slots, ROWS, block)
    dx = product(qg0_ref, qg_ref, 0) + product(qu0_ref, qu_ref, ff)
    dx_ref[...] = dx.astype(BF16).reshape(slots, ROWS, block)


def layer_kernel(routes_ref, gates_ref, y_ref, out_ref):
    slots, _, width = y_ref.shape
    names, mask = dispatch_mask(routes_ref[...], slots)
    weight = slot_gates(names, gates_ref[...])
    rows = slots * ROWS
    gate = jnp.where(mask, weight[:, None, :], 0.0).reshape(rows, -1)
    high = gate.astype(BF16)
    low = (gate - high.astype(F32)).astype(BF16)
    step = 512
    for c in range(0, width, step):
        y = y_ref[:, :, c : c + step].reshape(rows, step)
        value = dot(high, y, ((0,), (0,))) + dot(low, y, ((0,), (0,)))
        out_ref[:, c : c + step] = value.astype(BF16)


def tokens_kernel(routes_ref, dx_ref, out_ref):
    slots, _, width = dx_ref.shape
    rows = slots * ROWS
    mask = dispatch_mask(routes_ref[...], slots)[1]
    pick = jnp.where(mask, 1.0, 0.0).reshape(rows, -1).astype(BF16)
    step = 512
    for c in range(0, width, step):
        dx = dx_ref[:, :, c : c + step].reshape(rows, step)
        out_ref[:, c : c + step] = dot(pick, dx, ((0,), (0,))).astype(BF16)


def join_kernel(early_plan, late_plan, which_ref, early_ref, came_ref, late_ref, out_ref):
    half, columns = came_ref.shape
    chunk = columns // len(early_plan)
    steps = out_ref.shape[2] // 3 // chunk
    own = early_ref[pl.ds(pl.multiple_of(which_ref[0] * half, half), half), :]
    total = (own.astype(F32) + came_ref[...].astype(F32)).astype(BF16)
    for plan, value in ((early_plan, total), (late_plan, late_ref[...])):
        for i, (j, n) in enumerate(plan):
            new = (n * steps + j) * chunk
            out_ref[0, :, new : new + chunk] = value[:, i * chunk : (i + 1) * chunk]


def params(mib):
    return pltpu.CompilerParams(vmem_limit_bytes=mib * 1024 * 1024)


def cost(flops, moved):
    return pl.CostEstimate(flops=flops, bytes_accessed=moved, transcendentals=0)


def local(tokens, out_grad, routes, gates, weights):
    slots = lax.axis_size("expert")
    groups = lax.axis_size("dp")
    count, width = tokens.shape
    top = routes.shape[1]
    weight = weights[0]
    ff = weight.shape[1] // 3
    rows = slots * ROWS
    chunk = 256
    steps = ff // chunk
    half = width // 2
    routes_t = routes.T
    gates_t = gates.T
    upper = (lax.axis_index("expert") >= slots // 2).astype(jnp.int32)
    which = upper.reshape(1)
    smem = pl.BlockSpec(memory_space=pltpu.SMEM)
    vmem = pl.BlockSpec(memory_space=pltpu.VMEM)
    pair = pltpu.HBM((slots, 2 * ROWS, width), BF16)
    step = 512
    sent = pl.pallas_call(
        pack_kernel,
        grid=(width // step,),
        in_specs=[
            pl.BlockSpec((top, count), lambda c: (0, 0)),
            pl.BlockSpec((top, count), lambda c: (0, 0)),
            pl.BlockSpec((count, step), lambda c: (0, c)),
            pl.BlockSpec((count, step), lambda c: (0, c)),
        ],
        out_specs=pl.BlockSpec((slots, 2 * ROWS, step), lambda c: (0, 0, c)),
        out_shape=pair,
        scratch_shapes=[pltpu.VMEM((rows, count), BF16), pltpu.VMEM((slots, ROWS, 1), F32)],
        compiler_params=params(24),
        cost_estimate=cost(4 * rows * count * width, 6 * rows * width),
        name="pack",
    )(routes_t, gates_t, tokens, out_grad)
    came = lax.all_to_all(sent, "expert", split_axis=0, concat_axis=0, tiled=True)

    early_plan = ((1, None), (1, 0), (1, 1), (2, None), (2, 0), (2, 1), (2, 2))
    late_plan = ((0, None), (0, 0), (0, 1), (0, 2), (1, 2))
    early_cols = tuple(one for one in early_plan if one[1] is not None)
    late_cols = tuple(one for one in late_plan if one[1] is not None)
    state = jax.ShapeDtypeStruct((rows, ff - chunk), BF16)
    state_spec = pl.BlockSpec((rows, chunk), lambda p: (0, jnp.where(p >= 3, 1, 0)))
    early, qg, qu, h = pl.pallas_call(
        functools.partial(early_kernel, early_plan, groups),
        grid=(len(early_plan),),
        in_specs=[vmem, vmem],
        out_specs=[
            pl.BlockSpec(
                (width, chunk), lambda p: (0, p - jnp.where(p > 0, 1, 0) - jnp.where(p > 3, 1, 0))
            )
        ]
        + [state_spec] * 3,
        out_shape=[pltpu.HBM((width, len(early_cols) * chunk), BF16)] + [state] * 3,
        compiler_params=params(16),
        cost_estimate=cost(8 * rows * width * ff, 16 * width * ff),
        name="early_grads",
    )(came, weight)
    early_sum = lax.psum_scatter(early, "dp", scatter_dimension=0, tiled=True)
    state = jax.ShapeDtypeStruct((rows, chunk), BF16)
    state_spec = pl.BlockSpec((rows, chunk), lambda p: (0, 0))
    half_spec = pl.BlockSpec((half, chunk), lambda p: (0, jnp.maximum(p - 1, 0)))
    own, sent_half, qg0, qu0, h0 = pl.pallas_call(
        functools.partial(late_kernel, late_plan),
        grid=(len(late_plan),),
        in_specs=[smem, pl.BlockSpec((slots, 2 * ROWS, width), lambda p: (0, 0, 0))]
        + [pl.BlockSpec((width, chunk), lambda p, n=n: (0, n * steps)) for n in range(3)]
        + [state_spec],
        out_specs=[half_spec] * 2 + [state_spec] * 3,
        out_shape=[pltpu.HBM((half, len(late_cols) * chunk), BF16)] * 2 + [state] * 3,
        compiler_params=params(50),
        cost_estimate=cost(4 * rows * width * ff, 8 * width * ff),
        name="late_grads",
    )(which, came, weight, weight, weight, h)
    route = [((i + slots // 2) % slots, i) for i in range(slots)]
    came_half = lax.ppermute(sent_half, "expert", route)
    block = 512
    y, dx = pl.pallas_call(
        back_kernel,
        grid=(width // block,),
        in_specs=[pl.BlockSpec((rows, chunk), lambda j: (0, 0))] * 3
        + [pl.BlockSpec((rows, ff - chunk), lambda j: (0, 0))] * 3
        + [pl.BlockSpec((block, 3 * ff), lambda j: (j, 0))],
        out_specs=[pl.BlockSpec((slots, ROWS, block), lambda j: (0, 0, j))] * 2,
        out_shape=[pltpu.HBM((slots, ROWS, width), BF16)] * 2,
        compiler_params=params(50),
        cost_estimate=cost(6 * rows * width * ff, 12 * width * ff),
        name="back",
    )(h0, qg0, qu0, h, qg, qu, weight)
    y = lax.all_to_all(y, "expert", split_axis=0, concat_axis=0, tiled=True)
    y, own = lax.optimization_barrier((y, own))
    dx = lax.all_to_all(dx, "expert", split_axis=0, concat_axis=0, tiled=True)
    late = (own.astype(F32) + came_half.astype(F32)).astype(BF16)
    late_sum = lax.psum_scatter(late, "dp", scatter_dimension=0, tiled=True)
    layer_out = pl.pallas_call(
        layer_kernel,
        out_shape=jax.ShapeDtypeStruct((count, width), BF16),
        compiler_params=params(24),
        cost_estimate=cost(4 * rows * count * width, 3 * rows * width),
        name="layer",
    )(routes_t, gates_t, y)
    grad_tokens = pl.pallas_call(
        tokens_kernel,
        out_shape=jax.ShapeDtypeStruct((count, width), BF16),
        compiler_params=params(24),
        cost_estimate=cost(2 * rows * count * width, 3 * rows * width),
        name="tokens",
    )(routes_t, dx)
    kept = half // groups
    other = lax.dynamic_slice_in_dim(early_sum, (1 - upper) * kept, kept, 0)
    came_early = lax.ppermute(other, "expert", route)
    grad_weights = pl.pallas_call(
        functools.partial(join_kernel, early_cols, late_cols),
        in_specs=[smem, vmem, vmem, vmem],
        out_shape=jax.ShapeDtypeStruct((1, kept, 3 * ff), BF16),
        compiler_params=params(8),
        name="join",
    )(which, early_sum, came_early, late_sum)
    return (layer_out, grad_tokens, grad_weights)


def solution(mesh):
    placed = (
        P(("dp", "expert"), None),
        P(("dp", "expert"), None),
        P(("dp", "expert"), None),
        P(("dp", "expert"), None),
        P("expert", None, None),
    )
    return jax.shard_map(
        local,
        mesh=mesh,
        in_specs=placed,
        out_specs=(P(("dp", "expert"), None), P(("dp", "expert"), None), P("expert", "dp", None)),
        check_vma=False,
    )
```

time: 212 us -> 218 us (1.028)
  blocking collectives: 56.2 us -> 117 us
  waiting for transfers between devices: 83.7 us -> 31.3 us
  local copies, waits for them, and re-layouts: 13.1 us -> 5.41 us
  Pallas kernels: 33 us -> 37.7 us
    all_to_all x0 -> x1, blocking collectives: none -> 61 us  [local(): y = lax.all_to_all(y, 'expert', split_axis=0, concat_axis=0, tiled=True)]
    reduce_scatter x1, waiting for transfers between devices: 24.5 us -> 0.02 us  [local(): early_sum = lax.psum_scatter(early, 'dp', scatter_dimension=0, tiled=True)]
    ppermute x1, waiting for transfers between devices: 23.6 us -> 0.01 us  [local(): came_half = lax.ppermute(sent_half, 'expert', route)]
    reduce_scatter x1, waiting for transfers between devices: 17 us -> 6.8 us  [local(): late_sum = lax.psum_scatter(late, 'dp', scatter_dimension=0, tiled=True)]
    unnamed x20 -> x22, local copies, waits for them, and re-layouts: 12 us -> 4.41 us
    pallas_call x5 -> x6, Pallas kernels: 27.9 us -> 33.9 us  [the longest x1 9.56 us: local(): pl.pallas_call(functools.partial(late_kernel, late_plan), grid=(len(late_...]
    all_to_all x1, waiting for transfers between devices: 18.5 us -> 24.5 us  [local(): dx = lax.all_to_all(dx, 'expert', split_axis=0, concat_axis=0, tiled=True)]
  transfers between devices with their start and end apart: 5 -> 5, of which waited for: 4 -> 2; matrix products, arithmetic and copies ran while one was open for 1% -> 2% of each run, Pallas kernels for 8% -> 11%
where the time goes in v3:
time: 218 us; the launch traced here: 217 us
  blocking collectives  117 us (54%)
  Pallas kernels  37.7 us (17%)
  waiting for transfers between devices  31.3 us (14%)
  between operations  14.1 us (6%)
  starting transfers between devices  9.28 us (4%)
  local copies, waits for them, and re-layouts  5.41 us (2%)
  other arithmetic  2.34 us (1%)
    all_to_all x1, blocking collectives, local(): y = lax.all_to_all(y, 'expert', split_axis=0, concat_axis=0, tiled=True)  61 us
    all_to_all x1, blocking collectives, local(): lax.all_to_all(sent, 'expert', split_axis=0, concat_axis=0, tiled=True)  56.3 us
    all_to_all x1, waiting for transfers between devices, local(): dx = lax.all_to_all(dx, 'expert', split_axis=0, concat_axis=0, tiled=True)  24.5 us
    pallas_call x1, Pallas kernels, local(): pl.pallas_call(functools.partial(late_kernel, late_plan), grid=(len(late_...  9.56 us
    pallas_call x1, Pallas kernels, local(): pl.pallas_call(functools.partial(early_kernel, early_plan, groups), grid=...  9.51 us
    pallas_call x1, Pallas kernels, local(): pl.pallas_call(back_kernel, grid=(width // block,), in_specs=[pl.BlockSpe...  9.25 us
    reduce_scatter x1, waiting for transfers between devices, local(): late_sum = lax.psum_scatter(late, 'dp', scatter_dimension=0, tiled=True)  6.8 us
    all_to_all x1, starting transfers between devices, local(): dx = lax.all_to_all(dx, 'expert', split_axis=0, concat_axis=0, tiled=True)  6.41 us
  transfers between devices with their start and end apart: 5, of which 2 were waited for; matrix products, arithmetic and copies ran while one was open for 2% of the time, Pallas kernels for 11%

profile of v3, /device:TPU:4, one launch (start us, length us, event | category | flops | bytes accessed | tf_op | source)
XLA Modules:
  0.0 217.4 jit_solution(7894617731484106141)
XLA Ops:
  7.2 0.0 reduce-scatter.3.cloned.1.call-start
  7.2 0.0 copy-start.3
  7.2 1.0 copy-done.3
  8.3 1.0 copy-done.4
  9.3 0.7 copy-done.6
  10.0 0.7 copy-done.8
  10.7 3.7 %pack.1 = bf16[32,32,2048]{2,1,0:T(8,128)(2,1)} custom-call(s32[2,128]{1,0:T(2,128)S(1)} %bitcast.9, f32[2,128]{1,0:T(2,128)S(1)} %bitcast.12, bf16[128,2048]{1,0:T(8,128)(2,1)S(1)} %copy-done.3, bf16[128,2048]{1,0:T(8,128)(2,1)S(1)} %copy-done.4), custom_call_target="tpu_custom_call" | custom-call | flops 536870912 | bytes 6291456 | tf_op jit(solution)/shard_map/pack/pallas_call | solution.py:214
  14.4 56.3 %all_to_all.15.rows_ref = bf16[32,32,2048]{2,1,0:T(8,128)(2,1)S(1)} all-to-all(bf16[32,32,2048]{2,1,0:T(8,128)(2,1)} %pack.1), channel_id=1, replica_groups=mesh['dp'=8,'expert'=32] {'expert'}, dimensions={0} | all-to-all | bytes 8388608 | tf_op jit(solution)/shard_map/all_to_all | solution.py:230
  70.7 9.5 %early_grads.1 = (bf16[2048,1280]{1,0:T(8,128)(2,1)}, bf16[512,512]{1,0:T(8,128)(2,1)S(1)}, bf16[512,512]{1,0:T(8,128)(2,1)S(1)}, bf16[512,512]{1,0:T(8,128)(2,1)S(1)}) custom-call(bf16[32,32,2048]{2,1,0:T(8,128)(2,1)S(1)} %all_to_all.15.rows_ref, bf16[2048,2304]{1,0:T(8,128)(2,1)S(1)} %bitcast.8), custom_call_target="tpu_custom_call" | custom-call | flops 6442450944 | bytes 25165824 | tf_op jit(solution)/shard_map/early_grads/pallas_call | solution.py:238
  80.2 0.0 reduce-scatter.3.cloned.1.call-update
  80.2 0.2 reduce-scatter.5.cloned.1.call-start
  80.4 9.6 %late_grads.1 = (bf16[1024,1024]{1,0:T(8,128)(2,1)}, bf16[1024,1024]{1,0:T(8,128)(2,1)}, bf16[512,256]{1,0:T(8,128)(2,1)S(1)}, bf16[512,256]{1,0:T(8,128)(2,1)S(1)}, bf16[512,256]{1,0:T(8,128)(2,1)S(1)}) custom-call(s32[1]{0:T(128)} %bitcast.2.which_ref, bf16[32,32,2048]{2,1,0:T(8,128)(2,1)} %copy-done.1, bf16[2048,2304]{1,0:T(8,128)(2,1)} %bitcast.4, ...), custom_call_target="tpu_custom_call" | custom-call | flops 3221225472 | bytes 12582912 | tf_op jit(solution)/shard_map/late_grads/pallas_call | solution.py:257
  90.0 2.2 %collective-permute-start.1 = (bf16[1024,1024]{1,0:T(8,128)(2,1)}, bf16[1024,1024]{1,0:T(8,128)(2,1)S(1)}, u32[]{:S(2)}, u32[]{:S(2)}) collective-permute-start(bf16[1024,1024]{1,0:T(8,128)(2,1)} %get-tuple-element.28), channel_id=1, source_target_pairs={{16,0},{17,1},{18,2},{19,3},{20,4},{21,5},{22,6},{23,7},{24,8},{25... | collective-permute-start | bytes 6291464 | tf_op jit(solution)/shard_map/ppermute | solution.py:270
  92.2 9.3 %back.1 = (bf16[32,16,2048]{2,1,0:T(8,128)(2,1)}, bf16[32,16,2048]{2,1,0:T(8,128)(2,1)}) custom-call(bf16[512,256]{1,0:T(8,128)(2,1)S(1)} %get-tuple-element.17.h0_ref, bf16[512,256]{1,0:T(8,128)(2,1)S(1)} %get-tuple-element.18.qg0_ref, bf16[512,256]{1,0:T(8,128)(2,1)S(1)} %get-tuple-element.19.qu0_ref, ...), custom_call_target="tpu_custom_call" | custom-call | flops 4831838208 | bytes 18874368 | tf_op jit(solution)/shard_map/back/pallas_call | solution.py:272
  101.5 61.0 %all_to_all.16.y_ref = bf16[32,16,2048]{2,1,0:T(8,128)(2,1)S(1)} all-to-all(bf16[32,16,2048]{2,1,0:T(8,128)(2,1)} %get-tuple-element.22), channel_id=1, replica_groups=mesh['dp'=8,'expert'=32] {'expert'}, dimensions={0} | all-to-all | bytes 4194304 | tf_op jit(solution)/shard_map/all_to_all | solution.py:284
  162.4 0.0 collective-permute-done.1
  162.5 2.3 %add_convert_fusion = bf16[1024,1024]{1,0:T(8,128)(2,1)} fusion(bf16[1024,1024]{1,0:T(8,128)(2,1)S(1)} %collective-permute-done.1, bf16[1024,1024]{1,0:T(8,128)(2,1)S(1)} %copy-done.10), kind=kLoop, calls=%fused_computation | loop fusion | flops 4194304 | bytes 6291456 | tf_op jit(solution)/shard_map/convert_element_type | solution.py:287
  164.8 0.0 reduce-scatter.5.cloned.1.call-update
  164.8 0.0 copy-start.7
  164.8 6.4 %all-to-all-start.2 = ((bf16[32,16,2048]{2,1,0:T(8,128)(2,1)}), bf16[32,16,2048]{2,1,0:T(8,128)(2,1)}, u32[]{:S(2)}, u32[]{:S(2)}) async-start(bf16[32,16,2048]{2,1,0:T(8,128)(2,1)} %get-tuple-element.25), calls=%async_computation.2 | async-start | bytes 4194304 | tf_op jit(solution)/shard_map/all_to_all | solution.py:286
  171.2 0.0 copy-start.9
  171.3 0.0 reduce-scatter.3.cloned.1.call-done.early_ref
  171.3 1.0 constant_dynamic-slice_fusion
  172.3 0.4 collective-permute-start
  172.7 24.5 %all-to-all-done.2.dx_ref = bf16[32,16,2048]{2,1,0:T(8,128)(2,1)} async-done(((bf16[32,16,2048]{2,1,0:T(8,128)(2,1)}), bf16[32,16,2048]{2,1,0:T(8,128)(2,1)}, u32[]{:S(2)}, u32[]{:S(2)}) %all-to-all-start.2) | async-done | bytes 2097184 | tf_op jit(solution)/shard_map/all_to_all | solution.py:286
  197.2 0.0 copy-done.7
  197.2 3.0 %tokens.1 = bf16[128,2048]{1,0:T(8,128)(2,1)} custom-call(s32[2,128]{1,0:T(2,128)S(1)} %bitcast.10, bf16[32,16,2048]{2,1,0:T(8,128)(2,1)} %all-to-all-done.2.dx_ref), custom_call_target="tpu_custom_call" | custom-call | flops 268435456 | bytes 3145728 | tf_op jit(solution)/shard_map/tokens/pallas_call | solution.py:296
  200.2 1.7 layer.1
  201.9 6.8 %reduce-scatter.5.cloned.1.call-done.late_ref = bf16[128,1024]{1,0:T(8,128)(2,1)} async-done(((bf16[1024,1024]{1,0:T(8,128)(2,1)}), bf16[128,1024]{1,0:T(8,128)(2,1)}) %reduce-scatter.5.cloned.1.call-update) | async-done | bytes 262160 | tf_op jit(solution)/shard_map/reduce_scatter | solution.py:288
  208.7 0.0 collective-permute-done.came_ref
  208.7 0.9 copy-done.5
  209.7 0.9 join.1
  (13 shorter events, 0.0 us)
Async XLA Ops:
  7.2 164.1 %reduce-scatter.3.cloned.1.call-start = ((), (), s32[]{:S(2)}) async-start(), calls=%async_computation.5 | async-start | bytes 5898240 | tf_op jit(solution)/shard_map/reduce_scatter | solution.py:253
  7.2 1.0 copy-start.3
  8.3 1.0 copy-start.4
  9.3 0.7 copy-start.6
  10.0 0.7 copy-start.8
  10.7 60.0 %copy-start = (bf16[1,2048,2304]{2,1,0:T(8,128)(2,1)S(1)}, bf16[1,2048,2304]{2,1,0:T(8,128)(2,1)}, u32[]{:S(2)}) copy-start(bf16[1,2048,2304]{2,1,0:T(8,128)(2,1)} %param.9) | copy-start | bytes 28311556
  70.7 9.5 %copy-start.1 = (bf16[32,32,2048]{2,1,0:T(8,128)(2,1)}, bf16[32,32,2048]{2,1,0:T(8,128)(2,1)S(1)}, u32[]{:S(2)}) copy-start(bf16[32,32,2048]{2,1,0:T(8,128)(2,1)S(1)} %all_to_all.15.rows_ref) | copy-start | bytes 12582916
  80.2 128.5 %reduce-scatter.5.cloned.1.call-start = ((), (), s32[]{:S(2)}) async-start(), calls=%async_computation.6 | async-start | bytes 2359296 | tf_op jit(solution)/shard_map/reduce_scatter | solution.py:288
  90.0 72.5 %collective-permute-start.1 = (bf16[1024,1024]{1,0:T(8,128)(2,1)}, bf16[1024,1024]{1,0:T(8,128)(2,1)S(1)}, u32[]{:S(2)}, u32[]{:S(2)}) collective-permute-start(bf16[1024,1024]{1,0:T(8,128)(2,1)} %get-tuple-element.28), channel_id=1, source_target_pairs={{16,0},{17,1},{18,2},{19,3},{20,4},{21,5},{22,6},{23,7},{24,8},{25... | collective-permute-start | bytes 6291464 | tf_op jit(solution)/shard_map/ppermute | solution.py:270
  101.5 61.0 %copy-start.10 = (bf16[1024,1024]{1,0:T(8,128)(2,1)S(1)}, bf16[1024,1024]{1,0:T(8,128)(2,1)}, u32[]{:S(2)}) copy-start(bf16[1024,1024]{1,0:T(8,128)(2,1)} %get-tuple-element.27) | copy-start | bytes 6291460
  164.8 32.3 %copy-start.7 = (s32[128,2]{0,1:T(2,128)S(1)}, s32[128,2]{0,1:T(2,128)}, u32[]{:S(2)}) copy-start(s32[128,2]{0,1:T(2,128)} %param.7) | copy-start | bytes 3076
  164.8 32.3 %all-to-all-start.2 = ((bf16[32,16,2048]{2,1,0:T(8,128)(2,1)}), bf16[32,16,2048]{2,1,0:T(8,128)(2,1)}, u32[]{:S(2)}, u32[]{:S(2)}) async-start(bf16[32,16,2048]{2,1,0:T(8,128)(2,1)} %get-tuple-element.25), calls=%async_computation.2 | async-start | bytes 4194304 | tf_op jit(solution)/shard_map/all_to_all | solution.py:286
  171.2 28.9 %copy-start.9 = (f32[128,2]{0,1:T(2,128)S(1)}, f32[128,2]{0,1:T(2,128)}, u32[]{:S(2)}) copy-start(f32[128,2]{0,1:T(2,128)} %param.8) | copy-start | bytes 3076
  172.3 36.4 %copy-start.2 = (bf16[256,1280]{1,0:T(8,128)(2,1)S(1)}, bf16[256,1280]{1,0:T(8,128)(2,1)}, u32[]{:S(2)}) copy-start(bf16[256,1280]{1,0:T(8,128)(2,1)} %reduce-scatter.3.cloned.1.call-done.early_ref) | copy-start | bytes 1966084
  172.3 36.4 %collective-permute-start = (bf16[128,1280]{1,0:T(8,128)(2,1)S(1)}, bf16[128,1280]{1,0:T(8,128)(2,1)S(1)}, u32[]{:S(2)}, u32[]{:S(2)}) collective-permute-start(bf16[128,1280]{1,0:T(8,128)(2,1)S(1)} %constant_dynamic-slice_fusion), channel_id=1, source_target_pairs={{16,0},{17,1},{18,2},{19,3},{20,4},{21,5},{22,6},{23,7},{24,8},{25... | collective-permute-start | bytes 983048 | tf_op jit(solution)/shard_map/ppermute | solution.py:305
  208.7 1.0 copy-start.5
Sparse Core Ops, SparseCore 0:
  80.3 66.5 reduce-scatter.2
  164.9 43.7 reduce-scatter.4

commit v4 on v3

v4 whole, which is shorter than its diff:
```python
import functools

import jax
import jax.numpy as jnp
from jax import lax
from jax.experimental import pallas as pl
from jax.experimental.pallas import tpu as pltpu
from jax.sharding import PartitionSpec as P

BF16 = jnp.bfloat16
F32 = jnp.float32
ROWS = 16


def dot(a, b, dims):
    return lax.dot_general(a, b, (dims, ((), ())), preferred_element_type=F32)


def dispatch_mask(routes, slots):
    top, tokens = routes.shape
    slot = lax.broadcasted_iota(jnp.int32, (slots, tokens), 0)
    names = [routes[k : k + 1, :] == slot for k in range(top)]
    named = names[0]
    for one in names[1:]:
        named = named | one
    earlier = (
        lax.broadcasted_iota(jnp.int32, (tokens, tokens), 0)
        < lax.broadcasted_iota(jnp.int32, (tokens, tokens), 1)
    )
    place = dot(
        jnp.where(named, 1.0, 0.0).astype(BF16),
        jnp.where(earlier, 1.0, 0.0).astype(BF16),
        ((1,), (0,)),
    ).astype(jnp.int32)
    place = jnp.where(named, place, ROWS)
    at = lax.broadcasted_iota(jnp.int32, (slots, ROWS, tokens), 1)
    return names, place[:, None, :] == at


def slot_gates(names, gates):
    total = jnp.where(names[0], gates[0:1, :], 0.0)
    for k in range(1, len(names)):
        total = total + jnp.where(names[k], gates[k : k + 1, :], 0.0)
    return total


def pack_kernel(
    routes_hbm,
    gates_hbm,
    tokens_hbm,
    out_grad_hbm,
    send_hbm,
    routes_ref,
    gates_ref,
    tokens_ref,
    out_grad_ref,
    send_ref,
    in_sems,
    out_sems,
):
    slots, _, width = send_ref.shape
    pieces = out_sems.shape[0]
    step = width // pieces
    pairs = (
        (routes_hbm, routes_ref),
        (gates_hbm, gates_ref),
        (tokens_hbm, tokens_ref),
        (out_grad_hbm, out_grad_ref),
    )
    loads = [pltpu.make_async_copy(*pair, in_sems.at[i]) for i, pair in enumerate(pairs)]
    for load in loads:
        load.start()
    loads[0].wait()
    names, mask = dispatch_mask(routes_ref[...], slots)
    pick = jnp.where(mask, 1.0, 0.0).reshape(slots * ROWS, -1).astype(BF16)
    loads[1].wait()
    weight = slot_gates(names, gates_ref[...])
    row_gate = jnp.sum(jnp.where(mask, weight[:, None, :], 0.0), axis=2, keepdims=True)
    loads[2].wait()
    loads[3].wait()
    stores = []
    for piece in range(pieces):
        cols = pl.ds(piece * step, step)
        x = dot(pick, tokens_ref[:, cols], ((1,), (0,)))
        send_ref[:, :ROWS, cols] = x.astype(BF16).reshape(slots, ROWS, step)
        g = dot(pick, out_grad_ref[:, cols], ((1,), (0,))).reshape(slots, ROWS, step)
        send_ref[:, ROWS:, cols] = (row_gate * g).astype(BF16)
        stores.append(
            pltpu.make_async_copy(
                send_ref.at[:, :, cols], send_hbm.at[:, :, cols], out_sems.at[piece]
            )
        )
        stores[-1].start()
    for store in stores:
        store.wait()


def expert_rows(rows_ref, g, u, v, qg_ref, qu_ref, h_ref):
    slots, _, width = rows_ref.shape
    rows = slots * ROWS
    x = rows_ref[:, :ROWS, :].reshape(rows, width)
    dy = rows_ref[:, ROWS:, :].reshape(rows, width)
    a = dot(x, g, ((1,), (0,)))
    b = dot(x, u, ((1,), (0,)))
    e = dot(dy, v, ((1,), (0,)))
    s = jax.nn.sigmoid(a)
    active = a * s
    h_ref[...] = (active * b).astype(BF16)
    qg_ref[...] = (e * b * s * (1.0 + a * (1.0 - s))).astype(BF16)
    qu_ref[...] = (e * active).astype(BF16)


def early_kernel(plan, groups, rows_ref, w_ref, partial_ref, qg_ref, qu_ref, h_ref):
    slots, _, width = rows_ref.shape
    rows = slots * ROWS
    block = width // 2 // groups
    refs = (qg_ref, qu_ref, h_ref)
    for step, (j, n) in enumerate(plan):

        @pl.when(pl.program_id(0) == step)
        def _(j=j, n=n):
            if n is None:
                chunk, ff = h_ref.shape[1], w_ref.shape[1] // 3
                begins = [n * ff + j * chunk for n in range(3)]
                expert_rows(rows_ref, *(w_ref[:, at : at + chunk] for at in begins), *refs)
                return
            begin = ROWS if n == 2 else 0
            lhs = rows_ref[:, begin : begin + ROWS, :].reshape(rows, width)
            value = dot(lhs, refs[n][...], ((0,), (0,))).astype(BF16)
            for half in range(2):
                for d in range(groups):
                    old, new = (half * groups + d) * block, (2 * d + half) * block
                    partial_ref[new : new + block] = value[old : old + block]


def late_kernel(
    plan,
    which_ref,
    rows_ref,
    g_ref,
    u_ref,
    v_ref,
    own_ref,
    sent_ref,
    qg_ref,
    qu_ref,
    h_ref,
):
    slots, _, width = rows_ref.shape
    rows, half = slots * ROWS, width // 2
    refs = (qg_ref, qu_ref, h_ref)
    for step, (j, n) in enumerate(plan):

        @pl.when(pl.program_id(0) == step)
        def _(j=j, n=n):
            if n is None:
                expert_rows(rows_ref, g_ref[...], u_ref[...], v_ref[...], *refs)
                return
            rhs = refs[n][...]
            begin = ROWS if n == 2 else 0
            for out_ref, which in ((own_ref, which_ref[0]), (sent_ref, 1 - which_ref[0])):
                cols = pl.ds(pl.multiple_of(which * half, half), half)
                lhs = rows_ref[:, begin : begin + ROWS, cols].reshape(rows, half)
                out_ref[...] = dot(lhs, rhs, ((0,), (0,))).astype(BF16)


def back_kernel(h0_ref, qg0_ref, qu0_ref, h_ref, qg_ref, qu_ref, w_ref, out_ref):
    slots, _, block = out_ref.shape
    chunk = h0_ref.shape[1]
    ff = w_ref.shape[1] // 3

    def product(first_ref, rest_ref, base):
        value = dot(first_ref[...], w_ref[:, base : base + chunk], ((1,), (1,)))
        return value + dot(rest_ref[...], w_ref[:, base + chunk : base + ff], ((1,), (1,)))

    y = product(h0_ref, h_ref, 2 * ff)
    out_ref[:, :ROWS, :] = y.astype(BF16).reshape(slots, ROWS, block)
    dx = product(qg0_ref, qg_ref, 0) + product(qu0_ref, qu_ref, ff)
    out_ref[:, ROWS:, :] = dx.astype(BF16).reshape(slots, ROWS, block)


def combine_kernel(routes_ref, gates_ref, back_ref, layer_ref, grad_ref):
    slots, _, width = back_ref.shape
    names, mask = dispatch_mask(routes_ref[...], slots)
    weight = slot_gates(names, gates_ref[...])
    rows = slots * ROWS
    gate = jnp.where(mask, weight[:, None, :], 0.0).reshape(rows, -1)
    high = gate.astype(BF16)
    low = (gate - high.astype(F32)).astype(BF16)
    pick = jnp.where(mask, 1.0, 0.0).reshape(rows, -1).astype(BF16)
    step = 512
    for c in range(0, width, step):
        cols = slice(c, c + step)
        y = back_ref[:, :ROWS, cols].reshape(rows, step)
        value = dot(high, y, ((0,), (0,))) + dot(low, y, ((0,), (0,)))
        layer_ref[:, cols] = value.astype(BF16)
        dx = back_ref[:, ROWS:, cols].reshape(rows, step)
        grad_ref[:, cols] = dot(pick, dx, ((0,), (0,))).astype(BF16)


def add_kernel(place_ref, own_ref, came_ref, *out_refs):
    groups, block = len(out_refs), out_refs[0].shape[0]
    for ahead, out_ref in enumerate(out_refs):
        at = lax.rem(place_ref[0] + ahead, groups)
        lines = pl.ds(pl.multiple_of(at * block, block), block)
        out_ref[...] = (own_ref[lines].astype(F32) + came_ref[lines].astype(F32)).astype(BF16)


def join_kernel(early_plan, late_plan, which_ref, early_ref, came_ref, *refs):
    late_refs, out_ref = refs[:-1], refs[-1]
    half, columns = came_ref.shape
    chunk = columns // len(early_plan)
    steps = out_ref.shape[2] // 3 // chunk
    own = early_ref[pl.ds(pl.multiple_of(which_ref[0] * half, half), half), :]
    total = (own.astype(F32) + came_ref[...].astype(F32)).astype(BF16)
    late = late_refs[0][...].astype(F32)
    for late_ref in late_refs[1:]:
        late = late + late_ref[...].astype(F32)
    for plan, value in ((early_plan, total), (late_plan, late.astype(BF16))):
        for i, (j, n) in enumerate(plan):
            new = (n * steps + j) * chunk
            out_ref[0, :, new : new + chunk] = value[:, i * chunk : (i + 1) * chunk]


def params(mib):
    return pltpu.CompilerParams(vmem_limit_bytes=int(mib * 1024 * 1024))


def cost(flops, moved):
    return pl.CostEstimate(flops=flops, bytes_accessed=moved, transcendentals=0)


def local(tokens, out_grad, routes, gates, weights):
    slots = lax.axis_size("expert")
    groups = lax.axis_size("dp")
    count, width = tokens.shape
    top = routes.shape[1]
    weight = weights[0]
    ff = weight.shape[1] // 3
    rows = slots * ROWS
    chunk = 256
    steps = ff // chunk
    half = width // 2
    routes_t = routes.T
    gates_t = gates.T
    upper = (lax.axis_index("expert") >= slots // 2).astype(jnp.int32)
    which = upper.reshape(1)
    smem = pl.BlockSpec(memory_space=pltpu.SMEM)
    vmem = pl.BlockSpec(memory_space=pltpu.VMEM)
    pair = pltpu.HBM((slots, 2 * ROWS, width), BF16)
    hbm = pl.BlockSpec(memory_space=pltpu.HBM)
    sent = pl.pallas_call(
        pack_kernel,
        in_specs=[hbm] * 4,
        out_specs=hbm,
        out_shape=pair,
        scratch_shapes=[
            pltpu.VMEM((top, count), jnp.int32),
            pltpu.VMEM((top, count), F32),
            pltpu.VMEM((count, width), BF16),
            pltpu.VMEM((count, width), BF16),
            pltpu.VMEM((slots, 2 * ROWS, width), BF16),
            pltpu.SemaphoreType.DMA((4,)),
            pltpu.SemaphoreType.DMA((4,)),
        ],
        compiler_params=params(54.2),
        cost_estimate=cost(4 * rows * count * width, 6 * rows * width),
        name="pack",
    )(routes_t, gates_t, tokens, out_grad)
    came = lax.all_to_all(sent, "expert", split_axis=0, concat_axis=0, tiled=True)

    early_plan = ((1, None), (1, 0), (1, 1), (1, 2), (2, None), (2, 0), (2, 1), (2, 2))
    late_plan = ((0, None), (0, 0), (0, 1), (0, 2))
    early_cols = tuple(one for one in early_plan if one[1] is not None)
    late_cols = tuple(one for one in late_plan if one[1] is not None)
    state = pltpu.HBM((rows, ff - chunk), BF16)
    state_spec = pl.BlockSpec((rows, chunk), lambda p: (0, jnp.where(p >= 4, 1, 0)))
    early, qg, qu, h = pl.pallas_call(
        functools.partial(early_kernel, early_plan, groups),
        grid=(len(early_plan),),
        in_specs=[vmem, vmem],
        out_specs=[
            pl.BlockSpec(
                (width, chunk), lambda p: (0, p - jnp.where(p > 0, 1, 0) - jnp.where(p > 4, 1, 0))
            )
        ]
        + [state_spec] * 3,
        out_shape=[pltpu.HBM((width, len(early_cols) * chunk), BF16)] + [state] * 3,
        compiler_params=params(16),
        cost_estimate=cost(8 * rows * width * ff, 16 * width * ff),
        name="early_grads",
    )(came, weight)
    early_sum = lax.psum_scatter(early, "dp", scatter_dimension=0, tiled=True)
    state = pltpu.HBM((rows, chunk), BF16)
    state_spec = pl.BlockSpec((rows, chunk), lambda p: (0, 0))
    half_spec = pl.BlockSpec((half, chunk), lambda p: (0, jnp.maximum(p - 1, 0)))
    own, sent_half, qg0, qu0, h0 = pl.pallas_call(
        functools.partial(late_kernel, late_plan),
        grid=(len(late_plan),),
        in_specs=[smem, pl.BlockSpec((slots, 2 * ROWS, width), lambda p: (0, 0, 0))]
        + [pl.BlockSpec((width, chunk), lambda p, n=n: (0, n * steps)) for n in range(3)],
        out_specs=[half_spec] * 2 + [state_spec] * 3,
        out_shape=[pltpu.HBM((half, len(late_cols) * chunk), BF16)] * 2 + [state] * 3,
        compiler_params=params(50),
        cost_estimate=cost(4 * rows * width * ff, 8 * width * ff),
        name="late_grads",
    )(which, came, weight, weight, weight)
    route = [((i + slots // 2) % slots, i) for i in range(slots)]
    came_half = lax.ppermute(sent_half, "expert", route)
    block = 512
    back = pl.pallas_call(
        back_kernel,
        grid=(width // block,),
        in_specs=[pl.BlockSpec((rows, chunk), lambda j: (0, 0))] * 3
        + [pl.BlockSpec((rows, ff - chunk), lambda j: (0, 0))] * 3
        + [pl.BlockSpec((block, 3 * ff), lambda j: (j, 0))],
        out_specs=pl.BlockSpec((slots, 2 * ROWS, block), lambda j: (0, 0, j)),
        out_shape=pair,
        compiler_params=params(50),
        cost_estimate=cost(6 * rows * width * ff, 12 * width * ff),
        name="back",
    )(h0, qg0, qu0, h, qg, qu, weight)
    home = lax.all_to_all(back, "expert", split_axis=0, concat_axis=0, tiled=True)
    kept = half // groups
    term = jax.ShapeDtypeStruct((kept, len(late_cols) * chunk), BF16)
    late_terms = list(pl.pallas_call(
        add_kernel,
        in_specs=[smem, vmem, vmem],
        out_shape=[term] * groups,
        compiler_params=params(16),
        name="late_sum",
    )(lax.axis_index("dp").reshape(1), own, came_half))
    for ahead in range(1, groups):
        hops = [(i, (i + ahead) % groups) for i in range(groups)]
        late_terms[ahead] = lax.ppermute(late_terms[ahead], "dp", hops)
    layer_out, grad_tokens = pl.pallas_call(
        combine_kernel,
        out_shape=[jax.ShapeDtypeStruct((count, width), BF16)] * 2,
        compiler_params=params(24),
        cost_estimate=cost(6 * rows * count * width, 6 * rows * width),
        name="combine",
    )(routes_t, gates_t, home)
    other = lax.dynamic_slice_in_dim(early_sum, (1 - upper) * kept, kept, 0)
    came_early = lax.ppermute(other, "expert", route)
    grad_weights = pl.pallas_call(
        functools.partial(join_kernel, early_cols, late_cols),
        in_specs=[smem] + [vmem] * (2 + groups),
        out_shape=jax.ShapeDtypeStruct((1, kept, 3 * ff), BF16),
        compiler_params=params(8),
        name="join",
    )(which, early_sum, came_early, *late_terms)
    return (layer_out, grad_tokens, grad_weights)


def solution(mesh):
    placed = (
        P(("dp", "expert"), None),
        P(("dp", "expert"), None),
        P(("dp", "expert"), None),
        P(("dp", "expert"), None),
        P("expert", None, None),
    )
    return jax.shard_map(
        local,
        mesh=mesh,
        in_specs=placed,
        out_specs=(P(("dp", "expert"), None), P(("dp", "expert"), None), P("expert", "dp", None)),
        check_vma=False,
    )
```

time: 218 us -> 254 us (1.17); the launches traced: 217 us -> 250 us
  waiting for transfers between devices: 31.3 us -> 109 us
  blocking collectives: 117 us -> 56.3 us
  starting transfers between devices: 9.28 us -> 25.1 us
    ppermute x1, waiting for transfers between devices: 0.01 us -> 83.7 us  [local(): came_half = lax.ppermute(sent_half, 'expert', route)]
    all_to_all x1 -> x0, blocking collectives: 61 us -> none  [local(): y = lax.all_to_all(y, 'expert', split_axis=0, concat_axis=0, tiled=True)]
    ppermute x0 -> x7, waiting for transfers between devices: none -> 25.1 us  [local(): late_terms[ahead] = lax.ppermute(late_terms[ahead], 'dp', hops)]
    all_to_all x1, waiting for transfers between devices: 24.5 us -> 0.01 us  [local(): lax.all_to_all(back, 'expert', split_axis=0, concat_axis=0, tiled=True)]
    ppermute x0 -> x7, starting transfers between devices: none -> 15.7 us  [local(): late_terms[ahead] = lax.ppermute(late_terms[ahead], 'dp', hops)]
    reduce_scatter x1 -> x0, waiting for transfers between devices: 6.8 us -> none  [local(): late_sum = lax.psum_scatter(late, 'dp', scatter_dimension=0, tiled=True)]
  transfers between devices with their start and end apart: 5 -> 11, of which waited for: 2 -> 6; matrix products, arithmetic and copies ran while one was open for 2% -> 0% of each run, Pallas kernels for 11% -> 10%
where the time goes in v4:
time: 254 us; the launch traced here: 250 us
  waiting for transfers between devices  109 us (43%)
  blocking collectives  56.3 us (22%)
  Pallas kernels  39.7 us (16%)
  starting transfers between devices  25.1 us (10%)
  between operations  14.2 us (6%)
  local copies, waits for them, and re-layouts  6.04 us (2%)
    ppermute x1, waiting for transfers between devices, local(): came_half = lax.ppermute(sent_half, 'expert', route)  83.7 us
    all_to_all x1, blocking collectives, local(): lax.all_to_all(sent, 'expert', split_axis=0, concat_axis=0, tiled=True)  56.3 us
    ppermute x7, waiting for transfers between devices, local(): late_terms[ahead] = lax.ppermute(late_terms[ahead], 'dp', hops)  25.1 us
    ppermute x7, starting transfers between devices, local(): late_terms[ahead] = lax.ppermute(late_terms[ahead], 'dp', hops)  15.7 us
    pallas_call x1, Pallas kernels, local(): pl.pallas_call(functools.partial(early_kernel, early_plan, groups), grid=...  10.6 us
    pallas_call x1, Pallas kernels, local(): pl.pallas_call(back_kernel, grid=(width // block,), in_specs=[pl.BlockSpe...  9.65 us
    pallas_call x1, Pallas kernels, local(): pl.pallas_call(functools.partial(late_kernel, late_plan), grid=(len(late_...  9.12 us
    all_to_all x1, starting transfers between devices, local(): lax.all_to_all(back, 'expert', split_axis=0, concat_axis=0, tiled=True)  6.46 us
  transfers between devices with their start and end apart: 11, of which 6 were waited for; matrix products, arithmetic and copies ran while one was open for 0% of the time, Pallas kernels for 10%

profile of v4, /device:TPU:4, one launch (start us, length us, event | category | flops | bytes accessed | tf_op | source)
XLA Modules:
  0.0 250.2 jit_solution(7331506887882080581)
XLA Ops:
  7.2 0.0 reduce-scatter.2.cloned.1.call-start
  7.2 4.0 %pack.1 = bf16[32,32,2048]{2,1,0:T(8,128)(2,1)} custom-call(s32[2,128]{1,0:T(2,128)} %bitcast.10, f32[2,128]{1,0:T(2,128)} %bitcast.12, bf16[128,2048]{1,0:T(8,128)(2,1)} %tokens_hbm.1, bf16[128,2048]{1,0:T(8,128)(2,1)} %out_grad_hbm.1), custom_call_target="tpu_custom_call" | custom-call | flops 536870912 | bytes 6291456 | tf_op jit(solution)/shard_map/pack/pallas_call | solution.py:252
  11.2 56.3 %all_to_all.10.rows_ref = bf16[32,32,2048]{2,1,0:T(8,128)(2,1)S(1)} all-to-all(bf16[32,32,2048]{2,1,0:T(8,128)(2,1)} %pack.1), channel_id=1, replica_groups=mesh['dp'=8,'expert'=32] {'expert'}, dimensions={0} | all-to-all | bytes 8388608 | tf_op jit(solution)/shard_map/all_to_all | solution.py:270
  67.5 10.6 %early_grads.1 = (bf16[2048,1536]{1,0:T(8,128)(2,1)}, bf16[512,512]{1,0:T(8,128)(2,1)}, bf16[512,512]{1,0:T(8,128)(2,1)}, bf16[512,512]{1,0:T(8,128)(2,1)}) custom-call(bf16[32,32,2048]{2,1,0:T(8,128)(2,1)S(1)} %all_to_all.10.rows_ref, bf16[2048,2304]{1,0:T(8,128)(2,1)S(1)} %bitcast.9), custom_call_target="tpu_custom_call" | custom-call | flops 6442450944 | bytes 25165824 | tf_op jit(solution)/shard_map/early_grads/pallas_call | solution.py:278
  78.1 0.0 reduce-scatter.2.cloned.1.call-update
  78.2 9.1 %late_grads.1 = (bf16[1024,768]{1,0:T(8,128)(2,1)}, bf16[1024,768]{1,0:T(8,128)(2,1)}, bf16[512,256]{1,0:T(8,128)(2,1)}, bf16[512,256]{1,0:T(8,128)(2,1)}, bf16[512,256]{1,0:T(8,128)(2,1)}) custom-call(s32[1]{0:T(128)} %bitcast.2.which_ref, bf16[32,32,2048]{2,1,0:T(8,128)(2,1)} %copy-done.1, bf16[2048,2304]{1,0:T(8,128)(2,1)} %bitcast.5, ...), custom_call_target="tpu_custom_call" | custom-call | flops 3221225472 | bytes 12582912 | tf_op jit(solution)/shard_map/late_grads/pallas_call | solution.py:297
  87.3 0.9 copy-done.6
  88.3 0.9 copy-done.7
  89.2 0.9 copy-done.8
  90.2 9.7 %back.1 = bf16[32,32,2048]{2,1,0:T(8,128)(2,1)} custom-call(bf16[512,256]{1,0:T(8,128)(2,1)S(1)} %copy-done.8, bf16[512,256]{1,0:T(8,128)(2,1)S(1)} %copy-done.6, bf16[512,256]{1,0:T(8,128)(2,1)S(1)} %copy-done.7, bf16[512,512]{1,0:T(8,128)(2,1)S(1)} %copy-done.14, bf16[512,512]{1,0:T(8,128)(2,1)S(1)} %copy-done.12, bf16[512,512]{1,0:T(8,128)(2,1)S(1)} %copy-done.13, ...), custom_call_target="tpu_custom_call" | custom-call | flops 4831838208 | bytes 18874368 | tf_op jit(solution)/shard_map/back/pallas_call | solution.py:311
  99.8 6.5 %all-to-all-start.1 = ((bf16[32,32,2048]{2,1,0:T(8,128)(2,1)}), bf16[32,32,2048]{2,1,0:T(8,128)(2,1)}, u32[]{:S(2)}, u32[]{:S(2)}) async-start(bf16[32,32,2048]{2,1,0:T(8,128)(2,1)} %back.1), calls=%async_computation.1 | async-start | bytes 8388608 | tf_op jit(solution)/shard_map/all_to_all | solution.py:323
  106.3 0.4 collective-permute-start.1
  106.7 83.7 %collective-permute-done.1.came_ref = bf16[1024,768]{1,0:T(8,128)(2,1)S(1)} collective-permute-done((bf16[1024,768]{1,0:T(8,128)(2,1)}, bf16[1024,768]{1,0:T(8,128)(2,1)S(1)}, u32[]{:S(2)}, u32[]{:S(2)}) %collective-permute-start.1) | collective-permute-done | bytes 1572896 | tf_op jit(solution)/shard_map/ppermute | solution.py:309
  190.4 1.0 late_sum.1
  191.5 0.7 copy-done.9
  192.1 0.7 copy-done.10
  192.8 0.7 copy-done.11
  193.5 1.9 collective-permute-start.2
  195.4 3.2 %collective-permute-start.3 = (bf16[128,768]{1,0:T(8,128)(2,1)}, bf16[128,768]{1,0:T(8,128)(2,1)S(1)}, u32[]{:S(2)}, u32[]{:S(2)}) collective-permute-start(bf16[128,768]{1,0:T(8,128)(2,1)} %get-tuple-element.35), channel_id=1, source_target_pairs={{0,64},{32,96},{64,128},{96,160},{128,192},{160,224},{192,0},{224,... | collective-permute-start | bytes 589832 | tf_op jit(solution)/shard_map/ppermute | solution.py:335
  198.7 4.0 %collective-permute-start.4 = (bf16[128,768]{1,0:T(8,128)(2,1)}, bf16[128,768]{1,0:T(8,128)(2,1)S(1)}, u32[]{:S(2)}, u32[]{:S(2)}) collective-permute-start(bf16[128,768]{1,0:T(8,128)(2,1)} %get-tuple-element.36), channel_id=1, source_target_pairs={{0,96},{32,128},{64,160},{96,192},{128,224},{160,0},{192,32},{224,... | collective-permute-start | bytes 589832 | tf_op jit(solution)/shard_map/ppermute | solution.py:335
  202.7 1.1 constant_dynamic-slice_fusion
  203.8 2.5 %collective-permute-start = (bf16[128,1536]{1,0:T(8,128)(2,1)S(1)}, bf16[128,1536]{1,0:T(8,128)(2,1)S(1)}, u32[]{:S(2)}, u32[]{:S(2)}) collective-permute-start(bf16[128,1536]{1,0:T(8,128)(2,1)S(1)} %constant_dynamic-slice_fusion), channel_id=1, source_target_pairs={{16,0},{17,1},{18,2},{19,3},{20,4},{21,5},{22,6},{23,7},{24,8},{25... | collective-permute-start | bytes 1179656 | tf_op jit(solution)/shard_map/ppermute | solution.py:344
  206.3 0.6 collective-permute-start.5
  207.0 4.9 %collective-permute-start.6 = (bf16[128,768]{1,0:T(8,128)(2,1)}, bf16[128,768]{1,0:T(8,128)(2,1)S(1)}, u32[]{:S(2)}, u32[]{:S(2)}) collective-permute-start(bf16[128,768]{1,0:T(8,128)(2,1)} %copy-done.10), channel_id=1, source_target_pairs={{0,160},{32,192},{64,224},{96,0},{128,32},{160,64},{192,96},{224,1... | collective-permute-start | bytes 589832 | tf_op jit(solution)/shard_map/ppermute | solution.py:335
  211.8 4.8 %collective-permute-done.3.refs_2_ = bf16[128,768]{1,0:T(8,128)(2,1)S(1)} collective-permute-done((bf16[128,768]{1,0:T(8,128)(2,1)}, bf16[128,768]{1,0:T(8,128)(2,1)S(1)}, u32[]{:S(2)}, u32[]{:S(2)}) %collective-permute-start.3) | collective-permute-done | bytes 196640 | tf_op jit(solution)/shard_map/ppermute | solution.py:335
  216.7 1.0 collective-permute-start.7
  217.7 12.2 %collective-permute-done.4.refs_3_ = bf16[128,768]{1,0:T(8,128)(2,1)S(1)} collective-permute-done((bf16[128,768]{1,0:T(8,128)(2,1)}, bf16[128,768]{1,0:T(8,128)(2,1)S(1)}, u32[]{:S(2)}, u32[]{:S(2)}) %collective-permute-start.4) | collective-permute-done | bytes 196640 | tf_op jit(solution)/shard_map/ppermute | solution.py:335
  229.9 4.3 %combine.1 = (bf16[128,2048]{1,0:T(8,128)(2,1)}, bf16[128,2048]{1,0:T(8,128)(2,1)}) custom-call(s32[2,128]{1,0:T(2,128)S(1)} %bitcast.11, f32[2,128]{1,0:T(2,128)S(1)} %bitcast.13, bf16[32,32,2048]{2,1,0:T(8,128)(2,1)} %all-to-all-done.1.back_ref), custom_call_target="tpu_custom_call" | custom-call | flops 805306368 | bytes 6291456 | tf_op jit(solution)/shard_map/combine/pallas_call | solution.py:336
  234.1 0.1 collective-permute-done.6.refs_5_
  234.2 5.6 %collective-permute-done.7.refs_6_ = bf16[128,768]{1,0:T(8,128)(2,1)S(1)} collective-permute-done((bf16[128,768]{1,0:T(8,128)(2,1)}, bf16[128,768]{1,0:T(8,128)(2,1)S(1)}, u32[]{:S(2)}, u32[]{:S(2)}) %collective-permute-start.7) | collective-permute-done | bytes 196640 | tf_op jit(solution)/shard_map/ppermute | solution.py:335
  239.8 2.4 collective-permute-done.8.refs_7_
  242.2 1.1 join.1
  (30 shorter events, 0.1 us)
Async XLA Ops:
  7.2 195.5 %reduce-scatter.2.cloned.1.call-start = ((), (), s32[]{:S(2)}) async-start(), calls=%async_computation.3 | async-start | bytes 7077888 | tf_op jit(solution)/shard_map/reduce_scatter | solution.py:293
  7.2 60.3 %copy-start = (bf16[1,2048,2304]{2,1,0:T(8,128)(2,1)S(1)}, bf16[1,2048,2304]{2,1,0:T(8,128)(2,1)}, u32[]{:S(2)}) copy-start(bf16[1,2048,2304]{2,1,0:T(8,128)(2,1)} %param.9) | copy-start | bytes 28311556
  67.5 10.6 %copy-start.1 = (bf16[32,32,2048]{2,1,0:T(8,128)(2,1)}, bf16[32,32,2048]{2,1,0:T(8,128)(2,1)S(1)}, u32[]{:S(2)}) copy-start(bf16[32,32,2048]{2,1,0:T(8,128)(2,1)S(1)} %all_to_all.10.rows_ref) | copy-start | bytes 12582916
  78.1 9.2 %copy-start.12 = (bf16[512,512]{1,0:T(8,128)(2,1)S(1)}, bf16[512,512]{1,0:T(8,128)(2,1)}, u32[]{:S(2)}) copy-start(bf16[512,512]{1,0:T(8,128)(2,1)} %get-tuple-element.26.qg_ref) | copy-start | bytes 1572868
  78.1 9.2 %copy-start.13 = (bf16[512,512]{1,0:T(8,128)(2,1)S(1)}, bf16[512,512]{1,0:T(8,128)(2,1)}, u32[]{:S(2)}) copy-start(bf16[512,512]{1,0:T(8,128)(2,1)} %get-tuple-element.27.qu_ref) | copy-start | bytes 1572868
  78.2 9.2 %copy-start.14 = (bf16[512,512]{1,0:T(8,128)(2,1)S(1)}, bf16[512,512]{1,0:T(8,128)(2,1)}, u32[]{:S(2)}) copy-start(bf16[512,512]{1,0:T(8,128)(2,1)} %get-tuple-element.25.h_ref) | copy-start | bytes 1572868
  87.3 1.0 copy-start.6
  88.3 0.9 copy-start.7
  89.2 0.9 copy-start.8
  99.8 90.6 %copy-start.3 = (bf16[1024,768]{1,0:T(8,128)(2,1)S(1)}, bf16[1024,768]{1,0:T(8,128)(2,1)}, u32[]{:S(2)}) copy-start(bf16[1024,768]{1,0:T(8,128)(2,1)} %get-tuple-element.31.own_ref) | copy-start | bytes 4718596
  99.8 130.0 %copy-start.4 = (s32[128,2]{0,1:T(2,128)S(1)}, s32[128,2]{0,1:T(2,128)}, u32[]{:S(2)}) copy-start(s32[128,2]{0,1:T(2,128)} %param.7) | copy-start | bytes 3076
  99.8 130.0 %copy-start.5 = (f32[128,2]{0,1:T(2,128)S(1)}, f32[128,2]{0,1:T(2,128)}, u32[]{:S(2)}) copy-start(f32[128,2]{0,1:T(2,128)} %param.8) | copy-start | bytes 3076
  99.8 130.0 %all-to-all-start.1 = ((bf16[32,32,2048]{2,1,0:T(8,128)(2,1)}), bf16[32,32,2048]{2,1,0:T(8,128)(2,1)}, u32[]{:S(2)}, u32[]{:S(2)}) async-start(bf16[32,32,2048]{2,1,0:T(8,128)(2,1)} %back.1), calls=%async_computation.1 | async-start | bytes 8388608 | tf_op jit(solution)/shard_map/all_to_all | solution.py:323
  106.3 84.1 %collective-permute-start.1 = (bf16[1024,768]{1,0:T(8,128)(2,1)}, bf16[1024,768]{1,0:T(8,128)(2,1)S(1)}, u32[]{:S(2)}, u32[]{:S(2)}) collective-permute-start(bf16[1024,768]{1,0:T(8,128)(2,1)} %get-tuple-element.32), channel_id=1, source_target_pairs={{16,0},{17,1},{18,2},{19,3},{20,4},{21,5},{22,6},{23,7},{24,8},{25... | collective-permute-start | bytes 4718600 | tf_op jit(solution)/shard_map/ppermute | solution.py:309
  191.4 0.7 copy-start.9
  192.1 0.7 copy-start.10
  192.8 0.7 copy-start.11
  193.5 13.4 %collective-permute-start.2 = (bf16[128,768]{1,0:T(8,128)(2,1)}, bf16[128,768]{1,0:T(8,128)(2,1)S(1)}, u32[]{:S(2)}, u32[]{:S(2)}) collective-permute-start(bf16[128,768]{1,0:T(8,128)(2,1)} %get-tuple-element.34), channel_id=1, source_target_pairs={{0,32},{32,64},{64,96},{96,128},{128,160},{160,192},{192,224},{224... | collective-permute-start | bytes 589832 | tf_op jit(solution)/shard_map/ppermute | solution.py:335
  195.4 21.2 %collective-permute-start.3 = (bf16[128,768]{1,0:T(8,128)(2,1)}, bf16[128,768]{1,0:T(8,128)(2,1)S(1)}, u32[]{:S(2)}, u32[]{:S(2)}) collective-permute-start(bf16[128,768]{1,0:T(8,128)(2,1)} %get-tuple-element.35), channel_id=1, source_target_pairs={{0,64},{32,96},{64,128},{96,160},{128,192},{160,224},{192,0},{224,... | collective-permute-start | bytes 589832 | tf_op jit(solution)/shard_map/ppermute | solution.py:335
  198.7 31.2 %collective-permute-start.4 = (bf16[128,768]{1,0:T(8,128)(2,1)}, bf16[128,768]{1,0:T(8,128)(2,1)S(1)}, u32[]{:S(2)}, u32[]{:S(2)}) collective-permute-start(bf16[128,768]{1,0:T(8,128)(2,1)} %get-tuple-element.36), channel_id=1, source_target_pairs={{0,96},{32,128},{64,160},{96,192},{128,224},{160,0},{192,32},{224,... | collective-permute-start | bytes 589832 | tf_op jit(solution)/shard_map/ppermute | solution.py:335
  202.7 39.5 %copy-start.2 = (bf16[256,1536]{1,0:T(8,128)(2,1)S(1)}, bf16[256,1536]{1,0:T(8,128)(2,1)}, u32[]{:S(2)}) copy-start(bf16[256,1536]{1,0:T(8,128)(2,1)} %reduce-scatter.2.cloned.1.call-done.early_ref) | copy-start | bytes 2359300
  203.8 38.4 %collective-permute-start = (bf16[128,1536]{1,0:T(8,128)(2,1)S(1)}, bf16[128,1536]{1,0:T(8,128)(2,1)S(1)}, u32[]{:S(2)}, u32[]{:S(2)}) collective-permute-start(bf16[128,1536]{1,0:T(8,128)(2,1)S(1)} %constant_dynamic-slice_fusion), channel_id=1, source_target_pairs={{16,0},{17,1},{18,2},{19,3},{20,4},{21,5},{22,6},{23,7},{24,8},{25... | collective-permute-start | bytes 1179656 | tf_op jit(solution)/shard_map/ppermute | solution.py:344
  206.3 27.8 %collective-permute-start.5 = (bf16[128,768]{1,0:T(8,128)(2,1)}, bf16[128,768]{1,0:T(8,128)(2,1)S(1)}, u32[]{:S(2)}, u32[]{:S(2)}) collective-permute-start(bf16[128,768]{1,0:T(8,128)(2,1)} %copy-done.11), channel_id=1, source_target_pairs={{0,128},{32,160},{64,192},{96,224},{128,0},{160,32},{192,64},{224,... | collective-permute-start | bytes 589832 | tf_op jit(solution)/shard_map/ppermute | solution.py:335
  207.0 27.3 %collective-permute-start.6 = (bf16[128,768]{1,0:T(8,128)(2,1)}, bf16[128,768]{1,0:T(8,128)(2,1)S(1)}, u32[]{:S(2)}, u32[]{:S(2)}) collective-permute-start(bf16[128,768]{1,0:T(8,128)(2,1)} %copy-done.10), channel_id=1, source_target_pairs={{0,160},{32,192},{64,224},{96,0},{128,32},{160,64},{192,96},{224,1... | collective-permute-start | bytes 589832 | tf_op jit(solution)/shard_map/ppermute | solution.py:335
  216.7 23.2 %collective-permute-start.7 = (bf16[128,768]{1,0:T(8,128)(2,1)}, bf16[128,768]{1,0:T(8,128)(2,1)S(1)}, u32[]{:S(2)}, u32[]{:S(2)}) collective-permute-start(bf16[128,768]{1,0:T(8,128)(2,1)} %copy-done.9), channel_id=1, source_target_pairs={{0,192},{32,224},{64,0},{96,32},{128,64},{160,96},{192,128},{224,1... | collective-permute-start | bytes 589832 | tf_op jit(solution)/shard_map/ppermute | solution.py:335
  229.9 12.4 %collective-permute-start.8 = (bf16[128,768]{1,0:T(8,128)(2,1)S(1)}, bf16[128,768]{1,0:T(8,128)(2,1)S(1)}, u32[]{:S(2)}, u32[]{:S(2)}) collective-permute-start(bf16[128,768]{1,0:T(8,128)(2,1)S(1)} %get-tuple-element.40), channel_id=1, source_target_pairs={{0,224},{32,0},{64,32},{96,64},{128,96},{160,128},{192,160},{224,1... | collective-permute-start | bytes 589832 | tf_op jit(solution)/shard_map/ppermute | solution.py:335
Sparse Core Ops, SparseCore 0:
  78.2 76.4 reduce-scatter.1

commit v5 on v4

--- a/solution.py
+++ b/solution.py
@@ -198,25 +198,13 @@
         grad_ref[:, cols] = dot(pick, dx, ((0,), (0,))).astype(BF16)
 
 
-def add_kernel(place_ref, own_ref, came_ref, *out_refs):
-    groups, block = len(out_refs), out_refs[0].shape[0]
-    for ahead, out_ref in enumerate(out_refs):
-        at = lax.rem(place_ref[0] + ahead, groups)
-        lines = pl.ds(pl.multiple_of(at * block, block), block)
-        out_ref[...] = (own_ref[lines].astype(F32) + came_ref[lines].astype(F32)).astype(BF16)
-
-
-def join_kernel(early_plan, late_plan, which_ref, early_ref, came_ref, *refs):
-    late_refs, out_ref = refs[:-1], refs[-1]
+def join_kernel(early_plan, late_plan, which_ref, early_ref, came_ref, late_ref, out_ref):
     half, columns = came_ref.shape
     chunk = columns // len(early_plan)
     steps = out_ref.shape[2] // 3 // chunk
     own = early_ref[pl.ds(pl.multiple_of(which_ref[0] * half, half), half), :]
     total = (own.astype(F32) + came_ref[...].astype(F32)).astype(BF16)
-    late = late_refs[0][...].astype(F32)
-    for late_ref in late_refs[1:]:
-        late = late + late_ref[...].astype(F32)
-    for plan, value in ((early_plan, total), (late_plan, late.astype(BF16))):
+    for plan, value in ((early_plan, total), (late_plan, late_ref[...])):
         for i, (j, n) in enumerate(plan):
             new = (n * steps + j) * chunk
             out_ref[0, :, new : new + chunk] = value[:, i * chunk : (i + 1) * chunk]
@@ -321,18 +309,8 @@
         name="back",
     )(h0, qg0, qu0, h, qg, qu, weight)
     home = lax.all_to_all(back, "expert", split_axis=0, concat_axis=0, tiled=True)
-    kept = half // groups
-    term = jax.ShapeDtypeStruct((kept, len(late_cols) * chunk), BF16)
-    late_terms = list(pl.pallas_call(
-        add_kernel,
-        in_specs=[smem, vmem, vmem],
-        out_shape=[term] * groups,
-        compiler_params=params(16),
-        name="late_sum",
-    )(lax.axis_index("dp").reshape(1), own, came_half))
-    for ahead in range(1, groups):
-        hops = [(i, (i + ahead) % groups) for i in range(groups)]
-        late_terms[ahead] = lax.ppermute(late_terms[ahead], "dp", hops)
+    late = (own.astype(F32) + came_half.astype(F32)).astype(BF16)
+    late_sum = lax.psum_scatter(late, "dp", scatter_dimension=0, tiled=True)
     layer_out, grad_tokens = pl.pallas_call(
         combine_kernel,
         out_shape=[jax.ShapeDtypeStruct((count, width), BF16)] * 2,
@@ -340,15 +318,16 @@
         cost_estimate=cost(6 * rows * count * width, 6 * rows * width),
         name="combine",
     )(routes_t, gates_t, home)
+    kept = half // groups
     other = lax.dynamic_slice_in_dim(early_sum, (1 - upper) * kept, kept, 0)
     came_early = lax.ppermute(other, "expert", route)
     grad_weights = pl.pallas_call(
         functools.partial(join_kernel, early_cols, late_cols),
-        in_specs=[smem] + [vmem] * (2 + groups),
+        in_specs=[smem, vmem, vmem, vmem],
         out_shape=jax.ShapeDtypeStruct((1, kept, 3 * ff), BF16),
         compiler_params=params(8),
         name="join",
-    )(which, early_sum, came_early, *late_terms)
+    )(which, early_sum, came_early, late_sum)
     return (layer_out, grad_tokens, grad_weights)
 
 

time: 254 us -> 206 us (0.81); the launches traced: 250 us -> 205 us
  waiting for transfers between devices: 109 us -> 80.3 us
  starting transfers between devices: 25.1 us -> 9.56 us
    ppermute x1, waiting for transfers between devices: 83.7 us -> 18.2 us  [local(): came_half = lax.ppermute(sent_half, 'expert', route)]
    reduce_scatter x1, waiting for transfers between devices: 0.01 us -> 26.5 us  [local(): early_sum = lax.psum_scatter(early, 'dp', scatter_dimension=0, tiled=True)]
    ppermute x7 -> x0, waiting for transfers between devices: 25.1 us -> none  [local(): late_terms[ahead] = lax.ppermute(late_terms[ahead], 'dp', hops)]
    reduce_scatter x0 -> x1, waiting for transfers between devices: none -> 19 us  [local(): late_sum = lax.psum_scatter(late, 'dp', scatter_dimension=0, tiled=True)]
    all_to_all x1, waiting for transfers between devices: 0.01 us -> 16.6 us  [local(): lax.all_to_all(back, 'expert', split_axis=0, concat_axis=0, tiled=True)]
    ppermute x7 -> x0, starting transfers between devices: 15.7 us -> none  [local(): late_terms[ahead] = lax.ppermute(late_terms[ahead], 'dp', hops)]
  transfers between devices with their start and end apart: 11 -> 5, of which waited for: 6 -> 4; matrix products, arithmetic and copies ran while one was open for 0% -> 1% of each run, Pallas kernels for 10% -> 11%
where the time goes in v5:
time: 206 us; the launch traced here: 205 us
  waiting for transfers between devices  80.3 us (39%)
  blocking collectives  56.3 us (27%)
  Pallas kernels  38.2 us (19%)
  between operations  14.1 us (7%)
  starting transfers between devices  9.56 us (5%)
  local copies, waits for them, and re-layouts  4.98 us (2%)
    all_to_all x1, blocking collectives, local(): lax.all_to_all(sent, 'expert', split_axis=0, concat_axis=0, tiled=True)  56.3 us
    reduce_scatter x1, waiting for transfers between devices, local(): early_sum = lax.psum_scatter(early, 'dp', scatter_dimension=0, tiled=True)  26.5 us
    reduce_scatter x1, waiting for transfers between devices, local(): late_sum = lax.psum_scatter(late, 'dp', scatter_dimension=0, tiled=True)  19 us
    ppermute x1, waiting for transfers between devices, local(): came_half = lax.ppermute(sent_half, 'expert', route)  18.2 us
    all_to_all x1, waiting for transfers between devices, local(): lax.all_to_all(back, 'expert', split_axis=0, concat_axis=0, tiled=True)  16.6 us
    pallas_call x1, Pallas kernels, local(): pl.pallas_call(functools.partial(early_kernel, early_plan, groups), grid=...  10.6 us
    pallas_call x1, Pallas kernels, local(): pl.pallas_call(back_kernel, grid=(width // block,), in_specs=[pl.BlockSpe...  9.18 us
    pallas_call x1, Pallas kernels, local(): pl.pallas_call(functools.partial(late_kernel, late_plan), grid=(len(late_...  9.17 us
  transfers between devices with their start and end apart: 5, of which 4 were waited for; matrix products, arithmetic and copies ran while one was open for 1% of the time, Pallas kernels for 11%

profile of v5, /device:TPU:4, one launch (start us, length us, event | category | flops | bytes accessed | tf_op | source)
XLA Modules:
  0.0 205.1 jit_solution(7570157416810802258)
XLA Ops:
  7.2 0.0 reduce-scatter.3.cloned.1.call-start
  7.2 0.0 copy-start
  7.2 4.0 %pack.1 = bf16[32,32,2048]{2,1,0:T(8,128)(2,1)} custom-call(s32[2,128]{1,0:T(2,128)} %bitcast.9, f32[2,128]{1,0:T(2,128)} %bitcast.11, bf16[128,2048]{1,0:T(8,128)(2,1)} %tokens_hbm.1, bf16[128,2048]{1,0:T(8,128)(2,1)} %out_grad_hbm.1), custom_call_target="tpu_custom_call" | custom-call | flops 536870912 | bytes 6291456 | tf_op jit(solution)/shard_map/pack/pallas_call | solution.py:240
  11.2 56.3 %all_to_all.10.rows_ref = bf16[32,32,2048]{2,1,0:T(8,128)(2,1)S(1)} all-to-all(bf16[32,32,2048]{2,1,0:T(8,128)(2,1)} %pack.1), channel_id=1, replica_groups=mesh['dp'=8,'expert'=32] {'expert'}, dimensions={0} | all-to-all | bytes 8388608 | tf_op jit(solution)/shard_map/all_to_all | solution.py:258
  67.5 0.0 copy-done
  67.5 10.6 %early_grads.1 = (bf16[2048,1536]{1,0:T(8,128)(2,1)}, bf16[512,512]{1,0:T(8,128)(2,1)}, bf16[512,512]{1,0:T(8,128)(2,1)}, bf16[512,512]{1,0:T(8,128)(2,1)}) custom-call(bf16[32,32,2048]{2,1,0:T(8,128)(2,1)S(1)} %all_to_all.10.rows_ref, bf16[2048,2304]{1,0:T(8,128)(2,1)S(1)} %bitcast.8), custom_call_target="tpu_custom_call" | custom-call | flops 6442450944 | bytes 25165824 | tf_op jit(solution)/shard_map/early_grads/pallas_call | solution.py:266
  78.1 0.0 copy-done.1
  78.1 0.0 reduce-scatter.3.cloned.1.call-update
  78.2 0.0 copy-start.9
  78.2 0.0 copy-start.10
  78.2 0.0 copy-start.11
  78.2 9.2 %late_grads.1 = (bf16[1024,768]{1,0:T(8,128)(2,1)}, bf16[1024,768]{1,0:T(8,128)(2,1)}, bf16[512,256]{1,0:T(8,128)(2,1)}, bf16[512,256]{1,0:T(8,128)(2,1)}, bf16[512,256]{1,0:T(8,128)(2,1)}) custom-call(s32[1]{0:T(128)} %bitcast.2.which_ref, bf16[32,32,2048]{2,1,0:T(8,128)(2,1)} %copy-done.1, bf16[2048,2304]{1,0:T(8,128)(2,1)} %bitcast.4, ...), custom_call_target="tpu_custom_call" | custom-call | flops 3221225472 | bytes 12582912 | tf_op jit(solution)/shard_map/late_grads/pallas_call | solution.py:285
  87.4 2.5 %collective-permute-start.1 = (bf16[1024,768]{1,0:T(8,128)(2,1)}, bf16[1024,768]{1,0:T(8,128)(2,1)S(1)}, u32[]{:S(2)}, u32[]{:S(2)}) collective-permute-start(bf16[1024,768]{1,0:T(8,128)(2,1)} %get-tuple-element.24), channel_id=1, source_target_pairs={{16,0},{17,1},{18,2},{19,3},{20,4},{21,5},{22,6},{23,7},{24,8},{25... | collective-permute-start | bytes 4718600 | tf_op jit(solution)/shard_map/ppermute | solution.py:297
  89.9 0.0 copy-done.9
  89.9 0.9 copy-done.6
  90.8 1.0 copy-done.7
  91.8 0.9 copy-done.8
  92.8 9.2 %back.1 = bf16[32,32,2048]{2,1,0:T(8,128)(2,1)} custom-call(bf16[512,256]{1,0:T(8,128)(2,1)S(1)} %copy-done.8, bf16[512,256]{1,0:T(8,128)(2,1)S(1)} %copy-done.6, bf16[512,256]{1,0:T(8,128)(2,1)S(1)} %copy-done.7, bf16[512,512]{1,0:T(8,128)(2,1)S(1)} %copy-done.11, bf16[512,512]{1,0:T(8,128)(2,1)S(1)} %copy-done.9, bf16[512,512]{1,0:T(8,128)(2,1)S(1)} %copy-done.10, ...), custom_call_target="tpu_custom_call" | custom-call | flops 4831838208 | bytes 18874368 | tf_op jit(solution)/shard_map/back/pallas_call | solution.py:299
  102.0 6.4 %all-to-all-start.1 = ((bf16[32,32,2048]{2,1,0:T(8,128)(2,1)}), bf16[32,32,2048]{2,1,0:T(8,128)(2,1)}, u32[]{:S(2)}, u32[]{:S(2)}) async-start(bf16[32,32,2048]{2,1,0:T(8,128)(2,1)} %back.1), calls=%async_computation.1 | async-start | bytes 8388608 | tf_op jit(solution)/shard_map/all_to_all | solution.py:311
  108.3 0.0 reduce-scatter.5.cloned.1.call-start
  108.4 18.2 %collective-permute-done.1 = bf16[1024,768]{1,0:T(8,128)(2,1)S(1)} collective-permute-done((bf16[1024,768]{1,0:T(8,128)(2,1)}, bf16[1024,768]{1,0:T(8,128)(2,1)S(1)}, u32[]{:S(2)}, u32[]{:S(2)}) %collective-permute-start.1) | collective-permute-done | bytes 1572896 | tf_op jit(solution)/shard_map/ppermute | solution.py:297
  126.6 1.6 add_convert_fusion
  128.2 0.0 reduce-scatter.5.cloned.1.call-update
  128.2 26.5 %reduce-scatter.3.cloned.1.call-done.early_ref = bf16[256,1536]{1,0:T(8,128)(2,1)} async-done(((bf16[2048,1536]{1,0:T(8,128)(2,1)}), bf16[256,1536]{1,0:T(8,128)(2,1)}) %reduce-scatter.3.cloned.1.call-update) | async-done | bytes 786448 | tf_op jit(solution)/shard_map/reduce_scatter | solution.py:281
  154.8 1.1 constant_dynamic-slice_fusion
  155.9 0.6 collective-permute-start
  156.5 16.6 %all-to-all-done.1.back_ref = bf16[32,32,2048]{2,1,0:T(8,128)(2,1)} async-done(((bf16[32,32,2048]{2,1,0:T(8,128)(2,1)}), bf16[32,32,2048]{2,1,0:T(8,128)(2,1)}, u32[]{:S(2)}, u32[]{:S(2)}) %all-to-all-start.1) | async-done | bytes 4194336 | tf_op jit(solution)/shard_map/all_to_all | solution.py:311
  173.1 4.3 %combine.1 = (bf16[128,2048]{1,0:T(8,128)(2,1)}, bf16[128,2048]{1,0:T(8,128)(2,1)}) custom-call(s32[2,128]{1,0:T(2,128)S(1)} %bitcast.10, f32[2,128]{1,0:T(2,128)S(1)} %bitcast.12, bf16[32,32,2048]{2,1,0:T(8,128)(2,1)} %all-to-all-done.1.back_ref), custom_call_target="tpu_custom_call" | custom-call | flops 805306368 | bytes 6291456 | tf_op jit(solution)/shard_map/combine/pallas_call | solution.py:314
  177.4 19.0 %reduce-scatter.5.cloned.1.call-done.late_ref = bf16[128,768]{1,0:T(8,128)(2,1)} async-done(((bf16[1024,768]{1,0:T(8,128)(2,1)}), bf16[128,768]{1,0:T(8,128)(2,1)}) %reduce-scatter.5.cloned.1.call-update) | async-done | bytes 196624 | tf_op jit(solution)/shard_map/reduce_scatter | solution.py:313
  196.4 0.0 collective-permute-done.came_ref
  196.4 0.9 copy-done.3
  197.3 0.9 join.1
  (15 shorter events, 0.0 us)
Async XLA Ops:
  7.2 147.6 %reduce-scatter.3.cloned.1.call-start = ((), (), s32[]{:S(2)}) async-start(), calls=%async_computation.4 | async-start | bytes 7077888 | tf_op jit(solution)/shard_map/reduce_scatter | solution.py:281
  7.2 60.3 %copy-start = (bf16[1,2048,2304]{2,1,0:T(8,128)(2,1)S(1)}, bf16[1,2048,2304]{2,1,0:T(8,128)(2,1)}, u32[]{:S(2)}) copy-start(bf16[1,2048,2304]{2,1,0:T(8,128)(2,1)} %param.9) | copy-start | bytes 28311556
  67.5 10.6 %copy-start.1 = (bf16[32,32,2048]{2,1,0:T(8,128)(2,1)}, bf16[32,32,2048]{2,1,0:T(8,128)(2,1)S(1)}, u32[]{:S(2)}) copy-start(bf16[32,32,2048]{2,1,0:T(8,128)(2,1)S(1)} %all_to_all.10.rows_ref) | copy-start | bytes 12582916
  78.2 11.7 %copy-start.9 = (bf16[512,512]{1,0:T(8,128)(2,1)S(1)}, bf16[512,512]{1,0:T(8,128)(2,1)}, u32[]{:S(2)}) copy-start(bf16[512,512]{1,0:T(8,128)(2,1)} %get-tuple-element.18.qg_ref) | copy-start | bytes 1572868
  78.2 11.7 %copy-start.10 = (bf16[512,512]{1,0:T(8,128)(2,1)S(1)}, bf16[512,512]{1,0:T(8,128)(2,1)}, u32[]{:S(2)}) copy-start(bf16[512,512]{1,0:T(8,128)(2,1)} %get-tuple-element.19.qu_ref) | copy-start | bytes 1572868
  78.2 11.7 %copy-start.11 = (bf16[512,512]{1,0:T(8,128)(2,1)S(1)}, bf16[512,512]{1,0:T(8,128)(2,1)}, u32[]{:S(2)}) copy-start(bf16[512,512]{1,0:T(8,128)(2,1)} %get-tuple-element.17.h_ref) | copy-start | bytes 1572868
  87.4 39.2 %collective-permute-start.1 = (bf16[1024,768]{1,0:T(8,128)(2,1)}, bf16[1024,768]{1,0:T(8,128)(2,1)S(1)}, u32[]{:S(2)}, u32[]{:S(2)}) collective-permute-start(bf16[1024,768]{1,0:T(8,128)(2,1)} %get-tuple-element.24), channel_id=1, source_target_pairs={{16,0},{17,1},{18,2},{19,3},{20,4},{21,5},{22,6},{23,7},{24,8},{25... | collective-permute-start | bytes 4718600 | tf_op jit(solution)/shard_map/ppermute | solution.py:297
  89.9 1.0 copy-start.6
  90.8 1.0 copy-start.7
  91.8 0.9 copy-start.8
  102.0 24.6 %copy-start.12 = (bf16[1024,768]{1,0:T(8,128)(2,1)S(1)}, bf16[1024,768]{1,0:T(8,128)(2,1)}, u32[]{:S(2)}) copy-start(bf16[1024,768]{1,0:T(8,128)(2,1)} %get-tuple-element.23) | copy-start | bytes 4718596
  102.0 71.1 %all-to-all-start.1 = ((bf16[32,32,2048]{2,1,0:T(8,128)(2,1)}), bf16[32,32,2048]{2,1,0:T(8,128)(2,1)}, u32[]{:S(2)}, u32[]{:S(2)}) async-start(bf16[32,32,2048]{2,1,0:T(8,128)(2,1)} %back.1), calls=%async_computation.1 | async-start | bytes 8388608 | tf_op jit(solution)/shard_map/all_to_all | solution.py:311
  108.3 88.0 %reduce-scatter.5.cloned.1.call-start = ((), (), s32[]{:S(2)}) async-start(), calls=%async_computation.5 | async-start | bytes 1769472 | tf_op jit(solution)/shard_map/reduce_scatter | solution.py:313
  126.6 46.5 %copy-start.4 = (s32[128,2]{0,1:T(2,128)S(1)}, s32[128,2]{0,1:T(2,128)}, u32[]{:S(2)}) copy-start(s32[128,2]{0,1:T(2,128)} %param.7) | copy-start | bytes 3076
  126.6 46.5 %copy-start.5 = (f32[128,2]{0,1:T(2,128)S(1)}, f32[128,2]{0,1:T(2,128)}, u32[]{:S(2)}) copy-start(f32[128,2]{0,1:T(2,128)} %param.8) | copy-start | bytes 3076
  154.8 41.6 %copy-start.2 = (bf16[256,1536]{1,0:T(8,128)(2,1)S(1)}, bf16[256,1536]{1,0:T(8,128)(2,1)}, u32[]{:S(2)}) copy-start(bf16[256,1536]{1,0:T(8,128)(2,1)} %reduce-scatter.3.cloned.1.call-done.early_ref) | copy-start | bytes 2359300
  155.9 40.5 %collective-permute-start = (bf16[128,1536]{1,0:T(8,128)(2,1)S(1)}, bf16[128,1536]{1,0:T(8,128)(2,1)S(1)}, u32[]{:S(2)}, u32[]{:S(2)}) collective-permute-start(bf16[128,1536]{1,0:T(8,128)(2,1)S(1)} %constant_dynamic-slice_fusion), channel_id=1, source_target_pairs={{16,0},{17,1},{18,2},{19,3},{20,4},{21,5},{22,6},{23,7},{24,8},{25... | collective-permute-start | bytes 1179656 | tf_op jit(solution)/shard_map/ppermute | solution.py:323
  196.4 0.9 copy-start.3
Sparse Core Ops, SparseCore 0:
  78.3 76.4 reduce-scatter.2
  157.3 39.0 reduce-scatter.4

commit v6 on v5

--- a/solution.py
+++ b/solution.py
@@ -140,6 +140,7 @@
     g_ref,
     u_ref,
     v_ref,
+    kept_ref,
     own_ref,
     sent_ref,
     qg_ref,
@@ -156,7 +157,7 @@
             if n is None:
                 expert_rows(rows_ref, g_ref[...], u_ref[...], v_ref[...], *refs)
                 return
-            rhs = refs[n][...]
+            rhs = refs[n][...] if j == 0 else kept_ref[...]
             begin = ROWS if n == 2 else 0
             for out_ref, which in ((own_ref, which_ref[0]), (sent_ref, 1 - which_ref[0])):
                 cols = pl.ds(pl.multiple_of(which * half, half), half)
@@ -196,6 +197,12 @@
         layer_ref[:, cols] = value.astype(BF16)
         dx = back_ref[:, ROWS:, cols].reshape(rows, step)
         grad_ref[:, cols] = dot(pick, dx, ((0,), (0,))).astype(BF16)
+
+
+def other_kernel(which_ref, summed_ref, out_ref):
+    half = out_ref.shape[0]
+    begin = pl.multiple_of((1 - which_ref[0]) * half, half)
+    out_ref[...] = summed_ref[pl.ds(begin, half), :]
 
 
 def join_kernel(early_plan, late_plan, which_ref, early_ref, came_ref, late_ref, out_ref):
@@ -257,19 +264,19 @@
     )(routes_t, gates_t, tokens, out_grad)
     came = lax.all_to_all(sent, "expert", split_axis=0, concat_axis=0, tiled=True)
 
-    early_plan = ((1, None), (1, 0), (1, 1), (1, 2), (2, None), (2, 0), (2, 1), (2, 2))
-    late_plan = ((0, None), (0, 0), (0, 1), (0, 2))
+    early_plan = ((1, None), (1, 0), (1, 1), (2, None), (2, 0), (2, 1), (2, 2))
+    late_plan = ((0, None), (0, 0), (0, 1), (0, 2), (1, 2))
     early_cols = tuple(one for one in early_plan if one[1] is not None)
     late_cols = tuple(one for one in late_plan if one[1] is not None)
     state = pltpu.HBM((rows, ff - chunk), BF16)
-    state_spec = pl.BlockSpec((rows, chunk), lambda p: (0, jnp.where(p >= 4, 1, 0)))
+    state_spec = pl.BlockSpec((rows, chunk), lambda p: (0, jnp.where(p >= 3, 1, 0)))
     early, qg, qu, h = pl.pallas_call(
         functools.partial(early_kernel, early_plan, groups),
         grid=(len(early_plan),),
         in_specs=[vmem, vmem],
         out_specs=[
             pl.BlockSpec(
-                (width, chunk), lambda p: (0, p - jnp.where(p > 0, 1, 0) - jnp.where(p > 4, 1, 0))
+                (width, chunk), lambda p: (0, p - jnp.where(p > 0, 1, 0) - jnp.where(p > 3, 1, 0))
             )
         ]
         + [state_spec] * 3,
@@ -286,13 +293,14 @@
         functools.partial(late_kernel, late_plan),
         grid=(len(late_plan),),
         in_specs=[smem, pl.BlockSpec((slots, 2 * ROWS, width), lambda p: (0, 0, 0))]
-        + [pl.BlockSpec((width, chunk), lambda p, n=n: (0, n * steps)) for n in range(3)],
+        + [pl.BlockSpec((width, chunk), lambda p, n=n: (0, n * steps)) for n in range(3)]
+        + [state_spec],
         out_specs=[half_spec] * 2 + [state_spec] * 3,
         out_shape=[pltpu.HBM((half, len(late_cols) * chunk), BF16)] * 2 + [state] * 3,
         compiler_params=params(50),
         cost_estimate=cost(4 * rows * width * ff, 8 * width * ff),
         name="late_grads",
-    )(which, came, weight, weight, weight)
+    )(which, came, weight, weight, weight, h)
     route = [((i + slots // 2) % slots, i) for i in range(slots)]
     came_half = lax.ppermute(sent_half, "expert", route)
     block = 512
@@ -315,11 +323,18 @@
         combine_kernel,
         out_shape=[jax.ShapeDtypeStruct((count, width), BF16)] * 2,
         compiler_params=params(24),
-        cost_estimate=cost(6 * rows * count * width, 6 * rows * width),
+        cost_estimate=cost(60 * rows * count * width, 6 * rows * width),
         name="combine",
     )(routes_t, gates_t, home)
     kept = half // groups
-    other = lax.dynamic_slice_in_dim(early_sum, (1 - upper) * kept, kept, 0)
+    other = pl.pallas_call(
+        other_kernel,
+        in_specs=[smem, vmem],
+        out_shape=jax.ShapeDtypeStruct((kept, early_sum.shape[1]), BF16),
+        compiler_params=params(8),
+        cost_estimate=cost(60 * rows * count * width, 4 * kept * width),
+        name="other",
+    )(which, early_sum)
     came_early = lax.ppermute(other, "expert", route)
     grad_weights = pl.pallas_call(
         functools.partial(join_kernel, early_cols, late_cols),

time: 206 us -> 207 us (level)
  the two profiles are of different devices: /device:TPU:4 before, /device:TPU:43 now
where the time goes in v6:
time: 207 us; the launch traced here: 206 us
  waiting for transfers between devices  76.9 us (37%)
  blocking collectives  56.4 us (27%)
  Pallas kernels  37.9 us (18%)
  between operations  14.1 us (7%)
  starting transfers between devices  10.9 us (5%)
  local copies, waits for them, and re-layouts  5.99 us (3%)
  other arithmetic  3.91 us (2%)
    all_to_all x1, blocking collectives, local(): lax.all_to_all(sent, 'expert', split_axis=0, concat_axis=0, tiled=True)  56.4 us
    all_to_all x1, waiting for transfers between devices, local(): lax.all_to_all(back, 'expert', split_axis=0, concat_axis=0, tiled=True)  48.3 us
    ppermute x1, waiting for transfers between devices, local(): came_half = lax.ppermute(sent_half, 'expert', route)  28.2 us
    pallas_call x1, Pallas kernels, local(): pl.pallas_call(functools.partial(late_kernel, late_plan), grid=(len(late_...  9.82 us
    pallas_call x1, Pallas kernels, local(): pl.pallas_call(functools.partial(early_kernel, early_plan, groups), grid=...  9.68 us
    pallas_call x1, Pallas kernels, local(): pl.pallas_call(back_kernel, grid=(width // block,), in_specs=[pl.BlockSpe...  9.17 us
    all_to_all x1, starting transfers between devices, local(): lax.all_to_all(back, 'expert', split_axis=0, concat_axis=0, tiled=True)  7.58 us
    unnamed x28, local copies, waits for them, and re-layouts  5.99 us
  transfers between devices with their start and end apart: 5, of which 3 were waited for; matrix products, arithmetic and copies ran while one was open for 2% of the time, Pallas kernels for 11%

profile of v6, /device:TPU:43, one launch (start us, length us, event | category | flops | bytes accessed | tf_op | source)
XLA Modules:
  0.0 206.1 jit_solution(4514088601366168511)
XLA Ops:
  7.2 0.0 reduce-scatter.3.cloned.1.call-start
  7.2 0.0 copy-start
  7.2 4.0 %pack.1 = bf16[32,32,2048]{2,1,0:T(8,128)(2,1)} custom-call(s32[2,128]{1,0:T(2,128)} %bitcast.9, f32[2,128]{1,0:T(2,128)} %bitcast.11, bf16[128,2048]{1,0:T(8,128)(2,1)} %tokens_hbm.1, bf16[128,2048]{1,0:T(8,128)(2,1)} %out_grad_hbm.1), custom_call_target="tpu_custom_call" | custom-call | flops 536870912 | bytes 6291456 | tf_op jit(solution)/shard_map/pack/pallas_call | solution.py:247
  11.2 56.4 %all_to_all.10.rows_ref = bf16[32,32,2048]{2,1,0:T(8,128)(2,1)S(1)} all-to-all(bf16[32,32,2048]{2,1,0:T(8,128)(2,1)} %pack.1), channel_id=1, replica_groups=mesh['dp'=8,'expert'=32] {'expert'}, dimensions={0} | all-to-all | bytes 8388608 | tf_op jit(solution)/shard_map/all_to_all | solution.py:265
  67.6 0.0 copy-done
  67.6 9.7 %early_grads.1 = (bf16[2048,1280]{1,0:T(8,128)(2,1)}, bf16[512,512]{1,0:T(8,128)(2,1)}, bf16[512,512]{1,0:T(8,128)(2,1)}, bf16[512,512]{1,0:T(8,128)(2,1)}) custom-call(bf16[32,32,2048]{2,1,0:T(8,128)(2,1)S(1)} %all_to_all.10.rows_ref, bf16[2048,2304]{1,0:T(8,128)(2,1)S(1)} %bitcast.8), custom_call_target="tpu_custom_call" | custom-call | flops 6442450944 | bytes 25165824 | tf_op jit(solution)/shard_map/early_grads/pallas_call | solution.py:273
  77.3 0.0 copy-done.1
  77.3 0.0 reduce-scatter.3.cloned.1.call-update
  77.4 1.0 copy-done.4
  78.4 9.8 %late_grads.1 = (bf16[1024,1024]{1,0:T(8,128)(2,1)}, bf16[1024,1024]{1,0:T(8,128)(2,1)}, bf16[512,256]{1,0:T(8,128)(2,1)}, bf16[512,256]{1,0:T(8,128)(2,1)}, bf16[512,256]{1,0:T(8,128)(2,1)}) custom-call(s32[1]{0:T(128)} %bitcast.2.which_ref, bf16[32,32,2048]{2,1,0:T(8,128)(2,1)} %copy-done.1, bf16[2048,2304]{1,0:T(8,128)(2,1)} %bitcast.4, ...), custom_call_target="tpu_custom_call" | custom-call | flops 3221225472 | bytes 12582912 | tf_op jit(solution)/shard_map/late_grads/pallas_call | solution.py:292
  88.2 1.4 collective-permute-start.1
  89.6 0.0 copy-done.11
  89.6 0.0 copy-done.12
  89.6 1.0 copy-done.8
  90.6 1.0 copy-done.9
  91.5 0.9 copy-done.10
  92.5 9.2 %back.1 = bf16[32,32,2048]{2,1,0:T(8,128)(2,1)} custom-call(bf16[512,256]{1,0:T(8,128)(2,1)S(1)} %copy-done.10, bf16[512,256]{1,0:T(8,128)(2,1)S(1)} %copy-done.8, bf16[512,256]{1,0:T(8,128)(2,1)S(1)} %copy-done.9, bf16[512,512]{1,0:T(8,128)(2,1)S(1)} %copy-done.4, bf16[512,512]{1,0:T(8,128)(2,1)S(1)} %copy-done.11, bf16[512,512]{1,0:T(8,128)(2,1)S(1)} %copy-done.12, ...), custom_call_target="tpu_custom_call" | custom-call | flops 4831838208 | bytes 18874368 | tf_op jit(solution)/shard_map/back/pallas_call | solution.py:307
  101.7 7.6 %all-to-all-start.1 = ((bf16[32,32,2048]{2,1,0:T(8,128)(2,1)}), bf16[32,32,2048]{2,1,0:T(8,128)(2,1)}, u32[]{:S(2)}, u32[]{:S(2)}) async-start(bf16[32,32,2048]{2,1,0:T(8,128)(2,1)} %back.1), calls=%async_computation.1 | async-start | bytes 8388608 | tf_op jit(solution)/shard_map/all_to_all | solution.py:319
  109.3 0.0 reduce-scatter.5.cloned.1.call-start
  109.3 28.2 %collective-permute-done.1 = bf16[1024,1024]{1,0:T(8,128)(2,1)} collective-permute-done((bf16[1024,1024]{1,0:T(8,128)(2,1)}, bf16[1024,1024]{1,0:T(8,128)(2,1)}, u32[]{:S(2)}, u32[]{:S(2)}) %collective-permute-start.1) | collective-permute-done | bytes 2097184 | tf_op jit(solution)/shard_map/ppermute | solution.py:305
  137.5 0.0 copy-done.13
  137.5 3.9 %add_convert_fusion = bf16[1024,1024]{1,0:T(8,128)(2,1)} fusion(bf16[1024,1024]{1,0:T(8,128)(2,1)} %collective-permute-done.1, bf16[1024,1024]{1,0:T(8,128)(2,1)S(1)} %copy-done.13), kind=kLoop, calls=%fused_computation | loop fusion | flops 4194304 | bytes 6291456 | tf_op jit(solution)/shard_map/convert_element_type | solution.py:320
  141.4 0.0 reduce-scatter.5.cloned.1.call-update
  141.4 0.4 reduce-scatter.3.cloned.1.call-done.summed_ref.early_ref
  141.8 1.1 copy-done.2
  142.9 0.0 copy-start.3
  142.9 1.9 collective-permute-start
  144.8 48.3 %all-to-all-done.1.back_ref = bf16[32,32,2048]{2,1,0:T(8,128)(2,1)} async-done(((bf16[32,32,2048]{2,1,0:T(8,128)(2,1)}), bf16[32,32,2048]{2,1,0:T(8,128)(2,1)}, u32[]{:S(2)}, u32[]{:S(2)}) %all-to-all-start.1) | async-done | bytes 4194336 | tf_op jit(solution)/shard_map/all_to_all | solution.py:319
  193.2 4.3 %combine.1 = (bf16[128,2048]{1,0:T(8,128)(2,1)}, bf16[128,2048]{1,0:T(8,128)(2,1)}) custom-call(s32[2,128]{1,0:T(2,128)S(1)} %bitcast.10, f32[2,128]{1,0:T(2,128)S(1)} %bitcast.12, bf16[32,32,2048]{2,1,0:T(8,128)(2,1)} %all-to-all-done.1.back_ref), custom_call_target="tpu_custom_call" | custom-call | flops 8053063680 | bytes 6291456 | tf_op jit(solution)/shard_map/combine/pallas_call | solution.py:322
  197.4 0.0 collective-permute-done.came_ref
  197.5 0.9 copy-done.5
  198.4 0.9 join.1
  (17 shorter events, 0.0 us)
Async XLA Ops:
  7.2 134.7 %reduce-scatter.3.cloned.1.call-start = ((), (), s32[]{:S(2)}) async-start(), calls=%async_computation.4 | async-start | bytes 5898240 | tf_op jit(solution)/shard_map/reduce_scatter | solution.py:288
  7.2 60.4 %copy-start = (bf16[1,2048,2304]{2,1,0:T(8,128)(2,1)S(1)}, bf16[1,2048,2304]{2,1,0:T(8,128)(2,1)}, u32[]{:S(2)}) copy-start(bf16[1,2048,2304]{2,1,0:T(8,128)(2,1)} %param.9) | copy-start | bytes 28311556
  67.6 9.7 %copy-start.1 = (bf16[32,32,2048]{2,1,0:T(8,128)(2,1)}, bf16[32,32,2048]{2,1,0:T(8,128)(2,1)S(1)}, u32[]{:S(2)}) copy-start(bf16[32,32,2048]{2,1,0:T(8,128)(2,1)S(1)} %all_to_all.10.rows_ref) | copy-start | bytes 12582916
  77.3 1.0 copy-start.4
  78.4 11.2 %copy-start.11 = (bf16[512,512]{1,0:T(8,128)(2,1)S(1)}, bf16[512,512]{1,0:T(8,128)(2,1)}, u32[]{:S(2)}) copy-start(bf16[512,512]{1,0:T(8,128)(2,1)} %get-tuple-element.18.qg_ref) | copy-start | bytes 1572868
  78.4 11.2 %copy-start.12 = (bf16[512,512]{1,0:T(8,128)(2,1)S(1)}, bf16[512,512]{1,0:T(8,128)(2,1)}, u32[]{:S(2)}) copy-start(bf16[512,512]{1,0:T(8,128)(2,1)} %get-tuple-element.19.qu_ref) | copy-start | bytes 1572868
  88.2 49.3 %collective-permute-start.1 = (bf16[1024,1024]{1,0:T(8,128)(2,1)}, bf16[1024,1024]{1,0:T(8,128)(2,1)}, u32[]{:S(2)}, u32[]{:S(2)}) collective-permute-start(bf16[1024,1024]{1,0:T(8,128)(2,1)} %get-tuple-element.24), channel_id=1, source_target_pairs={{16,0},{17,1},{18,2},{19,3},{20,4},{21,5},{22,6},{23,7},{24,8},{25... | collective-permute-start | bytes 6291464 | tf_op jit(solution)/shard_map/ppermute | solution.py:305
  89.6 1.0 copy-start.8
  90.6 1.0 copy-start.9
  91.5 0.9 copy-start.10
  101.7 35.8 %copy-start.13 = (bf16[1024,1024]{1,0:T(8,128)(2,1)S(1)}, bf16[1024,1024]{1,0:T(8,128)(2,1)}, u32[]{:S(2)}) copy-start(bf16[1024,1024]{1,0:T(8,128)(2,1)} %get-tuple-element.23) | copy-start | bytes 6291460
  101.7 91.5 %all-to-all-start.1 = ((bf16[32,32,2048]{2,1,0:T(8,128)(2,1)}), bf16[32,32,2048]{2,1,0:T(8,128)(2,1)}, u32[]{:S(2)}, u32[]{:S(2)}) async-start(bf16[32,32,2048]{2,1,0:T(8,128)(2,1)} %back.1), calls=%async_computation.1 | async-start | bytes 8388608 | tf_op jit(solution)/shard_map/all_to_all | solution.py:319
  109.3 88.2 %reduce-scatter.5.cloned.1.call-start = ((), (), s32[]{:S(2)}) async-start(), calls=%async_computation.5 | async-start | bytes 2359296 | tf_op jit(solution)/shard_map/reduce_scatter | solution.py:321
  141.8 1.1 copy-start.2
  142.9 50.3 %copy-start.6 = (s32[128,2]{0,1:T(2,128)S(1)}, s32[128,2]{0,1:T(2,128)}, u32[]{:S(2)}) copy-start(s32[128,2]{0,1:T(2,128)} %param.7) | copy-start | bytes 3076
  142.9 50.3 %copy-start.7 = (f32[128,2]{0,1:T(2,128)S(1)}, f32[128,2]{0,1:T(2,128)}, u32[]{:S(2)}) copy-start(f32[128,2]{0,1:T(2,128)} %param.8) | copy-start | bytes 3076
  142.9 54.5 %copy-start.3 = (bf16[256,1280]{1,0:T(8,128)(2,1)S(1)}, bf16[256,1280]{1,0:T(8,128)(2,1)}, u32[]{:S(2)}) copy-start(bf16[256,1280]{1,0:T(8,128)(2,1)} %reduce-scatter.3.cloned.1.call-done.summed_ref.early_ref) | copy-start | bytes 1966084
  142.9 54.5 %collective-permute-start = (bf16[128,1280]{1,0:T(8,128)(2,1)S(1)}, bf16[128,1280]{1,0:T(8,128)(2,1)S(1)}, u32[]{:S(2)}, u32[]{:S(2)}) collective-permute-start(bf16[128,1280]{1,0:T(8,128)(2,1)S(1)} %other.1), channel_id=1, source_target_pairs={{16,0},{17,1},{18,2},{19,3},{20,4},{21,5},{22,6},{23,7},{24,8},{25... | collective-permute-start | bytes 983048 | tf_op jit(solution)/shard_map/ppermute | solution.py:338
  197.5 1.0 copy-start.5
Sparse Core Ops, SparseCore 0:
  77.5 64.3 reduce-scatter.2
  144.4 37.5 reduce-scatter.4

commit v7 on v6

--- a/solution.py
+++ b/solution.py
@@ -9,7 +9,9 @@
 
 BF16 = jnp.bfloat16
 F32 = jnp.float32
+CAP = 14
 ROWS = 16
+LANES = 128
 
 
 def dot(a, b, dims):
@@ -32,9 +34,61 @@
         jnp.where(earlier, 1.0, 0.0).astype(BF16),
         ((1,), (0,)),
     ).astype(jnp.int32)
-    place = jnp.where(named, place, ROWS)
-    at = lax.broadcasted_iota(jnp.int32, (slots, ROWS, tokens), 1)
-    return names, place[:, None, :] == at
+    return names, jnp.where(named, place, ROWS)
+
+
+def by_slot(place):
+    at = lax.broadcasted_iota(jnp.int32, (place.shape[0], ROWS, place.shape[1]), 1)
+    return place[:, None, :] == at
+
+
+def by_place(place):
+    at = lax.broadcasted_iota(jnp.int32, (CAP,) + place.shape, 0)
+    return place[None, :, :] == at
+
+
+def onehot(mask):
+    return jnp.where(mask, 1.0, 0.0).astype(BF16)
+
+
+def strip_rows(slots, columns):
+    row = lax.broadcasted_iota(jnp.int32, (slots * ROWS, columns), 0)
+    col = lax.broadcasted_iota(jnp.int32, (slots * ROWS, columns), 1)
+    return onehot(row == (col % slots) * ROWS + CAP + col // slots)
+
+
+def strip_picks(slots):
+    row = lax.broadcasted_iota(jnp.int32, (2 * slots, slots * ROWS), 0)
+    col = lax.broadcasted_iota(jnp.int32, (2 * slots, slots * ROWS), 1)
+    return onehot(col == (row % slots) * ROWS + CAP + row // slots)
+
+
+def to_strips(tail, slots):
+    strips = [
+        jnp.concatenate(
+            [
+                tail[j * slots : (j + 1) * slots, q * LANES : (q + 1) * LANES]
+                for j in range(CAP)
+            ],
+            axis=1,
+        )
+        for q in range(2)
+    ]
+    return jnp.concatenate(strips, axis=0)
+
+
+def from_strips(strips, slots):
+    tails = [
+        jnp.concatenate(
+            [
+                strips[q * slots : (q + 1) * slots, j * LANES : (j + 1) * LANES]
+                for j in range(CAP)
+            ],
+            axis=0,
+        )
+        for q in range(2)
+    ]
+    return jnp.concatenate(tails, axis=1)
 
 
 def slot_gates(names, gates):
@@ -58,9 +112,9 @@
     in_sems,
     out_sems,
 ):
-    slots, _, width = send_ref.shape
+    slots, _, main = send_ref.shape
     pieces = out_sems.shape[0]
-    step = width // pieces
+    step = main // pieces
     pairs = (
         (routes_hbm, routes_ref),
         (gates_hbm, gates_ref),
@@ -71,19 +125,35 @@
     for load in loads:
         load.start()
     loads[0].wait()
-    names, mask = dispatch_mask(routes_ref[...], slots)
-    pick = jnp.where(mask, 1.0, 0.0).reshape(slots * ROWS, -1).astype(BF16)
+    names, place = dispatch_mask(routes_ref[...], slots)
+    mask, turned = by_slot(place), by_place(place)
+    rows = slots * ROWS
+    pick = jnp.concatenate([onehot(mask).reshape(rows, -1), strip_rows(slots, LANES)], axis=1)
+    tail_pick = onehot(turned).reshape(CAP * slots, -1)
     loads[1].wait()
     weight = slot_gates(names, gates_ref[...])
     row_gate = jnp.sum(jnp.where(mask, weight[:, None, :], 0.0), axis=2, keepdims=True)
+    row_gate = jnp.where(
+        lax.broadcasted_iota(jnp.int32, row_gate.shape, 1) < CAP, row_gate, 1.0
+    )
+    tail_gate = jnp.sum(jnp.where(turned, weight[None, :, :], 0.0), axis=2, keepdims=True)
+    tail_gate = tail_gate.reshape(CAP * slots, 1)
     loads[2].wait()
     loads[3].wait()
+    x_tail = dot(tail_pick, tokens_ref[:, main:], ((1,), (0,)))
+    dy_tail = dot(tail_pick, out_grad_ref[:, main:], ((1,), (0,))) * tail_gate
+    blank = jnp.zeros((LANES - 2 * slots, main), BF16)
+    x_strips = jnp.concatenate([to_strips(x_tail.astype(BF16), slots), blank], axis=0)
+    dy_strips = jnp.concatenate([to_strips(dy_tail.astype(BF16), slots), blank], axis=0)
     stores = []
     for piece in range(pieces):
+        at = slice(piece * step, (piece + 1) * step)
         cols = pl.ds(piece * step, step)
-        x = dot(pick, tokens_ref[:, cols], ((1,), (0,)))
+        source = jnp.concatenate([tokens_ref[:, at], x_strips[:, at]], axis=0)
+        x = dot(pick, source, ((1,), (0,)))
         send_ref[:, :ROWS, cols] = x.astype(BF16).reshape(slots, ROWS, step)
-        g = dot(pick, out_grad_ref[:, cols], ((1,), (0,))).reshape(slots, ROWS, step)
+        source = jnp.concatenate([out_grad_ref[:, at], dy_strips[:, at]], axis=0)
+        g = dot(pick, source, ((1,), (0,))).reshape(slots, ROWS, step)
         send_ref[:, ROWS:, cols] = (row_gate * g).astype(BF16)
         stores.append(
             pltpu.make_async_copy(
@@ -95,11 +165,22 @@
         store.wait()
 
 
-def expert_rows(rows_ref, g, u, v, qg_ref, qu_ref, h_ref):
-    slots, _, width = rows_ref.shape
+def unpack_rows(rows_ref, begin, out_ref):
+    slots, _, main = rows_ref.shape
     rows = slots * ROWS
-    x = rows_ref[:, :ROWS, :].reshape(rows, width)
-    dy = rows_ref[:, ROWS:, :].reshape(rows, width)
+    came = rows_ref[:, begin : begin + ROWS, :]
+    live = lax.broadcasted_iota(jnp.int32, (1, ROWS, 1), 1) < CAP
+    out_ref[:, :main] = jnp.where(live, came, jnp.zeros((), BF16)).reshape(rows, main)
+    strips = dot(strip_picks(slots), came.reshape(rows, main), ((1,), (0,))).astype(BF16)
+    row = lax.broadcasted_iota(jnp.int32, (rows, CAP * slots), 0)
+    col = lax.broadcasted_iota(jnp.int32, (rows, CAP * slots), 1)
+    turn = onehot(col == (row % ROWS) * slots + row // ROWS)
+    out_ref[:, main:] = dot(turn, from_strips(strips, slots), ((1,), (0,))).astype(BF16)
+
+
+def expert_rows(x_ref, dy_ref, g, u, v, qg_ref, qu_ref, h_ref):
+    x = x_ref[...]
+    dy = dy_ref[...]
     a = dot(x, g, ((1,), (0,)))
     b = dot(x, u, ((1,), (0,)))
     e = dot(dy, v, ((1,), (0,)))
@@ -110,33 +191,62 @@
     qu_ref[...] = (e * active).astype(BF16)
 
 
-def early_kernel(plan, groups, rows_ref, w_ref, partial_ref, qg_ref, qu_ref, h_ref):
-    slots, _, width = rows_ref.shape
-    rows = slots * ROWS
+def early_kernel(
+    plan,
+    groups,
+    rows_ref,
+    w_ref,
+    partial_ref,
+    qg_ref,
+    qu_ref,
+    h_ref,
+    x_hbm,
+    dy_hbm,
+    x_ref,
+    dy_ref,
+    sems,
+):
+    width = x_ref.shape[1]
     block = width // 2 // groups
     refs = (qg_ref, qu_ref, h_ref)
+
+    def copies():
+        return [
+            pltpu.make_async_copy(x_ref, x_hbm, sems.at[0]),
+            pltpu.make_async_copy(dy_ref, dy_hbm, sems.at[1]),
+        ]
+
     for step, (j, n) in enumerate(plan):
 
         @pl.when(pl.program_id(0) == step)
-        def _(j=j, n=n):
+        def _(step=step, j=j, n=n):
+            if step == 0:
+                unpack_rows(rows_ref, 0, x_ref)
+                unpack_rows(rows_ref, ROWS, dy_ref)
+                for copy in copies():
+                    copy.start()
             if n is None:
                 chunk, ff = h_ref.shape[1], w_ref.shape[1] // 3
                 begins = [n * ff + j * chunk for n in range(3)]
-                expert_rows(rows_ref, *(w_ref[:, at : at + chunk] for at in begins), *refs)
+                weights = (w_ref[:, at : at + chunk] for at in begins)
+                expert_rows(x_ref, dy_ref, *weights, *refs)
                 return
-            begin = ROWS if n == 2 else 0
-            lhs = rows_ref[:, begin : begin + ROWS, :].reshape(rows, width)
-            value = dot(lhs, refs[n][...], ((0,), (0,))).astype(BF16)
+            lhs_ref = dy_ref if n == 2 else x_ref
+            value = dot(lhs_ref[...], refs[n][...], ((0,), (0,))).astype(BF16)
             for half in range(2):
                 for d in range(groups):
                     old, new = (half * groups + d) * block, (2 * d + half) * block
                     partial_ref[new : new + block] = value[old : old + block]
+            if step == len(plan) - 1:
+                for copy in copies():
+                    copy.wait()
 
 
 def late_kernel(
     plan,
     which_ref,
-    rows_ref,
+    x_ref,
+    dy_ref,
     g_ref,
     u_ref,
     v_ref,
@@ -147,56 +257,91 @@
     qu_ref,
     h_ref,
 ):
-    slots, _, width = rows_ref.shape
-    rows, half = slots * ROWS, width // 2
+    half = x_ref.shape[1] // 2
     refs = (qg_ref, qu_ref, h_ref)
     for step, (j, n) in enumerate(plan):
 
         @pl.when(pl.program_id(0) == step)
         def _(j=j, n=n):
             if n is None:
-                expert_rows(rows_ref, g_ref[...], u_ref[...], v_ref[...], *refs)
+                expert_rows(x_ref, dy_ref, g_ref[...], u_ref[...], v_ref[...], *refs)
                 return
             rhs = refs[n][...] if j == 0 else kept_ref[...]
-            begin = ROWS if n == 2 else 0
+            lhs_ref = dy_ref if n == 2 else x_ref
             for out_ref, which in ((own_ref, which_ref[0]), (sent_ref, 1 - which_ref[0])):
                 cols = pl.ds(pl.multiple_of(which * half, half), half)
-                lhs = rows_ref[:, begin : begin + ROWS, cols].reshape(rows, half)
-                out_ref[...] = dot(lhs, rhs, ((0,), (0,))).astype(BF16)
-
-
-def back_kernel(h0_ref, qg0_ref, qu0_ref, h_ref, qg_ref, qu_ref, w_ref, out_ref):
+                out_ref[...] = dot(lhs_ref[:, cols], rhs, ((0,), (0,))).astype(BF16)
+
+
+def back_kernel(
+    h0_ref, qg0_ref, qu0_ref, h_ref, qg_ref, qu_ref, w_ref, tail_ref, out_ref, strips_ref
+):
     slots, _, block = out_ref.shape
+    rows = slots * ROWS
     chunk = h0_ref.shape[1]
     ff = w_ref.shape[1] // 3
-
-    def product(first_ref, rest_ref, base):
-        value = dot(first_ref[...], w_ref[:, base : base + chunk], ((1,), (1,)))
-        return value + dot(rest_ref[...], w_ref[:, base + chunk : base + ff], ((1,), (1,)))
-
-    y = product(h0_ref, h_ref, 2 * ff)
-    out_ref[:, :ROWS, :] = y.astype(BF16).reshape(slots, ROWS, block)
-    dx = product(qg0_ref, qg_ref, 0) + product(qu0_ref, qu_ref, ff)
-    out_ref[:, ROWS:, :] = dx.astype(BF16).reshape(slots, ROWS, block)
+    at = pl.program_id(0)
+
+    def product(first_ref, rest_ref, lines_ref, base):
+        value = dot(first_ref[...], lines_ref[:, base : base + chunk], ((1,), (1,)))
+        rest = lines_ref[:, base + chunk : base + ff]
+        return value + dot(rest_ref[...], rest, ((1,), (1,)))
+
+    def both(lines_ref):
+        y = product(h0_ref, h_ref, lines_ref, 2 * ff)
+        dx = product(qg0_ref, qg_ref, lines_ref, 0) + product(qu0_ref, qu_ref, lines_ref, ff)
+        return y, dx
+
+    @pl.when(at == 0)
+    def _():
+        row = lax.broadcasted_iota(jnp.int32, (CAP * slots, rows), 0)
+        col = lax.broadcasted_iota(jnp.int32, (CAP * slots, rows), 1)
+        turn = onehot(col == (row % slots) * ROWS + row // slots)
+        for i, value in enumerate(both(tail_ref)):
+            tail = dot(turn, value.astype(BF16), ((1,), (0,))).astype(BF16)
+            strips = to_strips(tail, slots)
+            for p in range(strips_ref.shape[0]):
+                strips_ref[p, i] = strips[:, p * block : (p + 1) * block]
+
+    spread = strip_rows(slots, 2 * slots)
+    for i, value in enumerate(both(w_ref)):
+        value = value.astype(BF16).astype(F32) + dot(spread, strips_ref[at, i], ((1,), (0,)))
+        out_ref[:, i * ROWS : (i + 1) * ROWS, :] = value.astype(BF16).reshape(slots, ROWS, block)
 
 
 def combine_kernel(routes_ref, gates_ref, back_ref, layer_ref, grad_ref):
-    slots, _, width = back_ref.shape
-    names, mask = dispatch_mask(routes_ref[...], slots)
+    slots, _, main = back_ref.shape
+    rows = slots * ROWS
+    names, place = dispatch_mask(routes_ref[...], slots)
     weight = slot_gates(names, gates_ref[...])
-    rows = slots * ROWS
-    gate = jnp.where(mask, weight[:, None, :], 0.0).reshape(rows, -1)
-    high = gate.astype(BF16)
-    low = (gate - high.astype(F32)).astype(BF16)
-    pick = jnp.where(mask, 1.0, 0.0).reshape(rows, -1).astype(BF16)
-    step = 512
-    for c in range(0, width, step):
+
+    def split(mask, value):
+        gate = jnp.where(mask, value, 0.0).reshape(-1, value.shape[-1])
+        high = gate.astype(BF16)
+        return high, (gate - high.astype(F32)).astype(BF16)
+
+    mask, turned = by_slot(place), by_place(place)
+    high, low = split(mask, weight[:, None, :])
+    tail_high, tail_low = split(turned, weight[None, :, :])
+    pick = onehot(mask).reshape(rows, -1)
+    tail_pick = onehot(turned).reshape(CAP * slots, -1)
+    take = strip_picks(slots)
+    step = 256
+    y_strips, dx_strips = [], []
+    for c in range(0, main, step):
         cols = slice(c, c + step)
         y = back_ref[:, :ROWS, cols].reshape(rows, step)
         value = dot(high, y, ((0,), (0,))) + dot(low, y, ((0,), (0,)))
         layer_ref[:, cols] = value.astype(BF16)
+        y_strips.append(dot(take, y, ((1,), (0,))).astype(BF16))
         dx = back_ref[:, ROWS:, cols].reshape(rows, step)
         grad_ref[:, cols] = dot(pick, dx, ((0,), (0,))).astype(BF16)
+        dx_strips.append(dot(take, dx, ((1,), (0,))).astype(BF16))
+    y = from_strips(jnp.concatenate(y_strips, axis=1), slots)
+    value = dot(tail_high, y, ((0,), (0,))) + dot(tail_low, y, ((0,), (0,)))
+    layer_ref[:, main:] = value.astype(BF16)
+    dx = from_strips(jnp.concatenate(dx_strips, axis=1), slots)
+    grad_ref[:, main:] = dot(tail_pick, dx, ((0,), (0,))).astype(BF16)
 
 
 def other_kernel(which_ref, summed_ref, out_ref):
@@ -242,7 +387,9 @@
     which = upper.reshape(1)
     smem = pl.BlockSpec(memory_space=pltpu.SMEM)
     vmem = pl.BlockSpec(memory_space=pltpu.VMEM)
-    pair = pltpu.HBM((slots, 2 * ROWS, width), BF16)
+    main = width - 2 * LANES
+    pair = pltpu.HBM((slots, 2 * ROWS, main), BF16)
+    flat = pltpu.HBM((rows, width), BF16)
     hbm = pl.BlockSpec(memory_space=pltpu.HBM)
     sent = pl.pallas_call(
         pack_kernel,
@@ -254,9 +401,9 @@
             pltpu.VMEM((top, count), F32),
             pltpu.VMEM((count, width), BF16),
             pltpu.VMEM((count, width), BF16),
-            pltpu.VMEM((slots, 2 * ROWS, width), BF16),
+            pltpu.VMEM((slots, 2 * ROWS, main), BF16),
             pltpu.SemaphoreType.DMA((4,)),
-            pltpu.SemaphoreType.DMA((4,)),
+            pltpu.SemaphoreType.DMA((7,)),
         ],
         compiler_params=params(54.2),
         cost_estimate=cost(4 * rows * count * width, 6 * rows * width),
@@ -270,7 +417,7 @@
     late_cols = tuple(one for one in late_plan if one[1] is not None)
     state = pltpu.HBM((rows, ff - chunk), BF16)
     state_spec = pl.BlockSpec((rows, chunk), lambda p: (0, jnp.where(p >= 3, 1, 0)))
-    early, qg, qu, h = pl.pallas_call(
+    early, qg, qu, h, x, dy = pl.pallas_call(
         functools.partial(early_kernel, early_plan, groups),
         grid=(len(early_plan),),
         in_specs=[vmem, vmem],
@@ -279,9 +426,15 @@
                 (width, chunk), lambda p: (0, p - jnp.where(p > 0, 1, 0) - jnp.where(p > 3, 1, 0))
             )
         ]
-        + [state_spec] * 3,
-        out_shape=[pltpu.HBM((width, len(early_cols) * chunk), BF16)] + [state] * 3,
-        compiler_params=params(16),
+        + [state_spec] * 3
+        + [hbm] * 2,
+        out_shape=[pltpu.HBM((width, len(early_cols) * chunk), BF16)] + [state] * 3 + [flat] * 2,
+        scratch_shapes=[
+            pltpu.VMEM((rows, width), BF16),
+            pltpu.VMEM((rows, width), BF16),
+            pltpu.SemaphoreType.DMA((2,)),
+        ],
+        compiler_params=params(26),
         cost_estimate=cost(8 * rows * width * ff, 16 * width * ff),
         name="early_grads",
     )(came, weight)
@@ -292,30 +445,35 @@
     own, sent_half, qg0, qu0, h0 = pl.pallas_call(
         functools.partial(late_kernel, late_plan),
         grid=(len(late_plan),),
-        in_specs=[smem, pl.BlockSpec((slots, 2 * ROWS, width), lambda p: (0, 0, 0))]
+        in_specs=[smem]
+        + [pl.BlockSpec((rows, width), lambda p: (0, 0))] * 2
         + [pl.BlockSpec((width, chunk), lambda p, n=n: (0, n * steps)) for n in range(3)]
         + [state_spec],
         out_specs=[half_spec] * 2 + [state_spec] * 3,
         out_shape=[pltpu.HBM((half, len(late_cols) * chunk), BF16)] * 2 + [state] * 3,
-        compiler_params=params(50),
+        compiler_params=params(63),
         cost_estimate=cost(4 * rows * width * ff, 8 * width * ff),
         name="late_grads",
-    )(which, came, weight, weight, weight, h)
+    )(which, x, dy, weight, weight, weight, h)
     route = [((i + slots // 2) % slots, i) for i in range(slots)]
     came_half = lax.ppermute(sent_half, "expert", route)
-    block = 512
+    block = main // 2
     back = pl.pallas_call(
         back_kernel,
-        grid=(width // block,),
+        grid=(main // block,),
         in_specs=[pl.BlockSpec((rows, chunk), lambda j: (0, 0))] * 3
         + [pl.BlockSpec((rows, ff - chunk), lambda j: (0, 0))] * 3
-        + [pl.BlockSpec((block, 3 * ff), lambda j: (j, 0))],
+        + [
+            pl.BlockSpec((block, 3 * ff), lambda j: (j, 0)),
+            pl.BlockSpec((2 * LANES, 3 * ff), lambda j: (main // (2 * LANES), 0)),
+        ],
         out_specs=pl.BlockSpec((slots, 2 * ROWS, block), lambda j: (0, 0, j)),
         out_shape=pair,
-        compiler_params=params(50),
+        scratch_shapes=[pltpu.VMEM((main // block, 2, 2 * slots, block), BF16)],
+        compiler_params=params(63),
         cost_estimate=cost(6 * rows * width * ff, 12 * width * ff),
         name="back",
-    )(h0, qg0, qu0, h, qg, qu, weight)
+    )(h0, qg0, qu0, h, qg, qu, weight, weight)
     home = lax.all_to_all(back, "expert", split_axis=0, concat_axis=0, tiled=True)
     late = (own.astype(F32) + came_half.astype(F32)).astype(BF16)
     late_sum = lax.psum_scatter(late, "dp", scatter_dimension=0, tiled=True)

time: 207 us -> 196 us (0.947)
  the two profiles are of different devices: /device:TPU:43 before, /device:TPU:4 now
where the time goes in v7:
time: 196 us; the launch traced here: 193 us
  waiting for transfers between devices  69.9 us (36%)
  blocking collectives  51 us (26%)
  Pallas kernels  42.9 us (22%)
  between operations  14.1 us (7%)
  starting transfers between devices  9.28 us (5%)
  other arithmetic  3.93 us (2%)
  local copies, waits for them, and re-layouts  2.05 us (1%)
    all_to_all x1, blocking collectives, local(): lax.all_to_all(sent, 'expert', split_axis=0, concat_axis=0, tiled=True)  51 us
    all_to_all x1, waiting for transfers between devices, local(): lax.all_to_all(back, 'expert', split_axis=0, concat_axis=0, tiled=True)  38.6 us
    ppermute x1, waiting for transfers between devices, local(): came_half = lax.ppermute(sent_half, 'expert', route)  29.4 us
    pallas_call x1, Pallas kernels, local(): pl.pallas_call(back_kernel, grid=(main // block,), in_specs=[pl.BlockSpec...  12.4 us
    pallas_call x1, Pallas kernels, local(): pl.pallas_call(functools.partial(early_kernel, early_plan, groups), grid=...  10.8 us
    pallas_call x1, Pallas kernels, local(): pl.pallas_call(functools.partial(late_kernel, late_plan), grid=(len(late_...  10.2 us
    all_to_all x1, starting transfers between devices, local(): lax.all_to_all(back, 'expert', split_axis=0, concat_axis=0, tiled=True)  6.65 us
    pallas_call x1, Pallas kernels, local(): pl.pallas_call(combine_kernel, out_shape=[jax.ShapeDtypeStruct((count, wi...  4.86 us
  transfers between devices with their start and end apart: 5, of which 3 were waited for; matrix products, arithmetic and copies ran while one was open for 2% of the time, Pallas kernels for 14%

profile of v7, /device:TPU:4, one launch (start us, length us, event | category | flops | bytes accessed | tf_op | source)
XLA Modules:
  0.0 193.2 jit_solution(2957324812708537219)
XLA Ops:
  7.2 0.0 reduce-scatter.3.cloned.1.call-start
  7.2 0.0 copy-start
  7.2 3.8 %pack.1 = bf16[32,32,1792]{2,1,0:T(8,128)(2,1)} custom-call(s32[2,128]{1,0:T(2,128)} %bitcast.10, f32[2,128]{1,0:T(2,128)} %bitcast.12, bf16[128,2048]{1,0:T(8,128)(2,1)} %tokens_hbm.1, bf16[128,2048]{1,0:T(8,128)(2,1)} %out_grad_hbm.1), custom_call_target="tpu_custom_call" | custom-call | flops 536870912 | bytes 6291456 | tf_op jit(solution)/shard_map/pack/pallas_call | solution.py:394
  11.0 51.0 %all_to_all.10.rows_ref = bf16[32,32,1792]{2,1,0:T(8,128)(2,1)S(1)} all-to-all(bf16[32,32,1792]{2,1,0:T(8,128)(2,1)} %pack.1), channel_id=1, replica_groups=mesh['dp'=8,'expert'=32] {'expert'}, dimensions={0} | all-to-all | bytes 7340032 | tf_op jit(solution)/shard_map/all_to_all | solution.py:412
  62.0 0.0 copy-done
  62.0 10.8 %early_grads.1 = (bf16[2048,1280]{1,0:T(8,128)(2,1)}, bf16[512,512]{1,0:T(8,128)(2,1)}, bf16[512,512]{1,0:T(8,128)(2,1)}, bf16[512,512]{1,0:T(8,128)(2,1)}, bf16...) custom-call(bf16[32,32,1792]{2,1,0:T(8,128)(2,1)S(1)} %all_to_all.10.rows_ref, bf16[2048,2304]{1,0:T(8,128)(2,1)S(1)} %bitcast.9), custom_call_target="tpu_custom_call" | custom-call | flops 6442450944 | bytes 25165824 | tf_op jit(solution)/shard_map/early_grads/pallas_call | solution.py:420
  72.8 0.0 reduce-scatter.3.cloned.1.call-update
  72.8 10.2 %late_grads.1 = (bf16[1024,1024]{1,0:T(8,128)(2,1)}, bf16[1024,1024]{1,0:T(8,128)(2,1)}, bf16[512,256]{1,0:T(8,128)(2,1)}, bf16[512,256]{1,0:T(8,128)(2,1)}, bf16[512,256]{1,0:T(8,128)(2,1)}) custom-call(s32[1]{0:T(128)} %bitcast.2.which_ref, bf16[512,2048]{1,0:T(8,128)(2,1)} %get-tuple-element.16.x_ref, bf16[512,2048]{1,0:T(8,128)(2,1)} %get-tuple-element.17.dy_ref, ...), custom_call_target="tpu_custom_call" | custom-call | flops 3221225472 | bytes 12582912 | tf_op jit(solution)/shard_map/late_grads/pallas_call | solution.py:445
  83.0 1.9 collective-permute-start.1
  84.9 12.4 %back.1 = bf16[32,32,1792]{2,1,0:T(8,128)(2,1)} custom-call(bf16[512,256]{1,0:T(8,128)(2,1)} %get-tuple-element.19.h0_ref, bf16[512,256]{1,0:T(8,128)(2,1)} %get-tuple-element.20.qg0_ref, bf16[512,256]{1,0:T(8,128)(2,1)} %get-tuple-element.21.qu0_ref, bf16[512,512]{1,0:T(8,128)(2,1)} %get-tuple-element.18.kept_ref.h_ref, ...), custom_call_target="tpu_custom_call" | custom-call | flops 4831838208 | bytes 18874368 | tf_op jit(solution)/shard_map/back/pallas_call | solution.py:461
  97.3 0.0 copy-start.6
  97.3 6.7 %all-to-all-start.1 = ((bf16[32,32,1792]{2,1,0:T(8,128)(2,1)}), bf16[32,32,1792]{2,1,0:T(8,128)(2,1)}, u32[]{:S(2)}, u32[]{:S(2)}) async-start(bf16[32,32,1792]{2,1,0:T(8,128)(2,1)} %back.1), calls=%async_computation.1 | async-start | bytes 7340032 | tf_op jit(solution)/shard_map/all_to_all | solution.py:477
  104.0 0.0 reduce-scatter.5.cloned.1.call-start
  104.0 29.4 %collective-permute-done.1 = bf16[1024,1024]{1,0:T(8,128)(2,1)} collective-permute-done((bf16[1024,1024]{1,0:T(8,128)(2,1)}, bf16[1024,1024]{1,0:T(8,128)(2,1)}, u32[]{:S(2)}, u32[]{:S(2)}) %collective-permute-start.1) | collective-permute-done | bytes 2097184 | tf_op jit(solution)/shard_map/ppermute | solution.py:459
  133.4 0.0 copy-done.6
  133.4 3.9 %add_convert_fusion = bf16[1024,1024]{1,0:T(8,128)(2,1)} fusion(bf16[1024,1024]{1,0:T(8,128)(2,1)} %collective-permute-done.1, bf16[1024,1024]{1,0:T(8,128)(2,1)S(1)} %copy-done.6), kind=kLoop, calls=%fused_computation | loop fusion | flops 4194304 | bytes 6291456 | tf_op jit(solution)/shard_map/convert_element_type | solution.py:478
  137.3 0.0 reduce-scatter.5.cloned.1.call-update
  137.4 1.8 reduce-scatter.3.cloned.1.call-done.summed_ref.early_ref
  139.2 0.0 copy-start.1
  139.2 1.1 copy-done.1
  140.3 0.0 copy-start.4
  140.3 0.0 copy-start.2
  140.3 0.6 collective-permute-start
  141.0 38.6 %all-to-all-done.1.back_ref = bf16[32,32,1792]{2,1,0:T(8,128)(2,1)} async-done(((bf16[32,32,1792]{2,1,0:T(8,128)(2,1)}), bf16[32,32,1792]{2,1,0:T(8,128)(2,1)}, u32[]{:S(2)}, u32[]{:S(2)}) %all-to-all-start.1) | async-done | bytes 3670048 | tf_op jit(solution)/shard_map/all_to_all | solution.py:477
  179.6 0.0 copy-done.4
  179.6 0.0 copy-done.5
  179.6 4.9 %combine.1 = (bf16[128,2048]{1,0:T(8,128)(2,1)}, bf16[128,2048]{1,0:T(8,128)(2,1)}) custom-call(s32[2,128]{1,0:T(2,128)S(1)} %bitcast.11, f32[2,128]{1,0:T(2,128)S(1)} %bitcast.13, bf16[32,32,1792]{2,1,0:T(8,128)(2,1)} %all-to-all-done.1.back_ref), custom_call_target="tpu_custom_call" | custom-call | flops 8053063680 | bytes 6291456 | tf_op jit(solution)/shard_map/combine/pallas_call | solution.py:480
  184.5 0.0 collective-permute-done.came_ref
  184.5 0.0 copy-done.2
  184.5 0.0 copy-start.3
  184.5 0.9 copy-done.3
  185.4 0.9 join.1
  (3 shorter events, 0.0 us)
Async XLA Ops:
  7.2 132.0 %reduce-scatter.3.cloned.1.call-start = ((), (), s32[]{:S(2)}) async-start(), calls=%async_computation.4 | async-start | bytes 5898240 | tf_op jit(solution)/shard_map/reduce_scatter | solution.py:441
  7.2 54.8 %copy-start = (bf16[1,2048,2304]{2,1,0:T(8,128)(2,1)S(1)}, bf16[1,2048,2304]{2,1,0:T(8,128)(2,1)}, u32[]{:S(2)}) copy-start(bf16[1,2048,2304]{2,1,0:T(8,128)(2,1)} %param.9) | copy-start | bytes 28311556
  83.0 50.4 %collective-permute-start.1 = (bf16[1024,1024]{1,0:T(8,128)(2,1)}, bf16[1024,1024]{1,0:T(8,128)(2,1)}, u32[]{:S(2)}, u32[]{:S(2)}) collective-permute-start(bf16[1024,1024]{1,0:T(8,128)(2,1)} %get-tuple-element.28), channel_id=1, source_target_pairs={{16,0},{17,1},{18,2},{19,3},{20,4},{21,5},{22,6},{23,7},{24,8},{25... | collective-permute-start | bytes 6291464 | tf_op jit(solution)/shard_map/ppermute | solution.py:459
  97.3 36.1 %copy-start.6 = (bf16[1024,1024]{1,0:T(8,128)(2,1)S(1)}, bf16[1024,1024]{1,0:T(8,128)(2,1)}, u32[]{:S(2)}) copy-start(bf16[1024,1024]{1,0:T(8,128)(2,1)} %get-tuple-element.27) | copy-start | bytes 6291460
  97.3 82.3 %all-to-all-start.1 = ((bf16[32,32,1792]{2,1,0:T(8,128)(2,1)}), bf16[32,32,1792]{2,1,0:T(8,128)(2,1)}, u32[]{:S(2)}, u32[]{:S(2)}) async-start(bf16[32,32,1792]{2,1,0:T(8,128)(2,1)} %back.1), calls=%async_computation.1 | async-start | bytes 7340032 | tf_op jit(solution)/shard_map/all_to_all | solution.py:477
  104.0 80.5 %reduce-scatter.5.cloned.1.call-start = ((), (), s32[]{:S(2)}) async-start(), calls=%async_computation.5 | async-start | bytes 2359296 | tf_op jit(solution)/shard_map/reduce_scatter | solution.py:479
  139.2 1.1 copy-start.1
  140.3 39.3 %copy-start.4 = (s32[128,2]{0,1:T(2,128)S(1)}, s32[128,2]{0,1:T(2,128)}, u32[]{:S(2)}) copy-start(s32[128,2]{0,1:T(2,128)} %param.7) | copy-start | bytes 3076
  140.3 39.3 %copy-start.5 = (f32[128,2]{0,1:T(2,128)S(1)}, f32[128,2]{0,1:T(2,128)}, u32[]{:S(2)}) copy-start(f32[128,2]{0,1:T(2,128)} %param.8) | copy-start | bytes 3076
  140.3 44.2 %copy-start.2 = (bf16[256,1280]{1,0:T(8,128)(2,1)S(1)}, bf16[256,1280]{1,0:T(8,128)(2,1)}, u32[]{:S(2)}) copy-start(bf16[256,1280]{1,0:T(8,128)(2,1)} %reduce-scatter.3.cloned.1.call-done.summed_ref.early_ref) | copy-start | bytes 1966084
  140.3 44.1 %collective-permute-start = (bf16[128,1280]{1,0:T(8,128)(2,1)S(1)}, bf16[128,1280]{1,0:T(8,128)(2,1)S(1)}, u32[]{:S(2)}, u32[]{:S(2)}) collective-permute-start(bf16[128,1280]{1,0:T(8,128)(2,1)S(1)} %other.1), channel_id=1, source_target_pairs={{16,0},{17,1},{18,2},{19,3},{20,4},{21,5},{22,6},{23,7},{24,8},{25... | collective-permute-start | bytes 983048 | tf_op jit(solution)/shard_map/ppermute | solution.py:496
  184.5 1.0 copy-start.3
Sparse Core Ops, SparseCore 0:
  73.0 66.2 reduce-scatter.2
  141.8 40.6 reduce-scatter.4

commit v8 on v7

--- a/solution.py
+++ b/solution.py
@@ -242,35 +242,49 @@
                     copy.wait()
 
 
+def half_grads(x_ref, dy_ref, n, which, rhs):
+    lhs_ref = dy_ref if n == 2 else x_ref
+    half = lhs_ref.shape[1] // 2
+    cols = pl.ds(pl.multiple_of(which * half, half), half)
+    return dot(lhs_ref[:, cols], rhs, ((0,), (0,))).astype(BF16)
+
+
 def late_kernel(
-    plan,
-    which_ref,
-    x_ref,
-    dy_ref,
-    g_ref,
-    u_ref,
-    v_ref,
-    kept_ref,
-    own_ref,
-    sent_ref,
-    qg_ref,
-    qu_ref,
-    h_ref,
+    plan, which_ref, x_ref, dy_ref, g_ref, u_ref, v_ref, sent_ref, qg_ref, qu_ref, h_ref
 ):
-    half = x_ref.shape[1] // 2
     refs = (qg_ref, qu_ref, h_ref)
-    for step, (j, n) in enumerate(plan):
+    for step, n in enumerate(plan):
 
         @pl.when(pl.program_id(0) == step)
-        def _(j=j, n=n):
+        def _(n=n):
             if n is None:
                 expert_rows(x_ref, dy_ref, g_ref[...], u_ref[...], v_ref[...], *refs)
                 return
+            sent_ref[...] = half_grads(x_ref, dy_ref, n, 1 - which_ref[0], refs[n][...])
+
+
+def later_kernel(
+    plan, which_ref, x_ref, dy_ref, qg_ref, qu_ref, h_ref, kept_ref, sent_ref, own_ref
+):
+    refs = (qg_ref, qu_ref, h_ref)
+    for step, (j, n, out) in enumerate(plan):
+
+        @pl.when(pl.program_id(0) == step)
+        def _(j=j, n=n, out=out):
             rhs = refs[n][...] if j == 0 else kept_ref[...]
-            lhs_ref = dy_ref if n == 2 else x_ref
-            for out_ref, which in ((own_ref, which_ref[0]), (sent_ref, 1 - which_ref[0])):
-                cols = pl.ds(pl.multiple_of(which * half, half), half)
-                out_ref[...] = dot(lhs_ref[:, cols], rhs, ((0,), (0,))).astype(BF16)
+            which = which_ref[0] if out else 1 - which_ref[0]
+            (sent_ref, own_ref)[out][...] = half_grads(x_ref, dy_ref, n, which, rhs)
+
+
+def late_sum_kernel(own_ref, came_ref, out_ref):
+    out_ref[...] = (own_ref[...].astype(F32) + came_ref[...].astype(F32)).astype(BF16)
+
+
+def late_join_kernel(first_ref, own_ref, came_ref, out_ref):
+    columns = came_ref.shape[1]
+    out_ref[:, :columns] = first_ref[...]
+    total = own_ref[...].astype(F32) + came_ref[...].astype(F32)
+    out_ref[:, columns:] = total.astype(BF16)
 
 
 def back_kernel(
@@ -309,9 +323,19 @@
         out_ref[:, i * ROWS : (i + 1) * ROWS, :] = value.astype(BF16).reshape(slots, ROWS, block)
 
 
-def combine_kernel(routes_ref, gates_ref, back_ref, layer_ref, grad_ref):
+def combine_kernel(routes_ref, gates_ref, back_hbm, layer_ref, grad_ref, back_ref, sems):
     slots, _, main = back_ref.shape
     rows = slots * ROWS
+    step = main // sems.shape[0]
+    loads = []
+    for c in range(0, main, step):
+        cols = pl.ds(c, step)
+        loads.append(
+            pltpu.make_async_copy(
+                back_hbm.at[:, :, cols], back_ref.at[:, :, cols], sems.at[c // step]
+            )
+        )
+        loads[-1].start()
     names, place = dispatch_mask(routes_ref[...], slots)
     weight = slot_gates(names, gates_ref[...])
 
@@ -326,10 +350,10 @@
     pick = onehot(mask).reshape(rows, -1)
     tail_pick = onehot(turned).reshape(CAP * slots, -1)
     take = strip_picks(slots)
-    step = 256
     y_strips, dx_strips = [], []
     for c in range(0, main, step):
         cols = slice(c, c + step)
+        loads[c // step].wait()
         y = back_ref[:, :ROWS, cols].reshape(rows, step)
         value = dot(high, y, ((0,), (0,))) + dot(low, y, ((0,), (0,)))
         layer_ref[:, cols] = value.astype(BF16)
@@ -412,9 +436,8 @@
     came = lax.all_to_all(sent, "expert", split_axis=0, concat_axis=0, tiled=True)
 
     early_plan = ((1, None), (1, 0), (1, 1), (2, None), (2, 0), (2, 1), (2, 2))
-    late_plan = ((0, None), (0, 0), (0, 1), (0, 2), (1, 2))
     early_cols = tuple(one for one in early_plan if one[1] is not None)
-    late_cols = tuple(one for one in late_plan if one[1] is not None)
+    late_cols = ((0, 0), (0, 1), (0, 2), (1, 2))
     state = pltpu.HBM((rows, ff - chunk), BF16)
     state_spec = pl.BlockSpec((rows, chunk), lambda p: (0, jnp.where(p >= 3, 1, 0)))
     early, qg, qu, h, x, dy = pl.pallas_call(
@@ -441,22 +464,37 @@
     early_sum = lax.psum_scatter(early, "dp", scatter_dimension=0, tiled=True)
     state = pltpu.HBM((rows, chunk), BF16)
     state_spec = pl.BlockSpec((rows, chunk), lambda p: (0, 0))
-    half_spec = pl.BlockSpec((half, chunk), lambda p: (0, jnp.maximum(p - 1, 0)))
-    own, sent_half, qg0, qu0, h0 = pl.pallas_call(
-        functools.partial(late_kernel, late_plan),
-        grid=(len(late_plan),),
-        in_specs=[smem]
-        + [pl.BlockSpec((rows, width), lambda p: (0, 0))] * 2
-        + [pl.BlockSpec((width, chunk), lambda p, n=n: (0, n * steps)) for n in range(3)]
-        + [state_spec],
-        out_specs=[half_spec] * 2 + [state_spec] * 3,
-        out_shape=[pltpu.HBM((half, len(late_cols) * chunk), BF16)] * 2 + [state] * 3,
+    flat_spec = pl.BlockSpec((rows, width), lambda p: (0, 0))
+    sent_shape = pltpu.HBM((half, 2 * chunk), BF16)
+    sent_first, qg0, qu0, h0 = pl.pallas_call(
+        functools.partial(late_kernel, (None, 0, 1)),
+        grid=(3,),
+        in_specs=[smem, flat_spec, flat_spec]
+        + [pl.BlockSpec((width, chunk), lambda p, n=n: (0, n * steps)) for n in range(3)],
+        out_specs=[pl.BlockSpec((half, chunk), lambda p: (0, jnp.maximum(p - 1, 0)))]
+        + [state_spec] * 3,
+        out_shape=[sent_shape] + [state] * 3,
         compiler_params=params(63),
-        cost_estimate=cost(4 * rows * width * ff, 8 * width * ff),
+        cost_estimate=cost(3 * rows * width * ff, 8 * width * ff),
         name="late_grads",
-    )(which, x, dy, weight, weight, weight, h)
+    )(which, x, dy, weight, weight, weight)
     route = [((i + slots // 2) % slots, i) for i in range(slots)]
-    came_half = lax.ppermute(sent_half, "expert", route)
+    came_first = lax.ppermute(sent_first, "expert", route)
+    plan = ((0, 2, 0), (1, 2, 0), (0, 0, 1), (0, 1, 1), (0, 2, 1), (1, 2, 1))
+    sent_second, own = pl.pallas_call(
+        functools.partial(later_kernel, plan),
+        grid=(len(plan),),
+        in_specs=[smem, flat_spec, flat_spec] + [state_spec] * 4,
+        out_specs=[
+            pl.BlockSpec((half, chunk), lambda p: (0, jnp.minimum(p, 1))),
+            pl.BlockSpec((half, chunk), lambda p: (0, jnp.maximum(p - 2, 0))),
+        ],
+        out_shape=[sent_shape, pltpu.HBM((half, len(late_cols) * chunk), BF16)],
+        compiler_params=params(63),
+        cost_estimate=cost(2 * rows * width * ff, 8 * width * ff),
+        name="later_grads",
+    )(which, x, dy, qg0, qu0, h0, h)
+    came_second = lax.ppermute(sent_second, "expert", route)
     block = main // 2
     back = pl.pallas_call(
         back_kernel,
@@ -475,12 +513,38 @@
         name="back",
     )(h0, qg0, qu0, h, qg, qu, weight, weight)
     home = lax.all_to_all(back, "expert", split_axis=0, concat_axis=0, tiled=True)
-    late = (own.astype(F32) + came_half.astype(F32)).astype(BF16)
+    lines = half // 4
+    part_spec = pl.BlockSpec((lines, 2 * chunk), lambda p: (p, 0))
+    late_first = pl.pallas_call(
+        late_sum_kernel,
+        grid=(4,),
+        in_specs=[part_spec] * 2,
+        out_specs=part_spec,
+        out_shape=sent_shape,
+        compiler_params=params(63),
+        cost_estimate=cost(60 * rows * count * width, 16 * half * chunk),
+        name="late_sum",
+    )(own, came_first)
+    late = pl.pallas_call(
+        late_join_kernel,
+        grid=(4,),
+        in_specs=[part_spec, pl.BlockSpec((lines, 2 * chunk), lambda p: (p, 1)), part_spec],
+        out_specs=pl.BlockSpec((lines, 4 * chunk), lambda p: (p, 0)),
+        out_shape=pltpu.HBM((half, 4 * chunk), BF16),
+        compiler_params=params(63),
+        cost_estimate=cost(half * 4 * chunk, 24 * half * chunk),
+        name="late_join",
+    )(late_first, own, came_second)
     late_sum = lax.psum_scatter(late, "dp", scatter_dimension=0, tiled=True)
     layer_out, grad_tokens = pl.pallas_call(
         combine_kernel,
+        in_specs=[vmem, vmem, hbm],
+        scratch_shapes=[
+            pltpu.VMEM((slots, 2 * ROWS, main), BF16),
+            pltpu.SemaphoreType.DMA((7,)),
+        ],
         out_shape=[jax.ShapeDtypeStruct((count, width), BF16)] * 2,
-        compiler_params=params(24),
+        compiler_params=params(63),
         cost_estimate=cost(60 * rows * count * width, 6 * rows * width),
         name="combine",
     )(routes_t, gates_t, home)

time: 196 us -> 193 us (0.985)
  Pallas kernels: 42.9 us -> 56.1 us
  waiting for transfers between devices: 69.9 us -> 57.4 us
  other arithmetic: 3.93 us -> 0 us
    pallas_call x2 -> x5, Pallas kernels: 15.1 us -> 27.7 us  [the longest x1 7.4 us: local(): pl.pallas_call(functools.partial(later_kernel, plan), grid=(len(plan),),...]
    ppermute x1 -> x2, waiting for transfers between devices: 29.4 us -> 17.2 us  [the longest x1 17.1 us: local(): came_second = lax.ppermute(sent_second, 'expert', route)]
    convert_element_type x1 -> x0, other arithmetic: 3.93 us -> none  [local(): late = (own.astype(F32) + came_half.astype(F32)).astype(BF16)]
    all_to_all x1, waiting for transfers between devices: 38.6 us -> 35 us  [local(): lax.all_to_all(back, 'expert', split_axis=0, concat_axis=0, tiled=True)]
    reduce_scatter x1, waiting for transfers between devices: 1.85 us -> 4.73 us  [local(): early_sum = lax.psum_scatter(early, 'dp', scatter_dimension=0, tiled=True)]
  transfers between devices with their start and end apart: 5 -> 6, of which waited for: 3 -> 4; matrix products, arithmetic and copies ran while one was open for 2% -> 0% of each run, Pallas kernels for 14% -> 21%
where the time goes in v8:
time: 193 us; the launch traced here: 191 us
  waiting for transfers between devices  57.4 us (30%)
  Pallas kernels  56.1 us (29%)
  blocking collectives  51 us (26%)
  between operations  14.1 us (7%)
  starting transfers between devices  10.5 us (5%)
  local copies, waits for them, and re-layouts  2.05 us (1%)
    all_to_all x1, blocking collectives, local(): lax.all_to_all(sent, 'expert', split_axis=0, concat_axis=0, tiled=True)  51 us
    all_to_all x1, waiting for transfers between devices, local(): lax.all_to_all(back, 'expert', split_axis=0, concat_axis=0, tiled=True)  35 us
    ppermute x1, waiting for transfers between devices, local(): came_second = lax.ppermute(sent_second, 'expert', route)  17.1 us
    pallas_call x1, Pallas kernels, local(): pl.pallas_call(back_kernel, grid=(main // block,), in_specs=[pl.BlockSpec...  12.2 us
    pallas_call x1, Pallas kernels, local(): pl.pallas_call(functools.partial(early_kernel, early_plan, groups), grid=...  10.8 us
    pallas_call x1, Pallas kernels, local(): pl.pallas_call(functools.partial(later_kernel, plan), grid=(len(plan),),...  7.4 us
    pallas_call x1, Pallas kernels, local(): pl.pallas_call(functools.partial(late_kernel, (None, 0, 1)), grid=(3,), i...  7.27 us
    all_to_all x1, starting transfers between devices, local(): lax.all_to_all(back, 'expert', split_axis=0, concat_axis=0, tiled=True)  6.29 us
  transfers between devices with their start and end apart: 6, of which 4 were waited for; matrix products, arithmetic and copies ran while one was open for 0% of the time, Pallas kernels for 21%

profile of v8, /device:TPU:4, one launch (start us, length us, event | category | flops | bytes accessed | tf_op | source)
XLA Modules:
  0.0 191.1 jit_solution(14046439284885184168)
XLA Ops:
  7.2 0.0 reduce-scatter.3.cloned.1.call-start
  7.2 0.0 copy-start
  7.2 3.8 %pack.1 = bf16[32,32,1792]{2,1,0:T(8,128)(2,1)} custom-call(s32[2,128]{1,0:T(2,128)} %bitcast.10, f32[2,128]{1,0:T(2,128)} %bitcast.12, bf16[128,2048]{1,0:T(8,128)(2,1)} %tokens_hbm.1, bf16[128,2048]{1,0:T(8,128)(2,1)} %out_grad_hbm.1), custom_call_target="tpu_custom_call" | custom-call | flops 536870912 | bytes 6291456 | tf_op jit(solution)/shard_map/pack/pallas_call | solution.py:418
  11.0 51.0 %all_to_all.10.rows_ref = bf16[32,32,1792]{2,1,0:T(8,128)(2,1)S(1)} all-to-all(bf16[32,32,1792]{2,1,0:T(8,128)(2,1)} %pack.1), channel_id=1, replica_groups=mesh['dp'=8,'expert'=32] {'expert'}, dimensions={0} | all-to-all | bytes 7340032 | tf_op jit(solution)/shard_map/all_to_all | solution.py:436
  62.0 0.0 copy-done
  62.0 10.8 %early_grads.1 = (bf16[2048,1280]{1,0:T(8,128)(2,1)}, bf16[512,512]{1,0:T(8,128)(2,1)}, bf16[512,512]{1,0:T(8,128)(2,1)}, bf16[512,512]{1,0:T(8,128)(2,1)}, bf16...) custom-call(bf16[32,32,1792]{2,1,0:T(8,128)(2,1)S(1)} %all_to_all.10.rows_ref, bf16[2048,2304]{1,0:T(8,128)(2,1)S(1)} %bitcast.9), custom_call_target="tpu_custom_call" | custom-call | flops 6442450944 | bytes 25165824 | tf_op jit(solution)/shard_map/early_grads/pallas_call | solution.py:443
  72.8 0.0 reduce-scatter.3.cloned.1.call-update
  72.8 7.3 %late_grads.1 = (bf16[1024,512]{1,0:T(8,128)(2,1)}, bf16[512,256]{1,0:T(8,128)(2,1)}, bf16[512,256]{1,0:T(8,128)(2,1)}, bf16[512,256]{1,0:T(8,128)(2,1)}) custom-call(s32[1]{0:T(128)} %bitcast.2.which_ref, bf16[512,2048]{1,0:T(8,128)(2,1)} %get-tuple-element.17.x_ref, bf16[512,2048]{1,0:T(8,128)(2,1)} %get-tuple-element.18.dy_ref, ...), custom_call_target="tpu_custom_call" | custom-call | flops 2415919104 | bytes 12582912 | tf_op jit(solution)/shard_map/late_grads/pallas_call | solution.py:469
  80.1 1.8 collective-permute-start.1
  81.9 7.4 %later_grads.1 = (bf16[1024,512]{1,0:T(8,128)(2,1)}, bf16[1024,1024]{1,0:T(8,128)(2,1)}) custom-call(s32[1]{0:T(128)} %bitcast.2.which_ref, bf16[512,2048]{1,0:T(8,128)(2,1)} %get-tuple-element.17.x_ref, bf16[512,2048]{1,0:T(8,128)(2,1)} %get-tuple-element.18.dy_ref, bf16[512,256]{1,0:T(8,128)(2,1)} %get-tuple-element.20.qg0_ref.qg_ref, ...), custom_call_target="tpu_custom_call" | custom-call | flops 1610612736 | bytes 12582912 | tf_op jit(solution)/shard_map/later_grads/pallas_call | solution.py:484
  89.3 1.7 collective-permute-start.2
  91.1 12.2 %back.1 = bf16[32,32,1792]{2,1,0:T(8,128)(2,1)} custom-call(bf16[512,256]{1,0:T(8,128)(2,1)} %get-tuple-element.19.h0_ref.h_ref, bf16[512,256]{1,0:T(8,128)(2,1)} %get-tuple-element.20.qg0_ref.qg_ref, bf16[512,256]{1,0:T(8,128)(2,1)} %get-tuple-element.21.qu0_ref.qu_ref, bf16[512,512]{1,0:T(8,128)(2,1)} %get-tuple-element.22.h_ref.kept_ref, ...), custom_call_target="tpu_custom_call" | custom-call | flops 4831838208 | bytes 18874368 | tf_op jit(solution)/shard_map/back/pallas_call | solution.py:499
  103.3 6.3 %all-to-all-start.1 = ((bf16[32,32,1792]{2,1,0:T(8,128)(2,1)}), bf16[32,32,1792]{2,1,0:T(8,128)(2,1)}, u32[]{:S(2)}, u32[]{:S(2)}) async-start(bf16[32,32,1792]{2,1,0:T(8,128)(2,1)} %back.1), calls=%async_computation.1 | async-start | bytes 7340032 | tf_op jit(solution)/shard_map/all_to_all | solution.py:515
  109.6 0.0 reduce-scatter.5.cloned.1.call-start
  109.6 0.0 collective-permute-done.1.came_ref
  109.6 3.6 %late_sum.1.first_ref = bf16[1024,512]{1,0:T(8,128)(2,1)} custom-call(bf16[1024,1024]{1,0:T(8,128)(2,1)} %get-tuple-element.28.own_ref, bf16[1024,512]{1,0:T(8,128)(2,1)} %collective-permute-done.1.came_ref), custom_call_target="tpu_custom_call" | custom-call | flops 8053063680 | bytes 4194304 | tf_op jit(solution)/shard_map/late_sum/pallas_call | solution.py:518
  113.3 17.1 %collective-permute-done.2.came_ref = bf16[1024,512]{1,0:T(8,128)(2,1)} collective-permute-done((bf16[1024,512]{1,0:T(8,128)(2,1)}, bf16[1024,512]{1,0:T(8,128)(2,1)}, u32[]{:S(2)}, u32[]{:S(2)}) %collective-permute-start.2) | collective-permute-done | bytes 1048608 | tf_op jit(solution)/shard_map/ppermute | solution.py:497
  130.4 4.0 %late_join.1 = bf16[1024,1024]{1,0:T(8,128)(2,1)} custom-call(bf16[1024,512]{1,0:T(8,128)(2,1)} %late_sum.1.first_ref, bf16[1024,1024]{1,0:T(8,128)(2,1)} %get-tuple-element.28.own_ref, bf16[1024,512]{1,0:T(8,128)(2,1)} %collective-permute-done.2.came_ref), custom_call_target="tpu_custom_call" | custom-call | flops 1048576 | bytes 6291456 | tf_op jit(solution)/shard_map/late_join/pallas_call | solution.py:528
  134.4 0.0 reduce-scatter.5.cloned.1.call-update
  134.5 4.7 %reduce-scatter.3.cloned.1.call-done.summed_ref.early_ref = bf16[256,1280]{1,0:T(8,128)(2,1)} async-done(((bf16[2048,1280]{1,0:T(8,128)(2,1)}), bf16[256,1280]{1,0:T(8,128)(2,1)}) %reduce-scatter.3.cloned.1.call-update) | async-done | bytes 655376 | tf_op jit(solution)/shard_map/reduce_scatter | solution.py:464
  139.2 0.0 copy-start.1
  139.2 1.1 copy-done.1
  140.3 0.7 other.1
  141.0 0.0 copy-start.2
  141.0 0.6 collective-permute-start
  141.6 35.0 %all-to-all-done.1.back_hbm = bf16[32,32,1792]{2,1,0:T(8,128)(2,1)} async-done(((bf16[32,32,1792]{2,1,0:T(8,128)(2,1)}), bf16[32,32,1792]{2,1,0:T(8,128)(2,1)}, u32[]{:S(2)}, u32[]{:S(2)}) %all-to-all-start.1) | async-done | bytes 3670048 | tf_op jit(solution)/shard_map/all_to_all | solution.py:515
  176.6 5.4 %combine.1 = (bf16[128,2048]{1,0:T(8,128)(2,1)}, bf16[128,2048]{1,0:T(8,128)(2,1)}) custom-call(s32[2,128]{1,0:T(2,128)} %bitcast.11, f32[2,128]{1,0:T(2,128)} %bitcast.13, bf16[32,32,1792]{2,1,0:T(8,128)(2,1)} %all-to-all-done.1.back_hbm), custom_call_target="tpu_custom_call" | custom-call | flops 8053063680 | bytes 6291456 | tf_op jit(solution)/shard_map/combine/pallas_call | solution.py:539
  182.0 0.4 reduce-scatter.5.cloned.1.call-done.late_ref
  182.4 0.0 collective-permute-done.came_ref
  182.4 0.0 copy-done.2
  182.4 0.9 copy-done.3
  183.4 0.9 join.1
  (1 shorter events, 0.0 us)
Async XLA Ops:
  7.2 132.0 %reduce-scatter.3.cloned.1.call-start = ((), (), s32[]{:S(2)}) async-start(), calls=%async_computation.4 | async-start | bytes 5898240 | tf_op jit(solution)/shard_map/reduce_scatter | solution.py:464
  7.2 54.8 %copy-start = (bf16[1,2048,2304]{2,1,0:T(8,128)(2,1)S(1)}, bf16[1,2048,2304]{2,1,0:T(8,128)(2,1)}, u32[]{:S(2)}) copy-start(bf16[1,2048,2304]{2,1,0:T(8,128)(2,1)} %param.9) | copy-start | bytes 28311556
  80.1 29.5 %collective-permute-start.1 = (bf16[1024,512]{1,0:T(8,128)(2,1)}, bf16[1024,512]{1,0:T(8,128)(2,1)}, u32[]{:S(2)}, u32[]{:S(2)}) collective-permute-start(bf16[1024,512]{1,0:T(8,128)(2,1)} %get-tuple-element.29), channel_id=1, source_target_pairs={{16,0},{17,1},{18,2},{19,3},{20,4},{21,5},{22,6},{23,7},{24,8},{25... | collective-permute-start | bytes 3145736 | tf_op jit(solution)/shard_map/ppermute | solution.py:482
  89.3 41.1 %collective-permute-start.2 = (bf16[1024,512]{1,0:T(8,128)(2,1)}, bf16[1024,512]{1,0:T(8,128)(2,1)}, u32[]{:S(2)}, u32[]{:S(2)}) collective-permute-start(bf16[1024,512]{1,0:T(8,128)(2,1)} %get-tuple-element.30), channel_id=1, source_target_pairs={{16,0},{17,1},{18,2},{19,3},{20,4},{21,5},{22,6},{23,7},{24,8},{25... | collective-permute-start | bytes 3145736 | tf_op jit(solution)/shard_map/ppermute | solution.py:497
  103.3 73.3 %all-to-all-start.1 = ((bf16[32,32,1792]{2,1,0:T(8,128)(2,1)}), bf16[32,32,1792]{2,1,0:T(8,128)(2,1)}, u32[]{:S(2)}, u32[]{:S(2)}) async-start(bf16[32,32,1792]{2,1,0:T(8,128)(2,1)} %back.1), calls=%async_computation.1 | async-start | bytes 7340032 | tf_op jit(solution)/shard_map/all_to_all | solution.py:515
  109.6 72.9 %reduce-scatter.5.cloned.1.call-start = ((), (), s32[]{:S(2)}) async-start(), calls=%async_computation.5 | async-start | bytes 2359296 | tf_op jit(solution)/shard_map/reduce_scatter | solution.py:538
  139.2 1.1 copy-start.1
  141.0 41.4 %copy-start.2 = (bf16[256,1280]{1,0:T(8,128)(2,1)S(1)}, bf16[256,1280]{1,0:T(8,128)(2,1)}, u32[]{:S(2)}) copy-start(bf16[256,1280]{1,0:T(8,128)(2,1)} %reduce-scatter.3.cloned.1.call-done.summed_ref.early_ref) | copy-start | bytes 1966084
  141.0 41.4 %collective-permute-start = (bf16[128,1280]{1,0:T(8,128)(2,1)}, bf16[128,1280]{1,0:T(8,128)(2,1)S(1)}, u32[]{:S(2)}, u32[]{:S(2)}) collective-permute-start(bf16[128,1280]{1,0:T(8,128)(2,1)} %other.1), channel_id=1, source_target_pairs={{16,0},{17,1},{18,2},{19,3},{20,4},{21,5},{22,6},{23,7},{24,8},{25... | collective-permute-start | bytes 983048 | tf_op jit(solution)/shard_map/ppermute | solution.py:560
  182.4 1.0 copy-start.3
Sparse Core Ops, SparseCore 0:
  72.9 66.2 reduce-scatter.2
  141.8 40.6 reduce-scatter.4

commit v9 on v8

--- a/solution.py
+++ b/solution.py
@@ -178,17 +178,20 @@
     out_ref[:, main:] = dot(turn, from_strips(strips, slots), ((1,), (0,))).astype(BF16)
 
 
-def expert_rows(x_ref, dy_ref, g, u, v, qg_ref, qu_ref, h_ref):
-    x = x_ref[...]
-    dy = dy_ref[...]
-    a = dot(x, g, ((1,), (0,)))
-    b = dot(x, u, ((1,), (0,)))
-    e = dot(dy, v, ((1,), (0,)))
+def state_rows(a, b, e, qg_ref, qu_ref, h_ref):
     s = jax.nn.sigmoid(a)
     active = a * s
     h_ref[...] = (active * b).astype(BF16)
     qg_ref[...] = (e * b * s * (1.0 + a * (1.0 - s))).astype(BF16)
     qu_ref[...] = (e * active).astype(BF16)
+
+
+def expert_rows(x_ref, dy_ref, g, u, v, qg_ref, qu_ref, h_ref):
+    x = x_ref[...]
+    a = dot(x, g, ((1,), (0,)))
+    b = dot(x, u, ((1,), (0,)))
+    e = dot(dy_ref[...], v, ((1,), (0,)))
+    state_rows(a, b, e, qg_ref, qu_ref, h_ref)
 
 
 def early_kernel(
@@ -250,16 +253,45 @@
 
 
 def late_kernel(
-    plan, which_ref, x_ref, dy_ref, g_ref, u_ref, v_ref, sent_ref, qg_ref, qu_ref, h_ref
+    plan,
+    which_ref,
+    x_hbm,
+    dy_hbm,
+    w_hbm,
+    sent_ref,
+    qg_ref,
+    qu_ref,
+    h_ref,
+    x_ref,
+    dy_ref,
+    w_ref,
+    sems,
 ):
     refs = (qg_ref, qu_ref, h_ref)
+    chunk = h_ref.shape[1]
+    ff = w_hbm.shape[1] // 3
+
+    @pl.when(pl.program_id(0) == 0)
+    def _():
+        pairs = [(w_hbm.at[:, pl.ds(n * ff, chunk)], w_ref.at[n]) for n in range(3)]
+        pairs = [(x_hbm, x_ref), pairs[0], pairs[1], (dy_hbm, dy_ref), pairs[2]]
+        loads = [pltpu.make_async_copy(*pair, sems.at[i]) for i, pair in enumerate(pairs)]
+        for load in loads:
+            load.start()
+        loads[0].wait()
+        loads[1].wait()
+        a = dot(x_ref[...], w_ref[0], ((1,), (0,)))
+        loads[2].wait()
+        b = dot(x_ref[...], w_ref[1], ((1,), (0,)))
+        loads[3].wait()
+        loads[4].wait()
+        e = dot(dy_ref[...], w_ref[2], ((1,), (0,)))
+        state_rows(a, b, e, *refs)
+
     for step, n in enumerate(plan):
 
-        @pl.when(pl.program_id(0) == step)
+        @pl.when(pl.program_id(0) == step + 1)
         def _(n=n):
-            if n is None:
-                expert_rows(x_ref, dy_ref, g_ref[...], u_ref[...], v_ref[...], *refs)
-                return
             sent_ref[...] = half_grads(x_ref, dy_ref, n, 1 - which_ref[0], refs[n][...])
 
 
@@ -326,6 +358,7 @@
 def combine_kernel(routes_ref, gates_ref, back_hbm, layer_ref, grad_ref, back_ref, sems):
     slots, _, main = back_ref.shape
     rows = slots * ROWS
+    count = layer_ref.shape[0]
     step = main // sems.shape[0]
     loads = []
     for c in range(0, main, step):
@@ -339,33 +372,35 @@
     names, place = dispatch_mask(routes_ref[...], slots)
     weight = slot_gates(names, gates_ref[...])
 
-    def split(mask, value):
-        gate = jnp.where(mask, value, 0.0).reshape(-1, value.shape[-1])
+    def split(gate):
         high = gate.astype(BF16)
-        return high, (gate - high.astype(F32)).astype(BF16)
+        return [high, (gate - high.astype(F32)).astype(BF16)]
+
+    def turned_rows(mask, value):
+        return jnp.where(mask, value, 0.0).reshape(-1, value.shape[-1]).T
 
     mask, turned = by_slot(place), by_place(place)
-    high, low = split(mask, weight[:, None, :])
-    tail_high, tail_low = split(turned, weight[None, :, :])
-    pick = onehot(mask).reshape(rows, -1)
-    tail_pick = onehot(turned).reshape(CAP * slots, -1)
     take = strip_picks(slots)
+    y_pick = jnp.concatenate(split(turned_rows(mask, weight[:, None, :])) + [take], axis=0)
+    dx_pick = turned_rows(mask, jnp.ones((1, 1, count), F32)).astype(BF16)
+    dx_pick = jnp.concatenate([dx_pick, take], axis=0)
     y_strips, dx_strips = [], []
     for c in range(0, main, step):
         cols = slice(c, c + step)
         loads[c // step].wait()
-        y = back_ref[:, :ROWS, cols].reshape(rows, step)
-        value = dot(high, y, ((0,), (0,))) + dot(low, y, ((0,), (0,)))
-        layer_ref[:, cols] = value.astype(BF16)
-        y_strips.append(dot(take, y, ((1,), (0,))).astype(BF16))
-        dx = back_ref[:, ROWS:, cols].reshape(rows, step)
-        grad_ref[:, cols] = dot(pick, dx, ((0,), (0,))).astype(BF16)
-        dx_strips.append(dot(take, dx, ((1,), (0,))).astype(BF16))
+        y = dot(y_pick, back_ref[:, :ROWS, cols].reshape(rows, step), ((1,), (0,)))
+        layer_ref[:, cols] = (y[:count] + y[count : 2 * count]).astype(BF16)
+        y_strips.append(y[2 * count :].astype(BF16))
+        dx = dot(dx_pick, back_ref[:, ROWS:, cols].reshape(rows, step), ((1,), (0,)))
+        grad_ref[:, cols] = dx[:count].astype(BF16)
+        dx_strips.append(dx[count:].astype(BF16))
+    high, low = split(turned_rows(turned, weight[None, :, :]))
     y = from_strips(jnp.concatenate(y_strips, axis=1), slots)
-    value = dot(tail_high, y, ((0,), (0,))) + dot(tail_low, y, ((0,), (0,)))
+    value = dot(high, y, ((1,), (0,))) + dot(low, y, ((1,), (0,)))
     layer_ref[:, main:] = value.astype(BF16)
+    pick = turned_rows(turned, jnp.ones((1, 1, count), F32)).astype(BF16)
     dx = from_strips(jnp.concatenate(dx_strips, axis=1), slots)
-    grad_ref[:, main:] = dot(tail_pick, dx, ((0,), (0,))).astype(BF16)
+    grad_ref[:, main:] = dot(pick, dx, ((1,), (0,))).astype(BF16)
 
 
 def other_kernel(which_ref, summed_ref, out_ref):
@@ -467,17 +502,22 @@
     flat_spec = pl.BlockSpec((rows, width), lambda p: (0, 0))
     sent_shape = pltpu.HBM((half, 2 * chunk), BF16)
     sent_first, qg0, qu0, h0 = pl.pallas_call(
-        functools.partial(late_kernel, (None, 0, 1)),
+        functools.partial(late_kernel, (0, 1)),
         grid=(3,),
-        in_specs=[smem, flat_spec, flat_spec]
-        + [pl.BlockSpec((width, chunk), lambda p, n=n: (0, n * steps)) for n in range(3)],
+        in_specs=[smem, hbm, hbm, hbm],
         out_specs=[pl.BlockSpec((half, chunk), lambda p: (0, jnp.maximum(p - 1, 0)))]
         + [state_spec] * 3,
         out_shape=[sent_shape] + [state] * 3,
+        scratch_shapes=[
+            pltpu.VMEM((rows, width), BF16),
+            pltpu.VMEM((rows, width), BF16),
+            pltpu.VMEM((3, width, chunk), BF16),
+            pltpu.SemaphoreType.DMA((5,)),
+        ],
         compiler_params=params(63),
         cost_estimate=cost(3 * rows * width * ff, 8 * width * ff),
         name="late_grads",
-    )(which, x, dy, weight, weight, weight)
+    )(which, x, dy, weight)
     route = [((i + slots // 2) % slots, i) for i in range(slots)]
     came_first = lax.ppermute(sent_first, "expert", route)
     plan = ((0, 2, 0), (1, 2, 0), (0, 0, 1), (0, 1, 1), (0, 2, 1), (1, 2, 1))

time: 193 us -> 193 us (level)
  no operation moved by 1% of the time
where the time goes in v9:
time: 193 us; the launch traced here: 191 us
  waiting for transfers between devices  57.1 us (30%)
  Pallas kernels  56.1 us (29%)
  blocking collectives  51 us (26%)
  between operations  14.1 us (7%)
  starting transfers between devices  10.8 us (6%)
  local copies, waits for them, and re-layouts  2.05 us (1%)
    all_to_all x1, blocking collectives, local(): lax.all_to_all(sent, 'expert', split_axis=0, concat_axis=0, tiled=True)  51 us
    all_to_all x1, waiting for transfers between devices, local(): lax.all_to_all(back, 'expert', split_axis=0, concat_axis=0, tiled=True)  35.4 us
    ppermute x1, waiting for transfers between devices, local(): came_second = lax.ppermute(sent_second, 'expert', route)  17.1 us
    pallas_call x1, Pallas kernels, local(): pl.pallas_call(back_kernel, grid=(main // block,), in_specs=[pl.BlockSpec...  12.2 us
    pallas_call x1, Pallas kernels, local(): pl.pallas_call(functools.partial(early_kernel, early_plan, groups), grid=...  10.8 us
    pallas_call x1, Pallas kernels, local(): pl.pallas_call(functools.partial(later_kernel, plan), grid=(len(plan),),...  7.4 us
    pallas_call x1, Pallas kernels, local(): pl.pallas_call(functools.partial(late_kernel, (0, 1)), grid=(3,), in_spec...  7.36 us
    all_to_all x1, starting transfers between devices, local(): lax.all_to_all(back, 'expert', split_axis=0, concat_axis=0, tiled=True)  6.05 us
  transfers between devices with their start and end apart: 6, of which 4 were waited for; matrix products, arithmetic and copies ran while one was open for 0% of the time, Pallas kernels for 21%

profile of v9, /device:TPU:4, one launch (start us, length us, event | category | flops | bytes accessed | tf_op | source)
XLA Modules:
  0.0 191.1 jit_solution(9059695319656459094)
XLA Ops:
  7.2 0.0 reduce-scatter.3.cloned.1.call-start
  7.2 0.0 copy-start
  7.2 3.8 %pack.1 = bf16[32,32,1792]{2,1,0:T(8,128)(2,1)} custom-call(s32[2,128]{1,0:T(2,128)} %bitcast.8, f32[2,128]{1,0:T(2,128)} %bitcast.10, bf16[128,2048]{1,0:T(8,128)(2,1)} %tokens_hbm.1, bf16[128,2048]{1,0:T(8,128)(2,1)} %out_grad_hbm.1), custom_call_target="tpu_custom_call" | custom-call | flops 536870912 | bytes 6291456 | tf_op jit(solution)/shard_map/pack/pallas_call | solution.py:453
  11.0 51.0 %all_to_all.10.rows_ref = bf16[32,32,1792]{2,1,0:T(8,128)(2,1)S(1)} all-to-all(bf16[32,32,1792]{2,1,0:T(8,128)(2,1)} %pack.1), channel_id=1, replica_groups=mesh['dp'=8,'expert'=32] {'expert'}, dimensions={0} | all-to-all | bytes 7340032 | tf_op jit(solution)/shard_map/all_to_all | solution.py:471
  62.0 0.0 copy-done
  62.0 10.8 %early_grads.1 = (bf16[2048,1280]{1,0:T(8,128)(2,1)}, bf16[512,512]{1,0:T(8,128)(2,1)}, bf16[512,512]{1,0:T(8,128)(2,1)}, bf16[512,512]{1,0:T(8,128)(2,1)}, bf16...) custom-call(bf16[32,32,1792]{2,1,0:T(8,128)(2,1)S(1)} %all_to_all.10.rows_ref, bf16[2048,2304]{1,0:T(8,128)(2,1)S(1)} %bitcast.7), custom_call_target="tpu_custom_call" | custom-call | flops 6442450944 | bytes 25165824 | tf_op jit(solution)/shard_map/early_grads/pallas_call | solution.py:478
  72.8 0.0 reduce-scatter.3.cloned.1.call-update
  72.8 7.4 %late_grads.1 = (bf16[1024,512]{1,0:T(8,128)(2,1)}, bf16[512,256]{1,0:T(8,128)(2,1)}, bf16[512,256]{1,0:T(8,128)(2,1)}, bf16[512,256]{1,0:T(8,128)(2,1)}) custom-call(s32[1]{0:T(128)} %bitcast.2.which_ref, bf16[512,2048]{1,0:T(8,128)(2,1)} %get-tuple-element.17.x_hbm.x_ref, bf16[512,2048]{1,0:T(8,128)(2,1)} %get-tuple-element.18.dy_hbm.dy_ref, ...), custom_call_target="tpu_custom_call" | custom-call | flops 2415919104 | bytes 12582912 | tf_op jit(solution)/shard_map/late_grads/pallas_call | solution.py:504
  80.2 2.1 %collective-permute-start.1 = (bf16[1024,512]{1,0:T(8,128)(2,1)}, bf16[1024,512]{1,0:T(8,128)(2,1)}, u32[]{:S(2)}, u32[]{:S(2)}) collective-permute-start(bf16[1024,512]{1,0:T(8,128)(2,1)} %get-tuple-element.29), channel_id=1, source_target_pairs={{16,0},{17,1},{18,2},{19,3},{20,4},{21,5},{22,6},{23,7},{24,8},{25... | collective-permute-start | bytes 3145736 | tf_op jit(solution)/shard_map/ppermute | solution.py:522
  82.3 7.4 %later_grads.1 = (bf16[1024,512]{1,0:T(8,128)(2,1)}, bf16[1024,1024]{1,0:T(8,128)(2,1)}) custom-call(s32[1]{0:T(128)} %bitcast.2.which_ref, bf16[512,2048]{1,0:T(8,128)(2,1)} %get-tuple-element.17.x_hbm.x_ref, bf16[512,2048]{1,0:T(8,128)(2,1)} %get-tuple-element.18.dy_hbm.dy_ref, bf16[512,256]{1,0:T(8,128)(2,1)} %get-tuple-element.20.qg0_ref.qg_ref, ...), custom_call_target="tpu_custom_call" | custom-call | flops 1610612736 | bytes 12582912 | tf_op jit(solution)/shard_map/later_grads/pallas_call | solution.py:524
  89.7 2.0 %collective-permute-start.2 = (bf16[1024,512]{1,0:T(8,128)(2,1)}, bf16[1024,512]{1,0:T(8,128)(2,1)}, u32[]{:S(2)}, u32[]{:S(2)}) collective-permute-start(bf16[1024,512]{1,0:T(8,128)(2,1)} %get-tuple-element.30), channel_id=1, source_target_pairs={{16,0},{17,1},{18,2},{19,3},{20,4},{21,5},{22,6},{23,7},{24,8},{25... | collective-permute-start | bytes 3145736 | tf_op jit(solution)/shard_map/ppermute | solution.py:537
  91.7 12.2 %back.1 = bf16[32,32,1792]{2,1,0:T(8,128)(2,1)} custom-call(bf16[512,256]{1,0:T(8,128)(2,1)} %get-tuple-element.19.h0_ref.h_ref, bf16[512,256]{1,0:T(8,128)(2,1)} %get-tuple-element.20.qg0_ref.qg_ref, bf16[512,256]{1,0:T(8,128)(2,1)} %get-tuple-element.21.qu0_ref.qu_ref, bf16[512,512]{1,0:T(8,128)(2,1)} %get-tuple-element.22.h_ref.kept_ref, ...), custom_call_target="tpu_custom_call" | custom-call | flops 4831838208 | bytes 18874368 | tf_op jit(solution)/shard_map/back/pallas_call | solution.py:539
  103.9 6.0 %all-to-all-start.1 = ((bf16[32,32,1792]{2,1,0:T(8,128)(2,1)}), bf16[32,32,1792]{2,1,0:T(8,128)(2,1)}, u32[]{:S(2)}, u32[]{:S(2)}) async-start(bf16[32,32,1792]{2,1,0:T(8,128)(2,1)} %back.1), calls=%async_computation.1 | async-start | bytes 7340032 | tf_op jit(solution)/shard_map/all_to_all | solution.py:555
  109.9 0.0 reduce-scatter.5.cloned.1.call-start
  110.0 0.0 collective-permute-done.1.came_ref
  110.0 3.6 %late_sum.1.first_ref = bf16[1024,512]{1,0:T(8,128)(2,1)} custom-call(bf16[1024,1024]{1,0:T(8,128)(2,1)} %get-tuple-element.28.own_ref, bf16[1024,512]{1,0:T(8,128)(2,1)} %collective-permute-done.1.came_ref), custom_call_target="tpu_custom_call" | custom-call | flops 8053063680 | bytes 4194304 | tf_op jit(solution)/shard_map/late_sum/pallas_call | solution.py:558
  113.6 17.1 %collective-permute-done.2.came_ref = bf16[1024,512]{1,0:T(8,128)(2,1)} collective-permute-done((bf16[1024,512]{1,0:T(8,128)(2,1)}, bf16[1024,512]{1,0:T(8,128)(2,1)}, u32[]{:S(2)}, u32[]{:S(2)}) %collective-permute-start.2) | collective-permute-done | bytes 1048608 | tf_op jit(solution)/shard_map/ppermute | solution.py:537
  130.8 4.0 %late_join.1 = bf16[1024,1024]{1,0:T(8,128)(2,1)} custom-call(bf16[1024,512]{1,0:T(8,128)(2,1)} %late_sum.1.first_ref, bf16[1024,1024]{1,0:T(8,128)(2,1)} %get-tuple-element.28.own_ref, bf16[1024,512]{1,0:T(8,128)(2,1)} %collective-permute-done.2.came_ref), custom_call_target="tpu_custom_call" | custom-call | flops 1048576 | bytes 6291456 | tf_op jit(solution)/shard_map/late_join/pallas_call | solution.py:568
  134.8 0.0 reduce-scatter.5.cloned.1.call-update
  134.8 4.4 %reduce-scatter.3.cloned.1.call-done.summed_ref.early_ref = bf16[256,1280]{1,0:T(8,128)(2,1)} async-done(((bf16[2048,1280]{1,0:T(8,128)(2,1)}), bf16[256,1280]{1,0:T(8,128)(2,1)}) %reduce-scatter.3.cloned.1.call-update) | async-done | bytes 655376 | tf_op jit(solution)/shard_map/reduce_scatter | solution.py:499
  139.2 0.0 copy-start.1
  139.2 1.1 copy-done.1
  140.3 0.7 other.1
  141.0 0.0 copy-start.2
  141.0 0.6 collective-permute-start
  141.6 35.4 %all-to-all-done.1.back_hbm = bf16[32,32,1792]{2,1,0:T(8,128)(2,1)} async-done(((bf16[32,32,1792]{2,1,0:T(8,128)(2,1)}), bf16[32,32,1792]{2,1,0:T(8,128)(2,1)}, u32[]{:S(2)}, u32[]{:S(2)}) %all-to-all-start.1) | async-done | bytes 3670048 | tf_op jit(solution)/shard_map/all_to_all | solution.py:555
  177.0 5.3 %combine.1 = (bf16[128,2048]{1,0:T(8,128)(2,1)}, bf16[128,2048]{1,0:T(8,128)(2,1)}) custom-call(s32[2,128]{1,0:T(2,128)} %bitcast.9, f32[2,128]{1,0:T(2,128)} %bitcast.11, bf16[32,32,1792]{2,1,0:T(8,128)(2,1)} %all-to-all-done.1.back_hbm), custom_call_target="tpu_custom_call" | custom-call | flops 8053063680 | bytes 6291456 | tf_op jit(solution)/shard_map/combine/pallas_call | solution.py:579
  182.2 0.1 reduce-scatter.5.cloned.1.call-done.late_ref
  182.4 0.0 collective-permute-done.came_ref
  182.4 0.0 copy-done.2
  182.4 0.9 copy-done.3
  183.3 0.9 join.1
  (1 shorter events, 0.0 us)
Async XLA Ops:
  7.2 132.0 %reduce-scatter.3.cloned.1.call-start = ((), (), s32[]{:S(2)}) async-start(), calls=%async_computation.4 | async-start | bytes 5898240 | tf_op jit(solution)/shard_map/reduce_scatter | solution.py:499
  7.2 54.8 %copy-start = (bf16[1,2048,2304]{2,1,0:T(8,128)(2,1)S(1)}, bf16[1,2048,2304]{2,1,0:T(8,128)(2,1)}, u32[]{:S(2)}) copy-start(bf16[1,2048,2304]{2,1,0:T(8,128)(2,1)} %param.9) | copy-start | bytes 28311556
  80.2 29.8 %collective-permute-start.1 = (bf16[1024,512]{1,0:T(8,128)(2,1)}, bf16[1024,512]{1,0:T(8,128)(2,1)}, u32[]{:S(2)}, u32[]{:S(2)}) collective-permute-start(bf16[1024,512]{1,0:T(8,128)(2,1)} %get-tuple-element.29), channel_id=1, source_target_pairs={{16,0},{17,1},{18,2},{19,3},{20,4},{21,5},{22,6},{23,7},{24,8},{25... | collective-permute-start | bytes 3145736 | tf_op jit(solution)/shard_map/ppermute | solution.py:522
  89.7 41.1 %collective-permute-start.2 = (bf16[1024,512]{1,0:T(8,128)(2,1)}, bf16[1024,512]{1,0:T(8,128)(2,1)}, u32[]{:S(2)}, u32[]{:S(2)}) collective-permute-start(bf16[1024,512]{1,0:T(8,128)(2,1)} %get-tuple-element.30), channel_id=1, source_target_pairs={{16,0},{17,1},{18,2},{19,3},{20,4},{21,5},{22,6},{23,7},{24,8},{25... | collective-permute-start | bytes 3145736 | tf_op jit(solution)/shard_map/ppermute | solution.py:537
  103.9 73.1 %all-to-all-start.1 = ((bf16[32,32,1792]{2,1,0:T(8,128)(2,1)}), bf16[32,32,1792]{2,1,0:T(8,128)(2,1)}, u32[]{:S(2)}, u32[]{:S(2)}) async-start(bf16[32,32,1792]{2,1,0:T(8,128)(2,1)} %back.1), calls=%async_computation.1 | async-start | bytes 7340032 | tf_op jit(solution)/shard_map/all_to_all | solution.py:555
  109.9 72.4 %reduce-scatter.5.cloned.1.call-start = ((), (), s32[]{:S(2)}) async-start(), calls=%async_computation.5 | async-start | bytes 2359296 | tf_op jit(solution)/shard_map/reduce_scatter | solution.py:578
  139.2 1.1 copy-start.1
  141.0 41.3 %copy-start.2 = (bf16[256,1280]{1,0:T(8,128)(2,1)S(1)}, bf16[256,1280]{1,0:T(8,128)(2,1)}, u32[]{:S(2)}) copy-start(bf16[256,1280]{1,0:T(8,128)(2,1)} %reduce-scatter.3.cloned.1.call-done.summed_ref.early_ref) | copy-start | bytes 1966084
  141.0 41.3 %collective-permute-start = (bf16[128,1280]{1,0:T(8,128)(2,1)}, bf16[128,1280]{1,0:T(8,128)(2,1)S(1)}, u32[]{:S(2)}, u32[]{:S(2)}) collective-permute-start(bf16[128,1280]{1,0:T(8,128)(2,1)} %other.1), channel_id=1, source_target_pairs={{16,0},{17,1},{18,2},{19,3},{20,4},{21,5},{22,6},{23,7},{24,8},{25... | collective-permute-start | bytes 983048 | tf_op jit(solution)/shard_map/ppermute | solution.py:600
  182.4 1.0 copy-start.3
Sparse Core Ops, SparseCore 0:
  72.9 66.2 reduce-scatter.2
  141.8 40.5 reduce-scatter.4

commit v10 on v9

--- a/solution.py
+++ b/solution.py
@@ -194,15 +194,27 @@
     state_rows(a, b, e, qg_ref, qu_ref, h_ref)
 
 
+def half_grads(x_ref, dy_ref, n, which, rhs):
+    lhs_ref = dy_ref if n == 2 else x_ref
+    half = lhs_ref.shape[1] // 2
+    cols = pl.ds(pl.multiple_of(which * half, half), half)
+    return dot(lhs_ref[:, cols], rhs, ((0,), (0,))).astype(BF16)
+
+
 def early_kernel(
     plan,
     groups,
+    which_ref,
     rows_ref,
     w_ref,
     partial_ref,
     qg_ref,
     qu_ref,
     h_ref,
+    sent_ref,
+    qg0_ref,
+    qu0_ref,
+    h0_ref,
     x_hbm,
     dy_hbm,
     x_ref,
@@ -211,7 +223,7 @@
 ):
     width = x_ref.shape[1]
     block = width // 2 // groups
-    refs = (qg_ref, qu_ref, h_ref)
+    all_refs = ((qg0_ref, qu0_ref, h0_ref), (qg_ref, qu_ref, h_ref))
 
     def copies():
         return [
@@ -228,11 +240,15 @@
                 unpack_rows(rows_ref, ROWS, dy_ref)
                 for copy in copies():
                     copy.start()
+            refs = all_refs[min(j, 1)]
             if n is None:
                 chunk, ff = h_ref.shape[1], w_ref.shape[1] // 3
                 begins = [n * ff + j * chunk for n in range(3)]
                 weights = (w_ref[:, at : at + chunk] for at in begins)
                 expert_rows(x_ref, dy_ref, *weights, *refs)
+                return
+            if j == 0:
+                sent_ref[...] = half_grads(x_ref, dy_ref, n, 1 - which_ref[0], refs[n][...])
                 return
             lhs_ref = dy_ref if n == 2 else x_ref
             value = dot(lhs_ref[...], refs[n][...], ((0,), (0,))).astype(BF16)
@@ -243,56 +259,6 @@
             if step == len(plan) - 1:
                 for copy in copies():
                     copy.wait()
-
-
-def half_grads(x_ref, dy_ref, n, which, rhs):
-    lhs_ref = dy_ref if n == 2 else x_ref
-    half = lhs_ref.shape[1] // 2
-    cols = pl.ds(pl.multiple_of(which * half, half), half)
-    return dot(lhs_ref[:, cols], rhs, ((0,), (0,))).astype(BF16)
-
-
-def late_kernel(
-    plan,
-    which_ref,
-    x_hbm,
-    dy_hbm,
-    w_hbm,
-    sent_ref,
-    qg_ref,
-    qu_ref,
-    h_ref,
-    x_ref,
-    dy_ref,
-    w_ref,
-    sems,
-):
-    refs = (qg_ref, qu_ref, h_ref)
-    chunk = h_ref.shape[1]
-    ff = w_hbm.shape[1] // 3
-
-    @pl.when(pl.program_id(0) == 0)
-    def _():
-        pairs = [(w_hbm.at[:, pl.ds(n * ff, chunk)], w_ref.at[n]) for n in range(3)]
-        pairs = [(x_hbm, x_ref), pairs[0], pairs[1], (dy_hbm, dy_ref), pairs[2]]
-        loads = [pltpu.make_async_copy(*pair, sems.at[i]) for i, pair in enumerate(pairs)]
-        for load in loads:
-            load.start()
-        loads[0].wait()
-        loads[1].wait()
-        a = dot(x_ref[...], w_ref[0], ((1,), (0,)))
-        loads[2].wait()
-        b = dot(x_ref[...], w_ref[1], ((1,), (0,)))
-        loads[3].wait()
-        loads[4].wait()
-        e = dot(dy_ref[...], w_ref[2], ((1,), (0,)))
-        state_rows(a, b, e, *refs)
-
-    for step, n in enumerate(plan):
-
-        @pl.when(pl.program_id(0) == step + 1)
-        def _(n=n):
-            sent_ref[...] = half_grads(x_ref, dy_ref, n, 1 - which_ref[0], refs[n][...])
 
 
 def later_kernel(
@@ -468,63 +434,54 @@
         cost_estimate=cost(4 * rows * count * width, 6 * rows * width),
         name="pack",
     )(routes_t, gates_t, tokens, out_grad)
+    sent, which = lax.optimization_barrier((sent, which))
     came = lax.all_to_all(sent, "expert", split_axis=0, concat_axis=0, tiled=True)
 
-    early_plan = ((1, None), (1, 0), (1, 1), (2, None), (2, 0), (2, 1), (2, 2))
-    early_cols = tuple(one for one in early_plan if one[1] is not None)
+    early_plan = ((0, None), (0, 0), (0, 1), (1, None), (1, 0), (1, 1))
+    early_plan += ((2, None), (2, 0), (2, 1), (2, 2))
+    early_cols = tuple(one for one in early_plan if one[0] > 0 and one[1] is not None)
     late_cols = ((0, 0), (0, 1), (0, 2), (1, 2))
     state = pltpu.HBM((rows, ff - chunk), BF16)
-    state_spec = pl.BlockSpec((rows, chunk), lambda p: (0, jnp.where(p >= 3, 1, 0)))
-    early, qg, qu, h, x, dy = pl.pallas_call(
+    state_spec = pl.BlockSpec((rows, chunk), lambda p: (0, jnp.where(p >= 6, 1, 0)))
+    first_state = pltpu.HBM((rows, chunk), BF16)
+    first_spec = pl.BlockSpec((rows, chunk), lambda p: (0, 0))
+    sent_shape = pltpu.HBM((half, 2 * chunk), BF16)
+    early, qg, qu, h, sent_first, qg0, qu0, h0, x, dy = pl.pallas_call(
         functools.partial(early_kernel, early_plan, groups),
         grid=(len(early_plan),),
-        in_specs=[vmem, vmem],
+        in_specs=[smem, vmem, vmem],
         out_specs=[
             pl.BlockSpec(
-                (width, chunk), lambda p: (0, p - jnp.where(p > 0, 1, 0) - jnp.where(p > 3, 1, 0))
+                (width, chunk), lambda p: (0, jnp.maximum(p - 4 - jnp.where(p > 6, 1, 0), 0))
             )
         ]
         + [state_spec] * 3
+        + [pl.BlockSpec((half, chunk), lambda p: (0, jnp.clip(p - 1, 0, 1)))]
+        + [first_spec] * 3
         + [hbm] * 2,
-        out_shape=[pltpu.HBM((width, len(early_cols) * chunk), BF16)] + [state] * 3 + [flat] * 2,
+        out_shape=[pltpu.HBM((width, len(early_cols) * chunk), BF16)]
+        + [state] * 3
+        + [sent_shape]
+        + [first_state] * 3
+        + [flat] * 2,
         scratch_shapes=[
             pltpu.VMEM((rows, width), BF16),
             pltpu.VMEM((rows, width), BF16),
             pltpu.SemaphoreType.DMA((2,)),
         ],
-        compiler_params=params(26),
+        compiler_params=params(27),
         cost_estimate=cost(8 * rows * width * ff, 16 * width * ff),
         name="early_grads",
-    )(came, weight)
+    )(which, came, weight)
     early_sum = lax.psum_scatter(early, "dp", scatter_dimension=0, tiled=True)
-    state = pltpu.HBM((rows, chunk), BF16)
-    state_spec = pl.BlockSpec((rows, chunk), lambda p: (0, 0))
     flat_spec = pl.BlockSpec((rows, width), lambda p: (0, 0))
-    sent_shape = pltpu.HBM((half, 2 * chunk), BF16)
-    sent_first, qg0, qu0, h0 = pl.pallas_call(
-        functools.partial(late_kernel, (0, 1)),
-        grid=(3,),
-        in_specs=[smem, hbm, hbm, hbm],
-        out_specs=[pl.BlockSpec((half, chunk), lambda p: (0, jnp.maximum(p - 1, 0)))]
-        + [state_spec] * 3,
-        out_shape=[sent_shape] + [state] * 3,
-        scratch_shapes=[
-            pltpu.VMEM((rows, width), BF16),
-            pltpu.VMEM((rows, width), BF16),
-            pltpu.VMEM((3, width, chunk), BF16),
-            pltpu.SemaphoreType.DMA((5,)),
-        ],
-        compiler_params=params(63),
-        cost_estimate=cost(3 * rows * width * ff, 8 * width * ff),
-        name="late_grads",
-    )(which, x, dy, weight)
     route = [((i + slots // 2) % slots, i) for i in range(slots)]
     came_first = lax.ppermute(sent_first, "expert", route)
     plan = ((0, 2, 0), (1, 2, 0), (0, 0, 1), (0, 1, 1), (0, 2, 1), (1, 2, 1))
     sent_second, own = pl.pallas_call(
         functools.partial(later_kernel, plan),
         grid=(len(plan),),
-        in_specs=[smem, flat_spec, flat_spec] + [state_spec] * 4,
+        in_specs=[smem, flat_spec, flat_spec] + [first_spec] * 4,
         out_specs=[
             pl.BlockSpec((half, chunk), lambda p: (0, jnp.minimum(p, 1))),
             pl.BlockSpec((half, chunk), lambda p: (0, jnp.maximum(p - 2, 0))),

time: 193 us -> 195 us (1.010)
  waiting for transfers between devices: 57.1 us -> 64.3 us
  Pallas kernels: 56.1 us -> 52.9 us
    reduce_scatter x1, waiting for transfers between devices: 0.14 us -> 7.57 us  [local(): late_sum = lax.psum_scatter(late, 'dp', scatter_dimension=0, tiled=True)]
    pallas_call x1 -> x0, Pallas kernels: 7.36 us -> none  [local(): pl.pallas_call(functools.partial(late_kernel, (0, 1)), grid=(3,), in_spec...]
    reduce_scatter x1, waiting for transfers between devices: 4.38 us -> 11.7 us  [local(): early_sum = lax.psum_scatter(early, 'dp', scatter_dimension=0, tiled=True)]
    all_to_all x1, waiting for transfers between devices: 35.4 us -> 28 us  [local(): lax.all_to_all(back, 'expert', split_axis=0, concat_axis=0, tiled=True)]
    pallas_call x1, Pallas kernels: 10.8 us -> 14.5 us  [local(): pl.pallas_call(functools.partial(early_kernel, early_plan, groups), grid=...]
  transfers between devices with their start and end apart: 6 -> 6, of which waited for: 4 -> 4; matrix products, arithmetic and copies ran while one was open for 0% -> 0% of each run, Pallas kernels for 21% -> 17%
where the time goes in v10:
time: 195 us
  waiting for transfers between devices  64.3 us (33%)
  Pallas kernels  52.9 us (27%)
  blocking collectives  51 us (26%)
  between operations  14.1 us (7%)
  starting transfers between devices  10.5 us (5%)
  local copies, waits for them, and re-layouts  2.05 us (1%)
    all_to_all x1, blocking collectives, local(): lax.all_to_all(sent, 'expert', split_axis=0, concat_axis=0, tiled=True)  51 us
    all_to_all x1, waiting for transfers between devices, local(): lax.all_to_all(back, 'expert', split_axis=0, concat_axis=0, tiled=True)  28 us
    ppermute x1, waiting for transfers between devices, local(): came_second = lax.ppermute(sent_second, 'expert', route)  17 us
    pallas_call x1, Pallas kernels, local(): pl.pallas_call(functools.partial(early_kernel, early_plan, groups), grid=...  14.5 us
    pallas_call x1, Pallas kernels, local(): pl.pallas_call(back_kernel, grid=(main // block,), in_specs=[pl.BlockSpec...  12.6 us
    reduce_scatter x1, waiting for transfers between devices, local(): early_sum = lax.psum_scatter(early, 'dp', scatter_dimension=0, tiled=True)  11.7 us
    reduce_scatter x1, waiting for transfers between devices, local(): late_sum = lax.psum_scatter(late, 'dp', scatter_dimension=0, tiled=True)  7.57 us
    pallas_call x1, Pallas kernels, local(): pl.pallas_call(functools.partial(later_kernel, plan), grid=(len(plan),),...  7.38 us
  transfers between devices with their start and end apart: 6, of which 4 were waited for; matrix products, arithmetic and copies ran while one was open for 0% of the time, Pallas kernels for 17%

profile of v10, /device:TPU:4, one launch (start us, length us, event | category | flops | bytes accessed | tf_op | source)
XLA Modules:
  0.0 194.9 jit_solution(7310563165259296740)
XLA Ops:
  7.2 0.0 reduce-scatter.3.cloned.1.call-start
  7.2 0.0 copy-start
  7.2 3.8 %pack.1 = bf16[32,32,1792]{2,1,0:T(8,128)(2,1)} custom-call(s32[2,128]{1,0:T(2,128)} %bitcast.7, f32[2,128]{1,0:T(2,128)} %bitcast.9, bf16[128,2048]{1,0:T(8,128)(2,1)} %tokens_hbm.1, bf16[128,2048]{1,0:T(8,128)(2,1)} %out_grad_hbm.1), custom_call_target="tpu_custom_call" | custom-call | flops 536870912 | bytes 6291456 | tf_op jit(solution)/shard_map/pack/pallas_call | solution.py:419
  11.0 51.0 %all_to_all.10.rows_ref = bf16[32,32,1792]{2,1,0:T(8,128)(2,1)S(1)} all-to-all(bf16[32,32,1792]{2,1,0:T(8,128)(2,1)} %pack.1), channel_id=1, replica_groups=mesh['dp'=8,'expert'=32] {'expert'}, dimensions={0} | all-to-all | bytes 7340032 | tf_op jit(solution)/shard_map/all_to_all | solution.py:438
  62.0 0.0 copy-done
  62.0 14.5 %early_grads.1 = (bf16[2048,1280]{1,0:T(8,128)(2,1)}, bf16[512,512]{1,0:T(8,128)(2,1)}, bf16[512,512]{1,0:T(8,128)(2,1)}, bf16[512,512]{1,0:T(8,128)(2,1)}, bf16...) custom-call(s32[1]{0:T(128)} %bitcast.2.which_ref, ...), custom_call_target="tpu_custom_call" | custom-call | flops 6442450944 | bytes 25165824 | tf_op jit(solution)/shard_map/early_grads/pallas_call | solution.py:449
  76.6 0.0 reduce-scatter.3.cloned.1.call-update
  76.6 2.1 %collective-permute-start.1 = (bf16[1024,512]{1,0:T(8,128)(2,1)}, bf16[1024,512]{1,0:T(8,128)(2,1)}, u32[]{:S(2)}, u32[]{:S(2)}) collective-permute-start(bf16[1024,512]{1,0:T(8,128)(2,1)} %get-tuple-element.33), channel_id=1, source_target_pairs={{16,0},{17,1},{18,2},{19,3},{20,4},{21,5},{22,6},{23,7},{24,8},{25... | collective-permute-start | bytes 3145736 | tf_op jit(solution)/shard_map/ppermute | solution.py:479
  78.7 7.4 %later_grads.1 = (bf16[1024,512]{1,0:T(8,128)(2,1)}, bf16[1024,1024]{1,0:T(8,128)(2,1)}) custom-call(s32[1]{0:T(128)} %bitcast.2.which_ref, bf16[512,2048]{1,0:T(8,128)(2,1)} %get-tuple-element.30.x_ref, bf16[512,2048]{1,0:T(8,128)(2,1)} %get-tuple-element.31.dy_ref, bf16[512,256]{1,0:T(8,128)(2,1)} %get-tuple-element.22.qg0_ref.qg_ref, ...), custom_call_target="tpu_custom_call" | custom-call | flops 1610612736 | bytes 12582912 | tf_op jit(solution)/shard_map/later_grads/pallas_call | solution.py:481
  86.0 1.7 collective-permute-start.2
  87.8 12.6 %back.1 = bf16[32,32,1792]{2,1,0:T(8,128)(2,1)} custom-call(bf16[512,256]{1,0:T(8,128)(2,1)} %get-tuple-element.21.h0_ref.h_ref, bf16[512,256]{1,0:T(8,128)(2,1)} %get-tuple-element.22.qg0_ref.qg_ref, bf16[512,256]{1,0:T(8,128)(2,1)} %get-tuple-element.23.qu0_ref.qu_ref, bf16[512,512]{1,0:T(8,128)(2,1)} %get-tuple-element.24.h_ref.kept_ref, ...), custom_call_target="tpu_custom_call" | custom-call | flops 4831838208 | bytes 18874368 | tf_op jit(solution)/shard_map/back/pallas_call | solution.py:496
  100.4 6.1 %all-to-all-start.1 = ((bf16[32,32,1792]{2,1,0:T(8,128)(2,1)}), bf16[32,32,1792]{2,1,0:T(8,128)(2,1)}, u32[]{:S(2)}, u32[]{:S(2)}) async-start(bf16[32,32,1792]{2,1,0:T(8,128)(2,1)} %back.1), calls=%async_computation.1 | async-start | bytes 7340032 | tf_op jit(solution)/shard_map/all_to_all | solution.py:512
  106.5 0.0 reduce-scatter.5.cloned.1.call-start
  106.5 0.0 collective-permute-done.1.came_ref
  106.5 3.6 %late_sum.1.first_ref = bf16[1024,512]{1,0:T(8,128)(2,1)} custom-call(bf16[1024,1024]{1,0:T(8,128)(2,1)} %get-tuple-element.32.own_ref, bf16[1024,512]{1,0:T(8,128)(2,1)} %collective-permute-done.1.came_ref), custom_call_target="tpu_custom_call" | custom-call | flops 8053063680 | bytes 4194304 | tf_op jit(solution)/shard_map/late_sum/pallas_call | solution.py:515
  110.2 17.0 %collective-permute-done.2.came_ref = bf16[1024,512]{1,0:T(8,128)(2,1)} collective-permute-done((bf16[1024,512]{1,0:T(8,128)(2,1)}, bf16[1024,512]{1,0:T(8,128)(2,1)}, u32[]{:S(2)}, u32[]{:S(2)}) %collective-permute-start.2) | collective-permute-done | bytes 1048608 | tf_op jit(solution)/shard_map/ppermute | solution.py:494
  127.1 4.1 %late_join.1 = bf16[1024,1024]{1,0:T(8,128)(2,1)} custom-call(bf16[1024,512]{1,0:T(8,128)(2,1)} %late_sum.1.first_ref, bf16[1024,1024]{1,0:T(8,128)(2,1)} %get-tuple-element.32.own_ref, bf16[1024,512]{1,0:T(8,128)(2,1)} %collective-permute-done.2.came_ref), custom_call_target="tpu_custom_call" | custom-call | flops 1048576 | bytes 6291456 | tf_op jit(solution)/shard_map/late_join/pallas_call | solution.py:525
  131.2 0.0 reduce-scatter.5.cloned.1.call-update
  131.2 11.7 %reduce-scatter.3.cloned.1.call-done.summed_ref.early_ref = bf16[256,1280]{1,0:T(8,128)(2,1)} async-done(((bf16[2048,1280]{1,0:T(8,128)(2,1)}), bf16[256,1280]{1,0:T(8,128)(2,1)}) %reduce-scatter.3.cloned.1.call-update) | async-done | bytes 655376 | tf_op jit(solution)/shard_map/reduce_scatter | solution.py:476
  143.0 0.0 copy-start.1
  143.0 1.1 copy-done.1
  144.1 0.7 other.1
  144.8 0.0 copy-start.2
  144.8 0.6 collective-permute-start
  145.4 28.0 %all-to-all-done.1.back_hbm = bf16[32,32,1792]{2,1,0:T(8,128)(2,1)} async-done(((bf16[32,32,1792]{2,1,0:T(8,128)(2,1)}), bf16[32,32,1792]{2,1,0:T(8,128)(2,1)}, u32[]{:S(2)}, u32[]{:S(2)}) %all-to-all-start.1) | async-done | bytes 3670048 | tf_op jit(solution)/shard_map/all_to_all | solution.py:512
  173.4 5.3 %combine.1 = (bf16[128,2048]{1,0:T(8,128)(2,1)}, bf16[128,2048]{1,0:T(8,128)(2,1)}) custom-call(s32[2,128]{1,0:T(2,128)} %bitcast.8, f32[2,128]{1,0:T(2,128)} %bitcast.10, bf16[32,32,1792]{2,1,0:T(8,128)(2,1)} %all-to-all-done.1.back_hbm), custom_call_target="tpu_custom_call" | custom-call | flops 8053063680 | bytes 6291456 | tf_op jit(solution)/shard_map/combine/pallas_call | solution.py:536
  178.6 7.6 %reduce-scatter.5.cloned.1.call-done.late_ref = bf16[128,1024]{1,0:T(8,128)(2,1)} async-done(((bf16[1024,1024]{1,0:T(8,128)(2,1)}), bf16[128,1024]{1,0:T(8,128)(2,1)}) %reduce-scatter.5.cloned.1.call-update) | async-done | bytes 262160 | tf_op jit(solution)/shard_map/reduce_scatter | solution.py:535
  186.2 0.0 collective-permute-done.came_ref
  186.2 0.0 copy-done.2
  186.2 0.0 copy-start.3
  186.2 0.9 copy-done.3
  187.2 0.9 join.1
Async XLA Ops:
  7.2 135.8 %reduce-scatter.3.cloned.1.call-start = ((), (), s32[]{:S(2)}) async-start(), calls=%async_computation.4 | async-start | bytes 5898240 | tf_op jit(solution)/shard_map/reduce_scatter | solution.py:476
  7.2 54.8 %copy-start = (bf16[1,2048,2304]{2,1,0:T(8,128)(2,1)S(1)}, bf16[1,2048,2304]{2,1,0:T(8,128)(2,1)}, u32[]{:S(2)}) copy-start(bf16[1,2048,2304]{2,1,0:T(8,128)(2,1)} %param.9) | copy-start | bytes 28311556
  76.6 29.9 %collective-permute-start.1 = (bf16[1024,512]{1,0:T(8,128)(2,1)}, bf16[1024,512]{1,0:T(8,128)(2,1)}, u32[]{:S(2)}, u32[]{:S(2)}) collective-permute-start(bf16[1024,512]{1,0:T(8,128)(2,1)} %get-tuple-element.33), channel_id=1, source_target_pairs={{16,0},{17,1},{18,2},{19,3},{20,4},{21,5},{22,6},{23,7},{24,8},{25... | collective-permute-start | bytes 3145736 | tf_op jit(solution)/shard_map/ppermute | solution.py:479
  86.0 41.1 %collective-permute-start.2 = (bf16[1024,512]{1,0:T(8,128)(2,1)}, bf16[1024,512]{1,0:T(8,128)(2,1)}, u32[]{:S(2)}, u32[]{:S(2)}) collective-permute-start(bf16[1024,512]{1,0:T(8,128)(2,1)} %get-tuple-element.34), channel_id=1, source_target_pairs={{16,0},{17,1},{18,2},{19,3},{20,4},{21,5},{22,6},{23,7},{24,8},{25... | collective-permute-start | bytes 3145736 | tf_op jit(solution)/shard_map/ppermute | solution.py:494
  100.4 73.0 %all-to-all-start.1 = ((bf16[32,32,1792]{2,1,0:T(8,128)(2,1)}), bf16[32,32,1792]{2,1,0:T(8,128)(2,1)}, u32[]{:S(2)}, u32[]{:S(2)}) async-start(bf16[32,32,1792]{2,1,0:T(8,128)(2,1)} %back.1), calls=%async_computation.1 | async-start | bytes 7340032 | tf_op jit(solution)/shard_map/all_to_all | solution.py:512
  106.5 79.7 %reduce-scatter.5.cloned.1.call-start = ((), (), s32[]{:S(2)}) async-start(), calls=%async_computation.5 | async-start | bytes 2359296 | tf_op jit(solution)/shard_map/reduce_scatter | solution.py:535
  143.0 1.1 copy-start.1
  144.8 41.4 %copy-start.2 = (bf16[256,1280]{1,0:T(8,128)(2,1)S(1)}, bf16[256,1280]{1,0:T(8,128)(2,1)}, u32[]{:S(2)}) copy-start(bf16[256,1280]{1,0:T(8,128)(2,1)} %reduce-scatter.3.cloned.1.call-done.summed_ref.early_ref) | copy-start | bytes 1966084
  144.8 41.4 %collective-permute-start = (bf16[128,1280]{1,0:T(8,128)(2,1)}, bf16[128,1280]{1,0:T(8,128)(2,1)S(1)}, u32[]{:S(2)}, u32[]{:S(2)}) collective-permute-start(bf16[128,1280]{1,0:T(8,128)(2,1)} %other.1), channel_id=1, source_target_pairs={{16,0},{17,1},{18,2},{19,3},{20,4},{21,5},{22,6},{23,7},{24,8},{25... | collective-permute-start | bytes 983048 | tf_op jit(solution)/shard_map/ppermute | solution.py:557
  186.2 1.0 copy-start.3
Sparse Core Ops, SparseCore 0:
  76.7 66.2 reduce-scatter.2
  145.5 40.6 reduce-scatter.4
